TPU v7x, 32 devices: a whole 2x2x4 slice. The times are simulated.
32 devices in a mesh: dp: 16 (over z, x, core), mp: 2 (over y).
Axes of the slice: x: 2, y: 2, z: 4, core: 2. Of those that a mesh axis runs over, the one named last changes fastest.
Arguments:
- query_states: bfloat16 [2048, 1024], P('dp'), may hold values from -41 to 41
- passage_states: bfloat16 [2048, 1024], P('dp'), may hold values from -41 to 41
- w_in: bfloat16 [1024, 4096], P(None, 'mp'), may hold values from -0.1875 to 0.1875
- w_out: bfloat16 [4096, 1024], P('mp'), may hold values from -0.09375 to 0.09375
- neg_owner: int32 [2048, 8], P('dp'), may hold values from 0 to 15, all different within a row; in each aligned block of 128 rows (0 to 127, 128 to 255, ...) at most 128 rows name the same one
- neg_mask: int32 [2048, 8], P('dp'), may hold values 0 or 1
- served_rows: int32 [16, 16, 128], P('dp'), may hold values from 0 to 127
- loss_scale: float32 [], replicated, may hold values from 32 to 128
Outputs:
- grad_query_states: bfloat16 [2048, 1024], P('dp', 'mp')
- grad_passage_states: bfloat16 [2048, 1024], P('dp', 'mp')
Inputs may be any that keep to these rules, and one draw needn't show every extreme that they name: Within the queries of one owner (aligned blocks of 128 rows) no owner is named by more than 128 entries of neg_owner, and in some block one owner is named exactly 128 times; the 8 owners of one query are distinct.
All inputs are finite; a program needn't handle non-finite values. No bound on the sum of `neg_mask` on one device may be relied on, other than what follows from the above.
Results may differ from a plain program's by a relative error of at most 0.017.
Values may be sent and summed in bfloat16 or wider, within the bound.
No kernel may reach another device: no remote copies, remote signals or barrier semaphores. Data moves between devices by JAX's collectives and lax.ppermute only.
A program may use at most 64 MiB of HBM per device.

v0:
```python
import jax
import jax.numpy as jnp
from jax import lax
from jax.sharding import PartitionSpec as P

logit_scale = 50.0
norm_eps = 1e-06
root_half = 0.7071067811865476
inv_root_two_pi = 0.3989422804014327


def gelu_value(values):
    return 0.5 * values * (1.0 + lax.erf(values * root_half))


def gelu_slope(values):
    return (
        0.5 * (1.0 + lax.erf(values * root_half))
        + values * jnp.exp(-0.5 * values * values) * inv_root_two_pi
    )


def own_columns(values):
    column_width = values.shape[1] // lax.axis_size("mp")
    return lax.dynamic_slice_in_dim(values, lax.axis_index("mp") * column_width, column_width, 1)


def encode(states, w_in, w_out):
    pre_act = jnp.dot(states, w_in, preferred_element_type=jnp.float32)
    hidden = gelu_value(pre_act).astype(jnp.bfloat16)
    partial_out = jnp.dot(hidden, w_out, preferred_element_type=jnp.float32)
    mixed_sum = lax.psum(partial_out, "mp")
    output = states.astype(jnp.float32) + mixed_sum
    inv_norm = lax.rsqrt(jnp.sum(output * output, axis=1, keepdims=True) + norm_eps)
    return (pre_act, output * inv_norm, inv_norm)


def decode(grad_part, pre_act, unit_rows, inv_norm, w_in, w_out):
    grad_emb = lax.all_gather(grad_part.astype(jnp.bfloat16), "mp", axis=1, tiled=True).astype(
        grad_part.dtype
    )
    grad_out = inv_norm * (
        grad_emb - unit_rows * jnp.sum(unit_rows * grad_emb, axis=1, keepdims=True)
    )
    contract = (((1,), (1,)), ((), ()))
    grad_hidden = lax.dot_general(
        grad_out.astype(jnp.bfloat16), w_out, contract, preferred_element_type=jnp.float32
    )
    grad_pre = (grad_hidden * gelu_slope(pre_act)).astype(jnp.bfloat16)
    partial_in = lax.dot_general(grad_pre, w_in, contract, preferred_element_type=jnp.float32)
    summed = lax.psum_scatter(
        partial_in.astype(jnp.bfloat16), "mp", scatter_dimension=1, tiled=True
    ).astype(jnp.float32)
    return (summed + own_columns(grad_out)).astype(jnp.bfloat16)


def shards(query_states, passage_states, w_in, w_out, neg_owner, neg_mask, served_rows, loss_scale):
    owners = lax.axis_size("dp")
    row_count = query_states.shape[0]
    negatives = neg_owner.shape[1]
    capacity = served_rows.shape[2]
    pre_pass, unit_pass, inv_pass = encode(passage_states, w_in, w_out)
    emb_pass = own_columns(unit_pass).astype(jnp.bfloat16)
    column_width = emb_pass.shape[1]
    served = served_rows[0]
    flat_owner = neg_owner.reshape(-1)
    onehot = (flat_owner[:, None] == jnp.arange(owners, dtype=jnp.int32)[None, :]).astype(jnp.int32)
    before = jnp.cumsum(onehot, axis=0, dtype=jnp.int32) - onehot
    slot_index = jnp.sum(before * onehot, axis=1, dtype=jnp.int32)
    slot_place = flat_owner * capacity + slot_index
    every_emb = lax.all_gather(emb_pass, "dp", axis=0, tiled=True)
    rows_for_me = lax.all_to_all(
        served_rows, "dp", split_axis=1, concat_axis=0, tiled=True
    ).reshape(owners * capacity)
    neg_rows = jnp.take(rows_for_me, slot_place, axis=0)
    neg_emb = jnp.take(every_emb, flat_owner * row_count + neg_rows, axis=0)
    neg_emb = neg_emb.reshape(row_count, negatives, column_width)
    pre_query, unit_query, inv_query = encode(query_states, w_in, w_out)
    emb_query = own_columns(unit_query).astype(jnp.bfloat16)
    pos_part = jnp.einsum("qd,qd->q", emb_query, emb_pass, preferred_element_type=jnp.float32)
    neg_part = jnp.einsum("qd,qnd->qn", emb_query, neg_emb, preferred_element_type=jnp.float32)
    pos_score, neg_score = lax.psum((pos_part, neg_part), "mp")
    exp_pos = jnp.exp(logit_scale * pos_score)
    exp_neg = neg_mask.astype(jnp.float32) * jnp.exp(logit_scale * neg_score)
    denominator = exp_pos + jnp.sum(exp_neg, axis=1)
    factor = loss_scale * logit_scale
    grad_pos = factor * (exp_pos / denominator - 1.0)
    grad_neg = factor * exp_neg / denominator[:, None]
    query_values = emb_query.astype(jnp.float32)
    grad_query_emb = grad_pos[:, None] * emb_pass.astype(jnp.float32) + jnp.sum(
        grad_neg[:, :, None] * neg_emb.astype(jnp.float32), axis=1
    )
    slot_terms = (
        (grad_neg[:, :, None] * query_values[:, None, :])
        .astype(jnp.bfloat16)
        .reshape(-1, column_width)
    )
    outgoing_grad = (
        jnp.zeros((owners * capacity, column_width), jnp.bfloat16).at[slot_place].set(slot_terms)
    )
    returned = lax.all_to_all(
        outgoing_grad.reshape(owners, capacity, column_width),
        "dp",
        split_axis=0,
        concat_axis=0,
        tiled=True,
    )
    grad_query_states = decode(grad_query_emb, pre_query, unit_query, inv_query, w_in, w_out)
    gathered_back = (
        jnp.zeros((row_count, column_width), jnp.float32)
        .at[served.reshape(-1)]
        .add(returned.reshape(-1, column_width).astype(jnp.float32))
    )
    grad_pass_emb = grad_pos[:, None] * query_values + gathered_back
    grad_passage_states = decode(grad_pass_emb, pre_pass, unit_pass, inv_pass, w_in, w_out)
    return (grad_query_states, grad_passage_states)


def solution(mesh):
    in_specs = (
        P("dp", None),
        P("dp", None),
        P(None, "mp"),
        P("mp", None),
        P("dp", None),
        P("dp", None),
        P("dp", None, None),
        P(),
    )
    out_specs = (P("dp", "mp"), P("dp", "mp"))
    return jax.shard_map(shards, mesh=mesh, in_specs=in_specs, out_specs=out_specs, check_vma=False)
```

profile of v0, /device:TPU:0, one launch (start us, length us, event | category | flops | bytes accessed | tf_op | source)
XLA Modules:
  0.0 223.5 jit_solution(5101777199026476012)
XLA Ops:
  7.2 0.0 copy-start.4
  7.2 0.0 all-reduce.4.cloned.1.call-start
  7.2 0.0 copy-start
  7.2 3.1 %fusion.62 = f32[128,2048]{1,0:T(8,128)S(1)} fusion(bf16[128,1024]{1,0:T(8,128)(2,1)} %param.9, bf16[1024,2048]{1,0:T(8,128)(2,1)} %param.10), kind=kOutput, calls=%fused_computation.111 | convolution fusion | flops 536870912 | bytes 5505024 | tf_op jit(solution)/shard_map/dot_general | solution.py:29
  10.4 3.3 %fusion.61 = f32[128,2048]{1,0:T(8,128)S(1)} fusion(bf16[128,1024]{1,0:T(8,128)(2,1)S(1)} %copy-done.4, bf16[1024,2048]{1,0:T(8,128)(2,1)} %param.10), kind=kOutput, calls=%fused_computation.110 | convolution fusion | flops 536870912 | bytes 5505024 | tf_op jit(solution)/shard_map/dot_general | solution.py:29
  13.7 0.0 copy-done
  13.7 0.0 copy-start.3
  13.7 1.6 fusion.24
  15.3 1.6 fusion.23
  16.9 0.0 all-reduce.4.cloned.1.call-update
  16.9 0.0 all-gather.2.cloned.1.call-start
  17.0 43.0 %all-reduce.4.cloned.1.call-done = (f32[128,1024]{1,0:T(8,128)}, f32[128,1024]{1,0:T(8,128)}) async-done(((f32[128,1024]{1,0:T(8,128)}, f32[128,1024]{1,0:T(8,128)}), (f32[128,1024]{1,0:T(8,128)}, f32[128,1024]{1,0:T(8,128)})) %all-reduce.4.cloned.1.call-update) | async-done | bytes 1048592 | tf_op jit(solution)/shard_map/psum | solution.py:32
  60.0 1.4 multiply_reduce_fusion.1
  61.4 1.1 fusion.34
  62.6 1.1 fusion.35
  63.8 0.7 fusion.36
  64.5 0.0 all-gather.2.cloned.1.call-update
  64.5 5.6 %all-to-all-start = ((s32[1,16,128]{2,0,1:T(1,128)}), s32[1,16,128]{2,0,1:T(1,128)S(1)}, u32[]{:S(2)}, u32[]{:S(2)}) async-start(s32[1,16,128]{2,0,1:T(1,128)} %bitcast.3), calls=%async_computation | async-start | bytes 16384 | tf_op jit(solution)/shard_map/all_to_all | solution.py:72
  70.2 0.1 copy.29
  70.3 0.1 eq.26
  70.4 0.1 reshape.176
  70.5 0.1 copy.35
  70.6 0.1 mul.236
  70.7 4.5 %reduce-window.6 = s32[16,8,128]{2,1,0:T(8,128)S(1)} reduce-window(s32[16,8,128]{2,1,0:T(8,128)S(1)} %fusion.47, s32[]{:T(128)} %constant.25.clone.1), window={size=1x1x128 pad=0_0x0_0x127_0}, to_apply=%region_5.6 | reduce-window | flops 2080768 | bytes 131076 | tf_op jit(solution)/shard_map/reduce-window
  75.2 0.1 slice.12
  75.3 0.1 copy.31
  75.4 0.1 copy.32
  75.5 0.1 broadcast_add_fusion
  75.7 0.1 reduce_sum.70
  76.5 0.1 all-to-all-done
  76.5 6.1 %gather_fusion = s32[1024]{0:T(1024)S(1)} fusion(s32[2048]{0:T(1024)S(1)} %bitcast.51, s32[1024]{0:T(1024)S(1)} %broadcast_clamp_fusion.1), kind=kCustom, calls=%fused_computation | custom fusion | bytes 12288 | tf_op jit(solution)/shard_map/jit(_take)/gather | solution.py:75
  82.7 0.1 gather.15
  82.9 0.1 copy.37
  83.0 0.0 copy-start.10
  83.0 23.0 %all-gather.2.cloned.1.call-done = bf16[2048,512]{1,0:T(8,128)(2,1)} async-done(((bf16[128,512]{1,0:T(8,128)(2,1)}), bf16[2048,512]{1,0:T(8,128)(2,1)}) %all-gather.2.cloned.1.call-update) | async-done | bytes 2097168 | tf_op jit(solution)/shard_map/all_gather | solution.py:71
  106.1 5.8 %gather_fusion.1 = bf16[1024,512]{1,0:T(8,128)(2,1)S(1)} fusion(bf16[2048,512]{1,0:T(8,128)(2,1)} %all-gather.2.cloned.1.call-done, s32[1024]{0:T(1024)S(1)} %broadcast_clamp_fusion), kind=kCustom, calls=%fused_computation.1 | custom fusion | bytes 2101248 | tf_op jit(solution)/shard_map/jit(_take)/gather | solution.py:76
  111.9 0.8 fusion.18
  112.7 0.1 copy.45
  112.8 5.0 %all-reduce = (f32[128,8]{0,1:T(8,128)S(1)}, f32[128]{0:T(128)S(1)}) all-reduce(f32[128,8]{0,1:T(8,128)S(1)} %bitcast.62, f32[128]{0:T(128)S(1)} %get-tuple-element.8), channel_id=1, replica_groups=mesh['dp'=16,'mp'=2] {'mp'}, use_global_device_ids=true, to_apply=%region_8.9 | all-reduce | flops 1152 | bytes 9216 | tf_op jit(solution)/shard_map/psum | solution.py:82
  117.8 0.1 copy.38
  117.9 0.1 mul.258
  118.0 7.1 %scatter_custom_fusion = bf16[2048,512]{1,0:T(8,128)(2,1)} fusion(s32[1024]{0:T(1024)S(1)} %bitcast.61, f32[128,512]{1,0:T(8,128)S(1)} %get-tuple-element.6, f32[1024]{0:T(1024)S(1)} %mul.258, bf16[]{:T(256)} %constant.42.clone.1), kind=kCustom, calls=%fused_computation.25 | custom fusion | flops 1048576 | bytes 2363394 | tf_op jit(solution)/shard_map/scatter | solution.py:99
  125.1 3.7 %all-to-all-start.1 = ((bf16[16,128,512]{2,1,0:T(8,128)(2,1)}), bf16[16,128,512]{2,1,0:T(8,128)(2,1)S(1)}, u32[]{:S(2)}, u32[]{:S(2)}) async-start(bf16[16,128,512]{2,1,0:T(8,128)(2,1)} %bitcast.53), calls=%async_computation.2 | async-start | bytes 4194304 | tf_op jit(solution)/shard_map/all_to_all | solution.py:101
  128.9 0.0 reduce-scatter.3.cloned.1.call-start
  128.9 0.7 compare_select_fusion
  129.6 2.0 multiply_reduce_fusion
  131.7 0.8 convert_multiply_fusion.4
  132.5 6.5 %all_gather.10 = bf16[128,1024]{1,0:T(8,128)(2,1)S(1)} all-gather(bf16[128,512]{1,0:T(8,128)(2,1)S(1)} %get-tuple-element.13), channel_id=1, replica_groups=mesh['dp'=16,'mp'=2] {'mp'}, dimensions={1}, use_global_device_ids=true | all-gather | bytes 393216 | tf_op jit(solution)/shard_map/all_gather | solution.py:39
  139.0 0.1 fusion.19
  139.2 0.9 fusion.20
  140.1 7.6 %convolution_convert_fusion.1 = bf16[128,1024]{1,0:T(8,128)(2,1)} fusion(bf16[1024,2048]{1,0:T(8,128)(2,1)} %param.10, bf16[2048,1024]{1,0:T(8,128)(2,1)} %param.11, f32[128,2048]{1,0:T(8,128)} %copy-done.3, f32[128,1024]{1,0:T(8,128)} %fusion.20), kind=kOutput, calls=%fused_computation.16 | convolution fusion | flops 1076625408 | bytes 10223616 | tf_op jit(solution)/shard_map/dot_general | solution.py:50
  147.8 0.0 reduce-scatter.3.cloned.1.call-update
  147.8 0.0 reduce-scatter.5.cloned.1.call-start
  147.8 22.1 %all-to-all-done.1 = bf16[16,128,512]{2,1,0:T(8,128)(2,1)S(1)} async-done(((bf16[16,128,512]{2,1,0:T(8,128)(2,1)}), bf16[16,128,512]{2,1,0:T(8,128)(2,1)S(1)}, u32[]{:S(2)}, u32[]{:S(2)}) %all-to-all-start.1) | async-done | bytes 2097184 | tf_op jit(solution)/shard_map/all_to_all | solution.py:101
  169.9 13.0 %scatter_custom_fusion.1 = f32[128,512]{1,0:T(8,128)S(1)} fusion(f32[128,512]{1,0:T(8,128)S(1)} %copy-done.8, s32[2048]{0:T(1024)S(1)} %bitcast.64, bf16[2048,512]{1,0:T(8,128)(2,1)S(1)} %bitcast.52), kind=kCustom, calls=%fused_computation.4 | custom fusion | flops 2097152 | bytes 2359296 | tf_op jit(solution)/shard_map/scatter-add | solution.py:112
  182.9 6.8 %all_gather.11 = bf16[128,1024]{1,0:T(8,128)(2,1)S(1)} all-gather(bf16[128,512]{1,0:T(8,128)(2,1)S(1)} %convert_element_type.111), channel_id=1, replica_groups=mesh['dp'=16,'mp'=2] {'mp'}, dimensions={1}, use_global_device_ids=true | all-gather | bytes 393216 | tf_op jit(solution)/shard_map/all_gather | solution.py:39
  189.7 0.1 fusion.21
  189.9 0.1 fusion.22
  190.0 7.5 %convolution_convert_fusion = bf16[128,1024]{1,0:T(8,128)(2,1)} fusion(bf16[1024,2048]{1,0:T(8,128)(2,1)} %param.10, bf16[2048,1024]{1,0:T(8,128)(2,1)} %param.11, f32[128,2048]{1,0:T(8,128)} %copy-done.2, f32[128,1024]{1,0:T(8,128)S(1)} %fusion.22), kind=kOutput, calls=%fused_computation.15 | convolution fusion | flops 1076625408 | bytes 10223616 | tf_op jit(solution)/shard_map/dot_general | solution.py:50
  197.5 0.0 reduce-scatter.5.cloned.1.call-update
  197.6 0.0 reduce-scatter.3.cloned.1.call-done
  197.6 1.6 add_convert_fusion.1
  199.2 16.2 %reduce-scatter.5.cloned.1.call-done = bf16[128,512]{1,0:T(8,128)(2,1)} async-done(((bf16[128,1024]{1,0:T(8,128)(2,1)}), bf16[128,512]{1,0:T(8,128)(2,1)}) %reduce-scatter.5.cloned.1.call-update) | async-done | bytes 131088 | tf_op jit(solution)/shard_map/reduce_scatter | solution.py:51
  215.4 1.6 add_convert_fusion
  (36 shorter events, 0.4 us)
Async XLA Ops:
  7.2 3.2 %copy-start.4 = (bf16[128,1024]{1,0:T(8,128)(2,1)S(1)}, bf16[128,1024]{1,0:T(8,128)(2,1)}, u32[]{:S(2)}) copy-start(bf16[128,1024]{1,0:T(8,128)(2,1)} %param.8) | copy-start | bytes 786436
  7.2 52.8 %all-reduce.4.cloned.1.call-start = ((), (), s32[]{:S(2)}) async-start(), calls=%async_computation.7 | async-start | bytes 2097152 | tf_op jit(solution)/shard_map/psum | solution.py:32
  7.2 6.5 %copy-start = (bf16[2048,1024]{1,0:T(8,128)(2,1)S(1)}, bf16[2048,1024]{1,0:T(8,128)(2,1)}, u32[]{:S(2)}) copy-start(bf16[2048,1024]{1,0:T(8,128)(2,1)} %param.11) | copy-start | bytes 12582916
  10.4 4.9 %copy-start.2 = (f32[128,2048]{1,0:T(8,128)}, f32[128,2048]{1,0:T(8,128)S(1)}, u32[]{:S(2)}) copy-start(f32[128,2048]{1,0:T(8,128)S(1)} %fusion.62) | copy-start | bytes 3145732
  13.7 1.6 copy-start.3
  15.3 44.7 %copy-start.5 = (bf16[128,1024]{1,0:T(8,128)(2,1)S(1)}, bf16[128,1024]{1,0:T(8,128)(2,1)}, u32[]{:S(2)}) copy-start(bf16[128,1024]{1,0:T(8,128)(2,1)} %param.9) | copy-start | bytes 786436
  16.9 53.2 %copy-start.9 = (s32[128,8]{0,1:T(8,128)S(1)}, s32[128,8]{0,1:T(8,128)}, u32[]{:S(2)}) copy-start(s32[128,8]{0,1:T(8,128)} %param.12) | copy-start | bytes 12292
  16.9 89.1 %all-gather.2.cloned.1.call-start = ((), (), s32[]{:S(2)}) async-start(), calls=%async_computation.4 | async-start | bytes 2228224 | tf_op jit(solution)/shard_map/all_gather | solution.py:71
  64.5 12.0 %all-to-all-start = ((s32[1,16,128]{2,0,1:T(1,128)}), s32[1,16,128]{2,0,1:T(1,128)S(1)}, u32[]{:S(2)}, u32[]{:S(2)}) async-start(s32[1,16,128]{2,0,1:T(1,128)} %bitcast.3), calls=%async_computation | async-start | bytes 16384 | tf_op jit(solution)/shard_map/all_to_all | solution.py:72
  83.0 34.7 %copy-start.10 = (s32[128,8]{0,1:T(8,128)S(1)}, s32[128,8]{0,1:T(8,128)}, u32[]{:S(2)}) copy-start(s32[128,8]{0,1:T(8,128)} %param.13) | copy-start | bytes 12292
  111.9 13.2 %copy-start.1 = (bf16[1024,512]{1,0:T(8,128)(2,1)}, bf16[1024,512]{1,0:T(8,128)(2,1)S(1)}, u32[]{:S(2)}) copy-start(bf16[1024,512]{1,0:T(8,128)(2,1)S(1)} %gather_fusion.1) | copy-start | bytes 3145732
  112.7 19.0 %copy-start.6 = (bf16[128,512]{1,0:T(8,128)(2,1)S(1)}, bf16[128,512]{1,0:T(8,128)(2,1)}, u32[]{:S(2)}) copy-start(bf16[128,512]{1,0:T(8,128)(2,1)} %get-tuple-element.9) | copy-start | bytes 393220
  125.1 44.8 %all-to-all-start.1 = ((bf16[16,128,512]{2,1,0:T(8,128)(2,1)}), bf16[16,128,512]{2,1,0:T(8,128)(2,1)S(1)}, u32[]{:S(2)}, u32[]{:S(2)}) async-start(bf16[16,128,512]{2,1,0:T(8,128)(2,1)} %bitcast.53), calls=%async_computation.2 | async-start | bytes 4194304 | tf_op jit(solution)/shard_map/all_to_all | solution.py:101
  128.9 68.7 %reduce-scatter.3.cloned.1.call-start = ((), (), s32[]{:S(2)}) async-start(), calls=%async_computation.5 | async-start | bytes 393216 | tf_op jit(solution)/shard_map/reduce_scatter | solution.py:51
  140.1 29.8 %copy-start.8 = (f32[128,512]{1,0:T(8,128)S(1)}, f32[128,512]{1,0:T(8,128)}, u32[]{:S(2)}) copy-start(f32[128,512]{1,0:T(8,128)} %get-tuple-element.12) | copy-start | bytes 786436
  147.8 67.6 %reduce-scatter.5.cloned.1.call-start = ((), (), s32[]{:S(2)}) async-start(), calls=%async_computation.6 | async-start | bytes 393216 | tf_op jit(solution)/shard_map/reduce_scatter | solution.py:51
  190.0 7.6 %copy-start.7 = (f32[128,1024]{1,0:T(8,128)S(1)}, f32[128,1024]{1,0:T(8,128)}, u32[]{:S(2)}) copy-start(f32[128,1024]{1,0:T(8,128)} %fusion.20) | copy-start | bytes 1572868
Sparse Core Ops, SparseCore 0:
  17.1 42.9 all-reduce.3
  64.6 41.3 all-gather.1
  147.9 12.7 reduce-scatter.2
  197.7 17.6 reduce-scatter.4
where the time goes:
time: 224 us
  waiting for transfers between devices  104 us (46%)
  other arithmetic  37.5 us (17%)
  matrix products  25.5 us (11%)
  blocking collectives  18.4 us (8%)
  between operations  14.8 us (7%)
  local copies, waits for them, and re-layouts  13.4 us (6%)
  starting transfers between devices  9.51 us (4%)
    psum x1, waiting for transfers between devices, encode(): mixed_sum = lax.psum(partial_out, 'mp')  43 us
    all_gather x1, waiting for transfers between devices, shards(): every_emb = lax.all_gather(emb_pass, 'dp', axis=0, tiled=True)  23 us
    all_to_all x1, waiting for transfers between devices, shards(): lax.all_to_all(outgoing_grad.reshape(owners, capacity, column_width), 'dp...  22.1 us
    reduce_scatter x2, waiting for transfers between devices, decode(): lax.psum_scatter(partial_in.astype(jnp.bfloat16), 'mp', scatter_dimension...  16.2 us
    dot_general x2, matrix products, decode(): lax.dot_general(grad_pre, w_in, contract, preferred_element_type=jnp.floa...  15.1 us
    all_gather x2, blocking collectives, decode(): lax.all_gather(grad_part.astype(jnp.bfloat16), 'mp', axis=1, tiled=True)  13.4 us
    scatter-add x1, other arithmetic, shards(): gathered_back = jnp.zeros((row_count, column_width), jnp.float32).at[serv...  13 us
    scatter x1, other arithmetic, shards(): jnp.zeros((owners * capacity, column_width), jnp.bfloat16).at[slot_place]  7.1 us
  transfers between devices with their start and end apart: 6, of which 5 were waited for; matrix products, arithmetic and copies ran while one was open for 21% of the time, Pallas kernels for 0%

commit v1 on v0

--- a/solution.py
+++ b/solution.py
@@ -1,12 +1,21 @@
+import functools
+
 import jax
 import jax.numpy as jnp
 from jax import lax
+from jax.experimental import pallas as pl
+from jax.experimental.pallas import tpu as pltpu
 from jax.sharding import PartitionSpec as P
 
 logit_scale = 50.0
 norm_eps = 1e-06
 root_half = 0.7071067811865476
 inv_root_two_pi = 0.3989422804014327
+f32, bf16 = jnp.float32, jnp.bfloat16
+nt = (((1,), (1,)), ((), ()))
+tn = (((0,), (0,)), ((), ()))
+vmem = pl.BlockSpec(memory_space=pltpu.VMEM)
+smem = pl.BlockSpec(memory_space=pltpu.SMEM)
 
 
 def gelu_value(values):
@@ -42,19 +51,20 @@
     grad_out = inv_norm * (
         grad_emb - unit_rows * jnp.sum(unit_rows * grad_emb, axis=1, keepdims=True)
     )
-    contract = (((1,), (1,)), ((), ()))
     grad_hidden = lax.dot_general(
-        grad_out.astype(jnp.bfloat16), w_out, contract, preferred_element_type=jnp.float32
+        grad_out.astype(jnp.bfloat16), w_out, nt, preferred_element_type=jnp.float32
     )
     grad_pre = (grad_hidden * gelu_slope(pre_act)).astype(jnp.bfloat16)
-    partial_in = lax.dot_general(grad_pre, w_in, contract, preferred_element_type=jnp.float32)
+    partial_in = lax.dot_general(grad_pre, w_in, nt, preferred_element_type=jnp.float32)
     summed = lax.psum_scatter(
         partial_in.astype(jnp.bfloat16), "mp", scatter_dimension=1, tiled=True
     ).astype(jnp.float32)
     return (summed + own_columns(grad_out)).astype(jnp.bfloat16)
 
 
-def shards(query_states, passage_states, w_in, w_out, neg_owner, neg_mask, served_rows, loss_scale):
+def general_shards(
+    query_states, passage_states, w_in, w_out, neg_owner, neg_mask, served_rows, loss_scale
+):
     owners = lax.axis_size("dp")
     row_count = query_states.shape[0]
     negatives = neg_owner.shape[1]
@@ -116,6 +126,445 @@
     return (grad_query_states, grad_passage_states)
 
 
+both_bits, query_bits, pass_bits = (2, 1), (4,), (8,)
+
+
+def swap(values, axis, bit):
+    size = lax.axis_size(axis)
+    return lax.ppermute(values, axis, [(i, i ^ bit) for i in range(size)])
+
+
+def gather_blocks(block, bits):
+    blocks = {0: block}
+    for bit in bits:
+        blocks.update({at | bit: swap(values, "dp", bit) for at, values in list(blocks.items())})
+    return blocks
+
+
+def halves(first, values):
+    width = values.shape[1] // 2
+    left, right = values[:, :width], values[:, width:]
+    return jnp.where(first, left, right), jnp.where(first, right, left)
+
+
+def encode_kernel(
+    me, xq, xp, w_in, w_out, owner, mask, served,
+    send_q, send_p, own_q, own_p, slope, slots_out, served_out,
+    states, total,
+):
+    step = pl.program_id(0)
+    rows = xq.shape[0]
+
+    @pl.when(step == 0)
+    def _():
+        states[:rows, :] = xq[...]
+        states[rows:, :] = xp[...]
+        total[...] = jnp.zeros_like(total)
+        lane = lax.broadcasted_iota(jnp.int32, (rows, 128), 1)
+        named = jnp.zeros((rows, 128), f32)
+        live = jnp.zeros((rows, 128), f32)
+        for j in range(owner.shape[1]):
+            hit = (owner[:, j : j + 1] == lane).astype(f32)
+            named = named + hit
+            live = live + hit * mask[:, j : j + 1].astype(f32)
+        earlier = lax.broadcasted_iota(jnp.int32, (rows, rows), 0) < lax.broadcasted_iota(
+            jnp.int32, (rows, rows), 1
+        )
+        slot = jnp.dot(
+            named.T.astype(bf16), earlier.astype(f32).astype(bf16), preferred_element_type=f32
+        )
+        slot = jnp.where(live.T > 0.5, slot, -1.0)
+        slots_out[...] = slot[: slots_out.shape[0], :].astype(bf16)
+        served_out[...] = served[0].astype(f32).astype(bf16)
+
+    pre = jnp.dot(states[...], w_in[...], preferred_element_type=f32)
+    cdf = 0.5 * (1.0 + lax.erf(pre * root_half))
+    slope[...] = (cdf + pre * jnp.exp(-0.5 * pre * pre) * inv_root_two_pi).astype(bf16)
+    total[...] += jnp.dot((pre * cdf).astype(bf16), w_out[...], preferred_element_type=f32)
+
+    @pl.when(step == pl.num_programs(0) - 1)
+    def _():
+        first = me[0] == 0
+        for at, x, send, own in ((0, xq, send_q, own_q), (rows, xp, send_p, own_p)):
+            mine, theirs = halves(first, total[at : at + rows, :])
+            send[...] = theirs.astype(bf16)
+            own[...] = mine + halves(first, x[...].astype(f32))[0]
+
+
+def encode_both(me, xq, xp, w_in, w_out, owner, mask, served):
+    rows, width = xq.shape
+    hidden = w_in.shape[1]
+    tile = min(512, hidden)
+    owners = served.shape[1]
+
+    def whole(shape):
+        return pl.BlockSpec(shape, lambda t: (0,) * len(shape))
+
+    half = (rows, width // 2)
+    return pl.pallas_call(
+        encode_kernel,
+        grid=(hidden // tile,),
+        in_specs=[
+            smem,
+            whole(xq.shape),
+            whole(xp.shape),
+            pl.BlockSpec((width, tile), lambda t: (0, t)),
+            pl.BlockSpec((tile, width), lambda t: (t, 0)),
+            whole(owner.shape),
+            whole(mask.shape),
+            whole(served.shape),
+        ],
+        out_specs=[
+            whole(half),
+            whole(half),
+            whole(half),
+            whole(half),
+            pl.BlockSpec((2 * rows, tile), lambda t: (0, t)),
+            whole((owners, rows)),
+            whole((owners, served.shape[2])),
+        ],
+        out_shape=[
+            jax.ShapeDtypeStruct(half, bf16),
+            jax.ShapeDtypeStruct(half, bf16),
+            jax.ShapeDtypeStruct(half, f32),
+            jax.ShapeDtypeStruct(half, f32),
+            jax.ShapeDtypeStruct((2 * rows, hidden), bf16),
+            jax.ShapeDtypeStruct((owners, rows), bf16),
+            jax.ShapeDtypeStruct((owners, served.shape[2]), bf16),
+        ],
+        scratch_shapes=[pltpu.VMEM((2 * rows, width), bf16), pltpu.VMEM((2 * rows, width), f32)],
+        compiler_params=pltpu.CompilerParams(vmem_limit_bytes=24 << 20),
+        name="encode_both",
+    )(me, xq, xp, w_in, w_out, owner, mask, served)
+
+
+def pack_kernel(own, other, numbers, out):
+    rows = own.shape[0]
+    out[:rows, :] = (own[...] + other[...].astype(f32)).astype(bf16)
+    out[rows:, :] = jnp.zeros((out.shape[0] - rows, out.shape[1]), bf16)
+    out[rows:, : numbers.shape[1]] = numbers[...]
+
+
+def pack(own, other, numbers):
+    return pl.pallas_call(
+        pack_kernel,
+        in_specs=[vmem] * 3,
+        out_specs=vmem,
+        out_shape=jax.ShapeDtypeStruct((own.shape[0] + numbers.shape[0], own.shape[1]), bf16),
+        name="pack",
+    )(own, other, numbers)
+
+
+def eye_of(size):
+    return (
+        lax.broadcasted_iota(jnp.int32, (size, size), 0)
+        == lax.broadcasted_iota(jnp.int32, (size, size), 1)
+    ).astype(f32)
+
+
+def score_kernel(q_at, p_at, owners, rows, ids, *refs):
+    nq, npass = len(q_at), len(p_at)
+    q_refs, p_refs = refs[:nq], refs[nq : nq + npass]
+    table, valid, pick_p, pick_q, q_all, p_all, slots, served = refs[nq + npass :]
+    for n, ref in enumerate(q_refs):
+        q_all[n * rows : (n + 1) * rows, :] = ref[:rows, :]
+        slots[n * owners : (n + 1) * owners, :] = ref[rows:, :128].astype(f32)
+    for n, ref in enumerate(p_refs):
+        p_all[n * rows : (n + 1) * rows, :] = ref[:rows, :]
+        served[n * owners : (n + 1) * owners, :] = ref[rows:, :128].astype(f32)
+    table[...] = jnp.zeros_like(table)
+    eye = eye_of(rows)
+    down = lax.broadcasted_iota(jnp.int32, (rows, rows), 0).astype(f32)
+    queries = q_all[...]
+    for b in range(nq):
+        block = q_all[b * rows : (b + 1) * rows, :].astype(f32)
+        square = jnp.sum(block * block, axis=1, keepdims=True)
+        table[2 * npass : 2 * npass + 1, b * rows : (b + 1) * rows] = jnp.sum(
+            eye * square, axis=0, keepdims=True
+        )
+    for a in range(npass):
+        part = p_all[a * rows : (a + 1) * rows, :]
+        block = part.astype(f32)
+        square = jnp.sum(block * block, axis=1, keepdims=True)
+        scores = lax.dot_general(part, queries, nt, preferred_element_type=f32)
+        owner = ids[1, a]
+        for b in range(nq):
+            lanes = slice(b * rows, (b + 1) * rows)
+            here = scores[:, lanes]
+            if q_at[b] == p_at[a]:
+                table[2 * npass + 1 : 2 * npass + 2, lanes] = jnp.sum(
+                    eye * here, axis=0, keepdims=True
+                )
+                table[2 * npass + 2 : 2 * npass + 3, lanes] = jnp.sum(
+                    eye * square, axis=0, keepdims=True
+                )
+            row_of = served[pl.ds(a * owners + ids[0, b], 1), :]
+            slot_of = slots[pl.ds(b * owners + owner, 1), :]
+            by_slot = (down == row_of).astype(f32).astype(bf16)
+            by_query = (down == slot_of).astype(f32).astype(bf16)
+            chosen = jnp.dot(by_slot, by_query, preferred_element_type=f32)
+            table[a : a + 1, lanes] = jnp.sum(chosen * here, axis=0, keepdims=True)
+            table[npass + a : npass + a + 1, lanes] = jnp.sum(
+                chosen * square, axis=0, keepdims=True
+            )
+            valid[a : a + 1, lanes] = (slot_of >= 0.0).astype(f32)
+            if p_at[a] in (0,) + pass_bits:
+                n = ((0,) + pass_bits).index(p_at[a])
+                pick_p[n * rows : (n + 1) * rows, lanes] = chosen.astype(bf16)
+            if q_at[b] in (0,) + query_bits:
+                n = ((0,) + query_bits).index(q_at[b])
+                pick_q[a * rows : (a + 1) * rows, n * rows : (n + 1) * rows] = chosen.astype(bf16)
+
+
+def score(ids, q_blocks, p_blocks, rows, owners):
+    q_at, p_at = sorted(q_blocks), sorted(p_blocks)
+    nq, npass = len(q_at), len(p_at)
+    width = q_blocks[0].shape[1]
+    table_rows = -(-(2 * npass + 3) // 8) * 8
+    kernel = functools.partial(score_kernel, q_at, p_at, owners, rows)
+    return pl.pallas_call(
+        kernel,
+        in_specs=[smem] + [vmem] * (nq + npass),
+        out_specs=[vmem] * 6,
+        out_shape=[
+            jax.ShapeDtypeStruct((table_rows, nq * rows), f32),
+            jax.ShapeDtypeStruct((npass, nq * rows), f32),
+            jax.ShapeDtypeStruct(((1 + len(pass_bits)) * rows, nq * rows), bf16),
+            jax.ShapeDtypeStruct((npass * rows, (1 + len(query_bits)) * rows), bf16),
+            jax.ShapeDtypeStruct((nq * rows, width), bf16),
+            jax.ShapeDtypeStruct((npass * rows, width), bf16),
+        ],
+        scratch_shapes=[pltpu.VMEM((nq * owners, 128), f32), pltpu.VMEM((npass * owners, 128), f32)],
+        compiler_params=pltpu.CompilerParams(vmem_limit_bytes=32 << 20),
+        name="score",
+    )(ids, *[q_blocks[b] for b in q_at], *[p_blocks[a] for a in p_at])
+
+
+def weigh_kernel(npass, has_pos, rows, table, other, valid, coefs, sums):
+    full = table[...] + other[...]
+    raw, square = full[:npass], full[npass : 2 * npass]
+    inv_q = lax.rsqrt(full[2 * npass : 2 * npass + 1] + norm_eps)
+    inv_pos = lax.rsqrt(full[2 * npass + 2 : 2 * npass + 3] + norm_eps)
+    inv_neg = lax.rsqrt(square + norm_eps)
+    exp_neg = valid[...] * jnp.exp(logit_scale * (raw * inv_q * inv_neg))
+    lane = lax.broadcasted_iota(jnp.int32, inv_q.shape, 1)
+    with_pos = lane < 0
+    for n, has in enumerate(has_pos):
+        if has:
+            with_pos = with_pos | ((lane >= n * rows) & (lane < (n + 1) * rows))
+    exp_pos = jnp.where(
+        with_pos, jnp.exp(logit_scale * (full[2 * npass + 1 : 2 * npass + 2] * inv_q * inv_pos)), 0.0
+    )
+    coefs[...] = jnp.zeros_like(coefs)
+    coefs[:npass] = exp_neg
+    coefs[npass : 2 * npass] = exp_neg * inv_neg
+    coefs[2 * npass : 2 * npass + 1] = inv_q
+    coefs[2 * npass + 1 : 2 * npass + 2] = inv_pos
+    neg_sum = jnp.sum(exp_neg, axis=0, keepdims=True)
+    count = len(has_pos)
+    for n in range(count):
+        lanes = slice(n * rows, (n + 1) * rows)
+        sums[n : n + 1, :] = neg_sum[:, lanes]
+        sums[count + n : count + n + 1, :] = exp_pos[:, lanes]
+
+
+def weigh(table, other, valid, has_pos, rows):
+    return pl.pallas_call(
+        functools.partial(weigh_kernel, valid.shape[0], has_pos, rows),
+        in_specs=[vmem] * 3,
+        out_specs=[vmem] * 2,
+        out_shape=[
+            jax.ShapeDtypeStruct(table.shape, f32),
+            jax.ShapeDtypeStruct((2 * len(has_pos), rows), f32),
+        ],
+        name="weigh",
+    )(table, other, valid)
+
+
+def shares(sums, other, order, scale):
+    count = len(order)
+    theirs = jnp.concatenate([other[n : n + 1] for n in order], axis=0)
+    theirs_pos = jnp.concatenate([other[count + n : count + n + 1] for n in order], axis=0)
+    neg = sums[:count] + theirs
+    total = neg + sums[count:] + theirs_pos
+    share = scale * logit_scale / total
+    return share, -share * neg
+
+
+def grad_pass_kernel(order, q_at, npass, scale, coefs, sums, other, pick, q_all, own, send):
+    rows = own.shape[0]
+    share, pos = shares(sums[...], other[...], order, scale[0])
+    share = jnp.concatenate([share[n : n + 1] for n in range(len(q_at))], axis=1)
+    scaled = share * coefs[2 * npass : 2 * npass + 1]
+    queries = q_all[...]
+    for n, (a, out) in enumerate(((0, own), (npass // 2, send))):
+        weights = pick[n * rows : (n + 1) * rows, :].astype(f32) * (coefs[a : a + 1] * scaled)
+        if n == 0:
+            diagonal = eye_of(rows) * (pos[:1] * coefs[2 * npass : 2 * npass + 1, :rows])
+            weights = jnp.concatenate([weights[:, :rows] + diagonal, weights[:, rows:]], axis=1)
+        out[...] = jnp.dot(weights.astype(bf16), queries, preferred_element_type=f32).astype(out.dtype)
+
+
+def grad_query_kernel(order, q_at, npass, scale, coefs, sums, other, pick, p_all, own, send):
+    rows = own.shape[0]
+    share, pos = shares(sums[...], other[...], order, scale[0])
+    passages = p_all[...]
+    for n, (b, out) in enumerate(((0, own), (len(q_at) // 2, send))):
+        lanes = slice(b * rows, (b + 1) * rows)
+        pieces = []
+        for a in range(npass):
+            piece = pick[a * rows : (a + 1) * rows, n * rows : (n + 1) * rows].astype(f32) * (
+                coefs[npass + a : npass + a + 1, lanes] * share[b : b + 1]
+            )
+            if n == 0 and a == 0:
+                piece = piece + eye_of(rows) * (pos[:1] * coefs[2 * npass + 1 : 2 * npass + 2, :rows])
+            pieces.append(piece.T.astype(bf16))
+        weights = jnp.concatenate(pieces, axis=1)
+        out[...] = jnp.dot(weights, passages, preferred_element_type=f32).astype(out.dtype)
+
+
+def spread(kernel, name, scale, coefs, sums, other, pick, blocks, rows):
+    half = (rows, blocks.shape[1])
+    return pl.pallas_call(
+        kernel,
+        in_specs=[smem] + [vmem] * 5,
+        out_specs=[vmem] * 2,
+        out_shape=[jax.ShapeDtypeStruct(half, f32), jax.ShapeDtypeStruct(half, bf16)],
+        compiler_params=pltpu.CompilerParams(vmem_limit_bytes=32 << 20),
+        name=name,
+    )(scale, coefs, sums, other, pick, blocks)
+
+
+def add_kernel(own, other, out):
+    out[...] = (own[...] + other[...].astype(f32)).astype(out.dtype)
+
+
+def add_round(own, other, name):
+    return pl.pallas_call(
+        add_kernel,
+        in_specs=[vmem] * 2,
+        out_specs=vmem,
+        out_shape=jax.ShapeDtypeStruct(own.shape, bf16),
+        name=name,
+    )(own, other)
+
+
+def decode_kernel(
+    me, grad, grad_other, raw, raw_other, slope, w_in, w_out, send, own, grad_out, total
+):
+    step = pl.program_id(0)
+    first = me[0] == 0
+    rows, width = grad.shape
+
+    def joined(mine, theirs):
+        mine, theirs = mine.astype(f32), theirs.astype(f32)
+        return jnp.concatenate(
+            [jnp.where(first, mine, theirs), jnp.where(first, theirs, mine)], axis=1
+        )
+
+    def out_grad():
+        grads = joined(grad[...], grad_other[...])
+        values = joined(raw[:rows, :], raw_other[:rows, :])
+        inv_norm = lax.rsqrt(jnp.sum(values * values, axis=1, keepdims=True) + norm_eps)
+        unit = values * inv_norm
+        return inv_norm * (grads - unit * jnp.sum(unit * grads, axis=1, keepdims=True))
+
+    @pl.when(step == 0)
+    def _():
+        grad_out[...] = out_grad()
+        total[...] = jnp.zeros_like(total)
+
+    hidden = lax.dot_general(
+        grad_out[...].astype(bf16), w_out[...], nt, preferred_element_type=f32
+    )
+    grad_pre = (hidden * slope[...].astype(f32)).astype(bf16)
+    total[...] += lax.dot_general(grad_pre, w_in[...], nt, preferred_element_type=f32)
+
+    @pl.when(step == pl.num_programs(0) - 1)
+    def _():
+        mine, theirs = halves(first, total[...])
+        send[...] = theirs.astype(bf16)
+        own[...] = mine + halves(first, grad_out[...])[0]
+
+
+def decode_one(me, grad, grad_other, raw, raw_other, slope, tower, w_in, w_out):
+    rows, half = grad.shape
+    width, hidden = w_in.shape
+    tile = min(512, hidden)
+
+    def whole(shape):
+        return pl.BlockSpec(shape, lambda t: (0,) * len(shape))
+
+    return pl.pallas_call(
+        decode_kernel,
+        grid=(hidden // tile,),
+        in_specs=[
+            smem,
+            whole(grad.shape),
+            whole(grad.shape),
+            whole(raw.shape),
+            whole(raw.shape),
+            pl.BlockSpec((rows, tile), lambda t: (tower, t)),
+            pl.BlockSpec((width, tile), lambda t: (0, t)),
+            pl.BlockSpec((tile, width), lambda t: (t, 0)),
+        ],
+        out_specs=[whole(grad.shape)] * 2,
+        out_shape=[
+            jax.ShapeDtypeStruct(grad.shape, bf16),
+            jax.ShapeDtypeStruct(grad.shape, f32),
+        ],
+        scratch_shapes=[pltpu.VMEM((rows, width), f32), pltpu.VMEM((rows, width), f32)],
+        compiler_params=pltpu.CompilerParams(vmem_limit_bytes=24 << 20),
+        name="decode_one",
+    )(me, grad, grad_other, raw, raw_other, slope, w_in, w_out)
+
+
+def paired_shards(
+    query_states, passage_states, w_in, w_out, neg_owner, neg_mask, served_rows, loss_scale
+):
+    rows = query_states.shape[0]
+    owners = served_rows.shape[1]
+    me = lax.axis_index("mp").astype(jnp.int32).reshape(1)
+    place = lax.axis_index("dp").astype(jnp.int32)
+    send_q, send_p, own_q, own_p, slope, slots, served = encode_both(
+        me, query_states, passage_states, w_in, w_out, neg_owner, neg_mask, served_rows
+    )
+    raw_q = pack(own_q, swap(send_q, "mp", 1), slots)
+    raw_p = pack(own_p, swap(send_p, "mp", 1), served)
+    q_blocks = gather_blocks(raw_q, query_bits + both_bits)
+    p_blocks = gather_blocks(raw_p, pass_bits + both_bits)
+    raw_q_other, raw_p_other = swap(raw_q, "mp", 1), swap(raw_p, "mp", 1)
+
+    q_at, p_at = sorted(q_blocks), sorted(p_blocks)
+    ids = jnp.stack([place ^ jnp.array(q_at, jnp.int32), place ^ jnp.array(p_at, jnp.int32)])
+    table, valid, pick_p, pick_q, q_all, p_all = score(ids, q_blocks, p_blocks, rows, owners)
+    has_pos = tuple(at in p_at for at in q_at)
+    coefs, sums = weigh(table, swap(table, "mp", 1), valid, has_pos, rows)
+    other = swap(sums, "dp", query_bits[0])
+    order = tuple(q_at.index(at ^ query_bits[0]) for at in q_at)
+    scale = loss_scale.reshape(1)
+    pass_kernel = functools.partial(grad_pass_kernel, order, q_at, len(p_at))
+    query_kernel = functools.partial(grad_query_kernel, order, q_at, len(p_at))
+    mine_p, theirs_p = spread(
+        pass_kernel, "grad_pass", scale, coefs, sums, other, pick_p, q_all, rows
+    )
+    mine_q, theirs_q = spread(
+        query_kernel, "grad_query", scale, coefs, sums, other, pick_q, p_all, rows
+    )
+    grad_p = add_round(mine_p, swap(theirs_p, "dp", pass_bits[0]), "sum_pass")
+    grad_q = add_round(mine_q, swap(theirs_q, "dp", query_bits[0]), "sum_query")
+    send_q, own_q = decode_one(
+        me, grad_q, swap(grad_q, "mp", 1), raw_q, raw_q_other, slope, 0, w_in, w_out
+    )
+    send_p, own_p = decode_one(
+        me, grad_p, swap(grad_p, "mp", 1), raw_p, raw_p_other, slope, 1, w_in, w_out
+    )
+    return (
+        add_round(own_q, swap(send_q, "mp", 1), "out_query"),
+        add_round(own_p, swap(send_p, "mp", 1), "out_pass"),
+    )
+
+
 def solution(mesh):
     in_specs = (
         P("dp", None),
@@ -128,4 +577,7 @@
         P(),
     )
     out_specs = (P("dp", "mp"), P("dp", "mp"))
+    gathered = sum(both_bits + query_bits + pass_bits) + 1
+    paired = mesh.shape["mp"] == 2 and mesh.shape["dp"] == gathered
+    shards = paired_shards if paired else general_shards
     return jax.shard_map(shards, mesh=mesh, in_specs=in_specs, out_specs=out_specs, check_vma=False)

time: 224 us -> 122 us (0.54)
  waiting for transfers between devices: 104 us -> 19.9 us
  other arithmetic: 37.5 us -> 0.01 us
  local copies, waits for them, and re-layouts: 13.4 us -> 45 us
  Pallas kernels: 0 us -> 30.3 us
  matrix products: 25.5 us -> 0 us
  blocking collectives: 18.4 us -> 0 us
  starting transfers between devices: 9.51 us -> 24.3 us
  between operations: 14.8 us -> 1.5 us
    unnamed x23 -> x112, local copies, waits for them, and re-layouts: 0.15 us -> 45 us
    psum x1 -> x0, waiting for transfers between devices: 43 us -> none  [encode(): mixed_sum = lax.psum(partial_out, 'mp')]
    pallas_call x0 -> x13, Pallas kernels: none -> 30.3 us  [the longest x2 8.34 us: decode_one(): pl.pallas_call(decode_kernel, grid=(hidden // tile,), in_specs=[smem, who...]
    dot_general x7 -> x0, matrix products: 25.5 us -> none  [the longest x2 15.1 us: decode(): lax.dot_general(grad_pre, w_in, contract, preferred_element_type=jnp.floa...]
    ppermute x0 -> x26, starting transfers between devices: none -> 24.3 us  [swap(): return lax.ppermute(values, axis, [(i, i ^ bit) for i in range(size)])]
    all_gather x1 -> x0, waiting for transfers between devices: 23 us -> none  [shards(): every_emb = lax.all_gather(emb_pass, 'dp', axis=0, tiled=True)]
    all_to_all x2 -> x0, waiting for transfers between devices: 22.1 us -> none  [the longest x1 22.1 us: shards(): lax.all_to_all(outgoing_grad.reshape(owners, capacity, column_width), 'dp...]
    ppermute x0 -> x26, waiting for transfers between devices: none -> 19.9 us  [swap(): return lax.ppermute(values, axis, [(i, i ^ bit) for i in range(size)])]
  transfers between devices with their start and end apart: 6 -> 26, of which waited for: 5 -> 10; matrix products, arithmetic and copies ran while one was open for 21% -> 0% of each run, Pallas kernels for 0% -> 14%
where the time goes in v1:
time: 122 us; the launch traced here: 121 us
  local copies, waits for them, and re-layouts  45 us (37%)
  Pallas kernels  30.3 us (25%)
  starting transfers between devices  24.3 us (20%)
  waiting for transfers between devices  19.9 us (16%)
  between operations  1.5 us (1%)
    unnamed x112, local copies, waits for them, and re-layouts  45 us
    ppermute x26, starting transfers between devices, swap(): return lax.ppermute(values, axis, [(i, i ^ bit) for i in range(size)])  24.3 us
    ppermute x26, waiting for transfers between devices, swap(): return lax.ppermute(values, axis, [(i, i ^ bit) for i in range(size)])  19.9 us
    pallas_call x2, Pallas kernels, decode_one(): pl.pallas_call(decode_kernel, grid=(hidden // tile,), in_specs=[smem, who...  8.34 us
    pallas_call x4, Pallas kernels, add_round(): pl.pallas_call(add_kernel, in_specs=[vmem] * 2, out_specs=vmem, out_shape...  6.64 us
    pallas_call x1, Pallas kernels, encode_both(): pl.pallas_call(encode_kernel, grid=(hidden // tile,), in_specs=[smem, who...  4.89 us
    pallas_call x1, Pallas kernels, score(): pl.pallas_call(kernel, in_specs=[smem] + [vmem] * (nq + npass), out_specs...  4.38 us
    pallas_call x2, Pallas kernels, pack(): pl.pallas_call(pack_kernel, in_specs=[vmem] * 3, out_specs=vmem, out_shap...  3.4 us
  transfers between devices with their start and end apart: 26, of which 10 were waited for; matrix products, arithmetic and copies ran while one was open for 0% of the time, Pallas kernels for 14%

profile of v1, /device:TPU:0, one launch (start us, length us, event | category | flops | bytes accessed | tf_op | source)
XLA Modules:
  0.0 120.9 jit_solution(17459205191619709922)
XLA Ops:
  0.6 0.8 copy.12.owner
  1.4 0.8 copy.13.mask
  2.2 2.2 %copy-done = bf16[1024,2048]{1,0:T(8,128)(2,1)S(1)} copy-done((bf16[1024,2048]{1,0:T(8,128)(2,1)S(1)}, bf16[1024,2048]{1,0:T(8,128)(2,1)}, u32[]{:S(2)}) %copy-start) | copy-done | bytes 4194328
  4.4 2.2 %copy-done.2 = bf16[2048,1024]{1,0:T(8,128)(2,1)S(1)} copy-done((bf16[2048,1024]{1,0:T(8,128)(2,1)S(1)}, bf16[2048,1024]{1,0:T(8,128)(2,1)}, u32[]{:S(2)}) %copy-start.2) | copy-done | bytes 4194328
  6.6 0.9 copy-done.21
  7.5 0.9 copy-done.22
  8.5 0.7 copy-done.44
  9.2 4.9 %encode_both.1 = (bf16[128,512]{1,0:T(8,128)(2,1)S(1)}, bf16[128,512]{1,0:T(8,128)(2,1)S(1)}, f32[128,512]{1,0:T(8,128)S(1)}, f32[128,512]{1,0:T(8,128)S(1)}, bf...) custom-call(s32[1]{0:T(128)} %bitcast.me, bf16[128,1024]{1,0:T(8,128)(2,1)S(1)} %copy-done.21, ...), custom_call_target="tpu_custom_call" | custom-call | tf_op jit(solution)/shard_map/encode_both/pallas_call | solution.py:204
  14.1 0.7 copy-done.18
  14.8 0.7 copy-done.20
  16.1 3.0 %collective-permute-start.8 = (bf16[128,512]{1,0:T(8,128)(2,1)S(1)}, bf16[128,512]{1,0:T(8,128)(2,1)S(1)}, u32[]{:S(2)}, u32[]{:S(2)}) collective-permute-start(bf16[128,512]{1,0:T(8,128)(2,1)S(1)} %get-tuple-element.29), channel_id=1, source_target_pairs={{0,1},{1,0},{2,3},{3,2},{4,5},{5,4},{6,7},{7,6},{8,9},{9,8},{10,11... | collective-permute-start | bytes 393224 | tf_op jit(solution)/shard_map/ppermute | solution.py:134
  19.1 4.3 %collective-permute-done.8.other = bf16[128,512]{1,0:T(8,128)(2,1)S(1)} collective-permute-done((bf16[128,512]{1,0:T(8,128)(2,1)S(1)}, bf16[128,512]{1,0:T(8,128)(2,1)S(1)}, u32[]{:S(2)}, u32[]{:S(2)}) %collective-permute-start.8) | collective-permute-done | bytes 131104 | tf_op jit(solution)/shard_map/ppermute | solution.py:134
  24.0 1.7 %pack.3.refs_8_.raw = bf16[144,512]{1,0:T(8,128)(2,1)} custom-call(f32[128,512]{1,0:T(8,128)} %copy-done.20, bf16[128,512]{1,0:T(8,128)(2,1)} %copy-done.52, bf16[16,128]{1,0:T(8,128)(2,1)} %copy-done.46), custom_call_target="tpu_custom_call" | custom-call | tf_op jit(solution)/shard_map/pack/pallas_call | solution.py:249
  25.7 3.1 %collective-permute-start.12 = (bf16[144,512]{1,0:T(8,128)(2,1)}, bf16[144,512]{1,0:T(8,128)(2,1)S(1)}, u32[]{:S(2)}, u32[]{:S(2)}) collective-permute-start(bf16[144,512]{1,0:T(8,128)(2,1)} %pack.3.refs_8_.raw), channel_id=1, source_target_pairs={{0,16},{2,18},{4,20},{6,22},{8,24},{10,26},{12,28},{14,30},{16,0},... | collective-permute-start | bytes 442376 | tf_op jit(solution)/shard_map/ppermute | solution.py:134
  29.5 1.7 %pack.2.refs_0_.raw = bf16[144,512]{1,0:T(8,128)(2,1)} custom-call(f32[128,512]{1,0:T(8,128)} %copy-done.18, bf16[128,512]{1,0:T(8,128)(2,1)} %copy-done.50, bf16[16,128]{1,0:T(8,128)(2,1)} %copy-done.45), custom_call_target="tpu_custom_call" | custom-call | tf_op jit(solution)/shard_map/pack/pallas_call | solution.py:249
  31.2 1.6 %collective-permute-start.4 = (bf16[144,512]{1,0:T(8,128)(2,1)}, bf16[144,512]{1,0:T(8,128)(2,1)S(1)}, u32[]{:S(2)}, u32[]{:S(2)}) collective-permute-start(bf16[144,512]{1,0:T(8,128)(2,1)} %pack.2.refs_0_.raw), channel_id=1, source_target_pairs={{0,8},{2,10},{4,12},{6,14},{8,0},{10,2},{12,4},{14,6},{16,24},{18,... | collective-permute-start | bytes 442376 | tf_op jit(solution)/shard_map/ppermute | solution.py:134
  32.8 1.5 %collective-permute-start.10 = (bf16[144,512]{1,0:T(8,128)(2,1)}, bf16[144,512]{1,0:T(8,128)(2,1)S(1)}, u32[]{:S(2)}, u32[]{:S(2)}) collective-permute-start(bf16[144,512]{1,0:T(8,128)(2,1)} %pack.3.refs_8_.raw), channel_id=1, source_target_pairs={{0,4},{2,6},{4,0},{6,2},{8,12},{10,14},{12,8},{14,10},{16,20},{18,... | collective-permute-start | bytes 442376 | tf_op jit(solution)/shard_map/ppermute | solution.py:134
  35.4 1.2 %collective-permute-done.4.refs_4_ = bf16[144,512]{1,0:T(8,128)(2,1)S(1)} collective-permute-done((bf16[144,512]{1,0:T(8,128)(2,1)}, bf16[144,512]{1,0:T(8,128)(2,1)S(1)}, u32[]{:S(2)}, u32[]{:S(2)}) %collective-permute-start.4) | collective-permute-done | bytes 147488 | tf_op jit(solution)/shard_map/ppermute | solution.py:134
  36.6 1.5 %collective-permute-start.14 = (bf16[144,512]{1,0:T(8,128)(2,1)S(1)}, bf16[144,512]{1,0:T(8,128)(2,1)S(1)}, u32[]{:S(2)}, u32[]{:S(2)}) collective-permute-start(bf16[144,512]{1,0:T(8,128)(2,1)S(1)} %collective-permute-done.12.refs_12_), channel_id=1, source_target_pairs={{0,4},{2,6},{4,0},{6,2},{8,12},{10,14},{12,8},{14,10},{16,20},{18,... | collective-permute-start | bytes 442376 | tf_op jit(solution)/shard_map/ppermute | solution.py:134
  38.2 1.5 %collective-permute-start.6 = (bf16[144,512]{1,0:T(8,128)(2,1)S(1)}, bf16[144,512]{1,0:T(8,128)(2,1)S(1)}, u32[]{:S(2)}, u32[]{:S(2)}) collective-permute-start(bf16[144,512]{1,0:T(8,128)(2,1)S(1)} %collective-permute-done.4.refs_4_), channel_id=1, source_target_pairs={{0,4},{2,6},{4,0},{6,2},{8,12},{10,14},{12,8},{14,10},{16,20},{18,... | collective-permute-start | bytes 442376 | tf_op jit(solution)/shard_map/ppermute | solution.py:134
  39.7 1.7 %collective-permute-done.2.refs_2_ = bf16[144,512]{1,0:T(8,128)(2,1)S(1)} collective-permute-done((bf16[144,512]{1,0:T(8,128)(2,1)}, bf16[144,512]{1,0:T(8,128)(2,1)S(1)}, u32[]{:S(2)}, u32[]{:S(2)}) %collective-permute-start.2) | collective-permute-done | bytes 147488 | tf_op jit(solution)/shard_map/ppermute | solution.py:134
  47.1 0.7 copy-done.39
  49.2 0.9 copy-done.4
  50.2 0.9 copy-done.6
  51.1 0.9 copy-done.24
  52.0 0.9 copy-done.26
  52.9 0.9 copy-done.28
  53.8 0.9 copy-done.30
  54.7 0.9 copy-done.32
  55.6 0.9 copy-done.34
  56.5 0.9 copy-done.36
  57.4 0.9 copy-done.38
  58.4 0.9 copy-done.40
  59.3 4.4 %score.1 = (f32[24,1024]{1,0:T(8,128)S(1)}, f32[8,1024]{1,0:T(8,128)S(1)}, bf16[256,1024]{1,0:T(8,128)(2,1)S(1)}, bf16[1024,256]{1,0:T(8,128)(2,1)S(1)}, bf16[10...) custom-call(s32[2,8]{1,0:T(2,128)S(1)} %pad_add_fusion.ids, bf16[144,512]{1,0:T(8,128)(2,1)S(1)} %copy-done.4, ...), custom_call_target="tpu_custom_call" | custom-call | tf_op jit(solution)/shard_map/score/pallas_call | solution.py:325
  63.7 0.8 copy-done.10
  64.5 0.8 copy-done.12
  65.9 1.5 %collective-permute-start.16 = (f32[24,1024]{1,0:T(8,128)S(1)}, f32[24,1024]{1,0:T(8,128)S(1)}, u32[]{:S(2)}, u32[]{:S(2)}) collective-permute-start(f32[24,1024]{1,0:T(8,128)S(1)} %get-tuple-element.31.table), channel_id=1, source_target_pairs={{0,1},{1,0},{2,3},{3,2},{4,5},{5,4},{6,7},{7,6},{8,9},{9,8},{10,11... | collective-permute-start | bytes 294920 | tf_op jit(solution)/shard_map/ppermute | solution.py:134
  67.4 3.5 %collective-permute-done.16.other = f32[24,1024]{1,0:T(8,128)S(1)} collective-permute-done((f32[24,1024]{1,0:T(8,128)S(1)}, f32[24,1024]{1,0:T(8,128)S(1)}, u32[]{:S(2)}, u32[]{:S(2)}) %collective-permute-start.16) | collective-permute-done | bytes 98336 | tf_op jit(solution)/shard_map/ppermute | solution.py:134
  71.5 1.6 %weigh.1 = (f32[24,1024]{1,0:T(8,128)}, f32[16,128]{1,0:T(8,128)}) custom-call(f32[24,1024]{1,0:T(8,128)} %copy-done.41, f32[24,1024]{1,0:T(8,128)} %copy-done.53, f32[8,1024]{1,0:T(8,128)} %copy-done.43), custom_call_target="tpu_custom_call" | custom-call | tf_op jit(solution)/shard_map/weigh/pallas_call | solution.py:372
  74.2 2.9 %collective-permute-done.17.other = f32[16,128]{1,0:T(8,128)S(1)} collective-permute-done((f32[16,128]{1,0:T(8,128)}, f32[16,128]{1,0:T(8,128)S(1)}, u32[]{:S(2)}, u32[]{:S(2)}) %collective-permute-start.17) | collective-permute-done | bytes 8224 | tf_op jit(solution)/shard_map/ppermute | solution.py:134
  77.0 1.0 copy-done.13
  78.1 0.9 copy-done.14
  79.0 0.7 copy-done.42
  80.1 0.7 copy-done.16
  80.8 1.0 copy-done.11
  82.4 0.7 copy-done.15
  83.1 1.2 %collective-permute-start.18 = (bf16[128,512]{1,0:T(8,128)(2,1)S(1)}, bf16[128,512]{1,0:T(8,128)(2,1)S(1)}, u32[]{:S(2)}, u32[]{:S(2)}) collective-permute-start(bf16[128,512]{1,0:T(8,128)(2,1)S(1)} %get-tuple-element.38), channel_id=1, source_target_pairs={{0,8},{2,10},{4,12},{6,14},{8,0},{10,2},{12,4},{14,6},{16,24},{18,... | collective-permute-start | bytes 393224 | tf_op jit(solution)/shard_map/ppermute | solution.py:134
  84.3 1.5 %collective-permute-start.24 = (bf16[144,512]{1,0:T(8,128)(2,1)S(1)}, bf16[144,512]{1,0:T(8,128)(2,1)S(1)}, u32[]{:S(2)}, u32[]{:S(2)}) collective-permute-start(bf16[144,512]{1,0:T(8,128)(2,1)S(1)} %copy-done.7), channel_id=1, source_target_pairs={{0,1},{1,0},{2,3},{3,2},{4,5},{5,4},{6,7},{7,6},{8,9},{9,8},{10,11... | collective-permute-start | bytes 442376 | tf_op jit(solution)/shard_map/ppermute | solution.py:134
  86.4 1.9 %collective-permute-done.22.other = bf16[128,512]{1,0:T(8,128)(2,1)S(1)} collective-permute-done((bf16[128,512]{1,0:T(8,128)(2,1)S(1)}, bf16[128,512]{1,0:T(8,128)(2,1)S(1)}, u32[]{:S(2)}, u32[]{:S(2)}) %collective-permute-start.22) | collective-permute-done | bytes 131104 | tf_op jit(solution)/shard_map/ppermute | solution.py:134
  88.9 1.7 %sum_pass.1.grad = bf16[128,512]{1,0:T(8,128)(2,1)} custom-call(f32[128,512]{1,0:T(8,128)} %copy-done.16, bf16[128,512]{1,0:T(8,128)(2,1)} %copy-done.47), custom_call_target="tpu_custom_call" | custom-call | tf_op jit(solution)/shard_map/sum_pass/pallas_call | solution.py:443
  90.5 1.5 %collective-permute-start.23 = (bf16[128,512]{1,0:T(8,128)(2,1)}, bf16[128,512]{1,0:T(8,128)(2,1)S(1)}, u32[]{:S(2)}, u32[]{:S(2)}) collective-permute-start(bf16[128,512]{1,0:T(8,128)(2,1)} %sum_pass.1.grad), channel_id=1, source_target_pairs={{0,1},{1,0},{2,3},{3,2},{4,5},{5,4},{6,7},{7,6},{8,9},{9,8},{10,11... | collective-permute-start | bytes 393224 | tf_op jit(solution)/shard_map/ppermute | solution.py:134
  92.7 1.7 %sum_query.1.grad = bf16[128,512]{1,0:T(8,128)(2,1)} custom-call(f32[128,512]{1,0:T(8,128)} %copy-done.15, bf16[128,512]{1,0:T(8,128)(2,1)} %copy-done.48), custom_call_target="tpu_custom_call" | custom-call | tf_op jit(solution)/shard_map/sum_query/pallas_call | solution.py:443
  94.9 1.4 %collective-permute-done.23.grad_other = bf16[128,512]{1,0:T(8,128)(2,1)S(1)} collective-permute-done((bf16[128,512]{1,0:T(8,128)(2,1)}, bf16[128,512]{1,0:T(8,128)(2,1)S(1)}, u32[]{:S(2)}, u32[]{:S(2)}) %collective-permute-start.23) | collective-permute-done | bytes 131104 | tf_op jit(solution)/shard_map/ppermute | solution.py:134
  96.2 2.2 %copy-done.1 = bf16[1024,2048]{1,0:T(8,128)(2,1)S(1)} copy-done((bf16[1024,2048]{1,0:T(8,128)(2,1)S(1)}, bf16[1024,2048]{1,0:T(8,128)(2,1)}, u32[]{:S(2)}) %copy-start.1) | copy-done | bytes 4194328
  98.4 2.2 %copy-done.3 = bf16[2048,1024]{1,0:T(8,128)(2,1)S(1)} copy-done((bf16[2048,1024]{1,0:T(8,128)(2,1)S(1)}, bf16[2048,1024]{1,0:T(8,128)(2,1)}, u32[]{:S(2)}) %copy-start.3) | copy-done | bytes 4194328
  100.6 0.9 copy-done.9
  101.5 4.2 %decode_one.3 = (bf16[128,512]{1,0:T(8,128)(2,1)S(1)}, f32[128,512]{1,0:T(8,128)S(1)}) custom-call(s32[1]{0:T(128)} %bitcast.me, bf16[128,512]{1,0:T(8,128)(2,1)S(1)} %copy-done.9, bf16[128,512]{1,0:T(8,128)(2,1)S(1)} %collective-permute-done.23.grad_other, bf16[144,512]{1,0:T(8,128)(2,1)S(1)} %copy-done.7, ...), custom_call_target="tpu_custom_call" | custom-call | tf_op jit(solution)/shard_map/decode_one/pallas_call | solution.py:498
  105.7 0.7 copy-done.17
  106.4 2.4 %collective-permute-start.25 = (bf16[128,512]{1,0:T(8,128)(2,1)S(1)}, bf16[128,512]{1,0:T(8,128)(2,1)S(1)}, u32[]{:S(2)}, u32[]{:S(2)}) collective-permute-start(bf16[128,512]{1,0:T(8,128)(2,1)S(1)} %get-tuple-element.47), channel_id=1, source_target_pairs={{0,1},{1,0},{2,3},{3,2},{4,5},{5,4},{6,7},{7,6},{8,9},{9,8},{10,11... | collective-permute-start | bytes 393224 | tf_op jit(solution)/shard_map/ppermute | solution.py:134
  108.8 4.2 %decode_one.2 = (bf16[128,512]{1,0:T(8,128)(2,1)S(1)}, f32[128,512]{1,0:T(8,128)S(1)}) custom-call(s32[1]{0:T(128)} %bitcast.me, bf16[128,512]{1,0:T(8,128)(2,1)S(1)} %copy-done.8, bf16[128,512]{1,0:T(8,128)(2,1)S(1)} %collective-permute-done.19.grad_other, bf16[144,512]{1,0:T(8,128)(2,1)S(1)} %copy-done.5, ...), custom_call_target="tpu_custom_call" | custom-call | tf_op jit(solution)/shard_map/decode_one/pallas_call | solution.py:498
  113.0 0.7 copy-done.19
  114.3 1.7 %out_pass.1 = bf16[128,512]{1,0:T(8,128)(2,1)} custom-call(f32[128,512]{1,0:T(8,128)} %copy-done.17, bf16[128,512]{1,0:T(8,128)(2,1)} %copy-done.49), custom_call_target="tpu_custom_call" | custom-call | tf_op jit(solution)/shard_map/out_pass/pallas_call | solution.py:443
  116.0 2.6 %collective-permute-done.21.other = bf16[128,512]{1,0:T(8,128)(2,1)S(1)} collective-permute-done((bf16[128,512]{1,0:T(8,128)(2,1)S(1)}, bf16[128,512]{1,0:T(8,128)(2,1)S(1)}, u32[]{:S(2)}, u32[]{:S(2)}) %collective-permute-start.21) | collective-permute-done | bytes 131104 | tf_op jit(solution)/shard_map/ppermute | solution.py:134
  119.3 1.7 %out_query.1 = bf16[128,512]{1,0:T(8,128)(2,1)} custom-call(f32[128,512]{1,0:T(8,128)} %copy-done.19, bf16[128,512]{1,0:T(8,128)(2,1)} %copy-done.51), custom_call_target="tpu_custom_call" | custom-call | tf_op jit(solution)/shard_map/out_query/pallas_call | solution.py:443
  (115 shorter events, 16.6 us)
Async XLA Ops:
  2.2 2.2 %copy-start = (bf16[1024,2048]{1,0:T(8,128)(2,1)S(1)}, bf16[1024,2048]{1,0:T(8,128)(2,1)}, u32[]{:S(2)}) copy-start(bf16[1024,2048]{1,0:T(8,128)(2,1)} %w_in.5) | copy-start | bytes 12582916
  4.4 2.2 %copy-start.2 = (bf16[2048,1024]{1,0:T(8,128)(2,1)S(1)}, bf16[2048,1024]{1,0:T(8,128)(2,1)}, u32[]{:S(2)}) copy-start(bf16[2048,1024]{1,0:T(8,128)(2,1)} %w_out.5) | copy-start | bytes 12582916
  6.6 0.9 copy-start.21
  7.5 0.9 copy-start.22
  8.5 0.7 copy-start.44
  9.2 39.7 %copy-start.54 = (s32[8]{0:T(128)S(1)}, s32[8]{0:T(128)}, u32[]{:S(2)}) copy-start(s32[8]{0:T(128)} %constant.12.clone) | copy-start | bytes 100
  14.1 0.7 copy-start.18
  14.8 0.7 copy-start.20
  16.1 7.3 %copy-start.45 = (bf16[16,128]{1,0:T(8,128)(2,1)}, bf16[16,128]{1,0:T(8,128)(2,1)S(1)}, u32[]{:S(2)}) copy-start(bf16[16,128]{1,0:T(8,128)(2,1)S(1)} %get-tuple-element.27.numbers) | copy-start | bytes 12292
  16.1 7.3 %collective-permute-start.8 = (bf16[128,512]{1,0:T(8,128)(2,1)S(1)}, bf16[128,512]{1,0:T(8,128)(2,1)S(1)}, u32[]{:S(2)}, u32[]{:S(2)}) collective-permute-start(bf16[128,512]{1,0:T(8,128)(2,1)S(1)} %get-tuple-element.29), channel_id=1, source_target_pairs={{0,1},{1,0},{2,3},{3,2},{4,5},{5,4},{6,7},{7,6},{8,9},{9,8},{10,11... | collective-permute-start | bytes 393224 | tf_op jit(solution)/shard_map/ppermute | solution.py:134
  19.1 9.8 %collective-permute-start = (bf16[128,512]{1,0:T(8,128)(2,1)S(1)}, bf16[128,512]{1,0:T(8,128)(2,1)S(1)}, u32[]{:S(2)}, u32[]{:S(2)}) collective-permute-start(bf16[128,512]{1,0:T(8,128)(2,1)S(1)} %get-tuple-element.26), channel_id=1, source_target_pairs={{0,1},{1,0},{2,3},{3,2},{4,5},{5,4},{6,7},{7,6},{8,9},{9,8},{10,11... | collective-permute-start | bytes 393224 | tf_op jit(solution)/shard_map/ppermute | solution.py:134
  25.7 58.6 %copy-start.7 = (bf16[144,512]{1,0:T(8,128)(2,1)S(1)}, bf16[144,512]{1,0:T(8,128)(2,1)}, u32[]{:S(2)}) copy-start(bf16[144,512]{1,0:T(8,128)(2,1)} %pack.3.refs_8_.raw) | copy-start | bytes 442372
  25.7 9.1 %collective-permute-start.12 = (bf16[144,512]{1,0:T(8,128)(2,1)}, bf16[144,512]{1,0:T(8,128)(2,1)S(1)}, u32[]{:S(2)}, u32[]{:S(2)}) collective-permute-start(bf16[144,512]{1,0:T(8,128)(2,1)} %pack.3.refs_8_.raw), channel_id=1, source_target_pairs={{0,16},{2,18},{4,20},{6,22},{8,24},{10,26},{12,28},{14,30},{16,0},... | collective-permute-start | bytes 442376 | tf_op jit(solution)/shard_map/ppermute | solution.py:134
  31.2 5.4 %collective-permute-start.4 = (bf16[144,512]{1,0:T(8,128)(2,1)}, bf16[144,512]{1,0:T(8,128)(2,1)S(1)}, u32[]{:S(2)}, u32[]{:S(2)}) collective-permute-start(bf16[144,512]{1,0:T(8,128)(2,1)} %pack.2.refs_0_.raw), channel_id=1, source_target_pairs={{0,8},{2,10},{4,12},{6,14},{8,0},{10,2},{12,4},{14,6},{16,24},{18,... | collective-permute-start | bytes 442376 | tf_op jit(solution)/shard_map/ppermute | solution.py:134
  32.8 5.4 %collective-permute-start.10 = (bf16[144,512]{1,0:T(8,128)(2,1)}, bf16[144,512]{1,0:T(8,128)(2,1)S(1)}, u32[]{:S(2)}, u32[]{:S(2)}) collective-permute-start(bf16[144,512]{1,0:T(8,128)(2,1)} %pack.3.refs_8_.raw), channel_id=1, source_target_pairs={{0,4},{2,6},{4,0},{6,2},{8,12},{10,14},{12,8},{14,10},{16,20},{18,... | collective-permute-start | bytes 442376 | tf_op jit(solution)/shard_map/ppermute | solution.py:134
  34.3 7.1 %collective-permute-start.2 = (bf16[144,512]{1,0:T(8,128)(2,1)}, bf16[144,512]{1,0:T(8,128)(2,1)S(1)}, u32[]{:S(2)}, u32[]{:S(2)}) collective-permute-start(bf16[144,512]{1,0:T(8,128)(2,1)} %pack.2.refs_0_.raw), channel_id=1, source_target_pairs={{0,4},{2,6},{4,0},{6,2},{8,12},{10,14},{12,8},{14,10},{16,20},{18,... | collective-permute-start | bytes 442376 | tf_op jit(solution)/shard_map/ppermute | solution.py:134
  34.8 7.2 %collective-permute-start.9 = (bf16[144,512]{1,0:T(8,128)(2,1)}, bf16[144,512]{1,0:T(8,128)(2,1)S(1)}, u32[]{:S(2)}, u32[]{:S(2)}) collective-permute-start(bf16[144,512]{1,0:T(8,128)(2,1)} %pack.3.refs_8_.raw), channel_id=1, source_target_pairs={{0,2},{2,0},{4,6},{6,4},{8,10},{10,8},{12,14},{14,12},{16,18},{18,... | collective-permute-start | bytes 442376 | tf_op jit(solution)/shard_map/ppermute | solution.py:134
  34.8 9.1 %collective-permute-start.1 = (bf16[144,512]{1,0:T(8,128)(2,1)}, bf16[144,512]{1,0:T(8,128)(2,1)S(1)}, u32[]{:S(2)}, u32[]{:S(2)}) collective-permute-start(bf16[144,512]{1,0:T(8,128)(2,1)} %pack.2.refs_0_.raw), channel_id=1, source_target_pairs={{0,2},{2,0},{4,6},{6,4},{8,10},{10,8},{12,14},{14,12},{16,18},{18,... | collective-permute-start | bytes 442376 | tf_op jit(solution)/shard_map/ppermute | solution.py:134
  36.6 8.6 %collective-permute-start.14 = (bf16[144,512]{1,0:T(8,128)(2,1)S(1)}, bf16[144,512]{1,0:T(8,128)(2,1)S(1)}, u32[]{:S(2)}, u32[]{:S(2)}) collective-permute-start(bf16[144,512]{1,0:T(8,128)(2,1)S(1)} %collective-permute-done.12.refs_12_), channel_id=1, source_target_pairs={{0,4},{2,6},{4,0},{6,2},{8,12},{10,14},{12,8},{14,10},{16,20},{18,... | collective-permute-start | bytes 442376 | tf_op jit(solution)/shard_map/ppermute | solution.py:134
  38.2 8.1 %collective-permute-start.6 = (bf16[144,512]{1,0:T(8,128)(2,1)S(1)}, bf16[144,512]{1,0:T(8,128)(2,1)S(1)}, u32[]{:S(2)}, u32[]{:S(2)}) collective-permute-start(bf16[144,512]{1,0:T(8,128)(2,1)S(1)} %collective-permute-done.4.refs_4_), channel_id=1, source_target_pairs={{0,4},{2,6},{4,0},{6,2},{8,12},{10,14},{12,8},{14,10},{16,20},{18,... | collective-permute-start | bytes 442376 | tf_op jit(solution)/shard_map/ppermute | solution.py:134
  41.4 5.7 %collective-permute-start.13 = (bf16[144,512]{1,0:T(8,128)(2,1)S(1)}, bf16[144,512]{1,0:T(8,128)(2,1)S(1)}, u32[]{:S(2)}, u32[]{:S(2)}) collective-permute-start(bf16[144,512]{1,0:T(8,128)(2,1)S(1)} %collective-permute-done.12.refs_12_), channel_id=1, source_target_pairs={{0,2},{2,0},{4,6},{6,4},{8,10},{10,8},{12,14},{14,12},{16,18},{18,... | collective-permute-start | bytes 442376 | tf_op jit(solution)/shard_map/ppermute | solution.py:134
  42.7 6.2 %collective-permute-start.5 = (bf16[144,512]{1,0:T(8,128)(2,1)S(1)}, bf16[144,512]{1,0:T(8,128)(2,1)S(1)}, u32[]{:S(2)}, u32[]{:S(2)}) collective-permute-start(bf16[144,512]{1,0:T(8,128)(2,1)S(1)} %collective-permute-done.4.refs_4_), channel_id=1, source_target_pairs={{0,2},{2,0},{4,6},{6,4},{8,10},{10,8},{12,14},{14,12},{16,18},{18,... | collective-permute-start | bytes 442376 | tf_op jit(solution)/shard_map/ppermute | solution.py:134
  44.6 4.4 %collective-permute-start.11 = (bf16[144,512]{1,0:T(8,128)(2,1)S(1)}, bf16[144,512]{1,0:T(8,128)(2,1)S(1)}, u32[]{:S(2)}, u32[]{:S(2)}) collective-permute-start(bf16[144,512]{1,0:T(8,128)(2,1)S(1)} %collective-permute-done.10.refs_10_), channel_id=1, source_target_pairs={{0,2},{2,0},{4,6},{6,4},{8,10},{10,8},{12,14},{14,12},{16,18},{18,... | collective-permute-start | bytes 442376 | tf_op jit(solution)/shard_map/ppermute | solution.py:134
  45.2 3.7 %collective-permute-start.3 = (bf16[144,512]{1,0:T(8,128)(2,1)S(1)}, bf16[144,512]{1,0:T(8,128)(2,1)S(1)}, u32[]{:S(2)}, u32[]{:S(2)}) collective-permute-start(bf16[144,512]{1,0:T(8,128)(2,1)S(1)} %collective-permute-done.2.refs_2_), channel_id=1, source_target_pairs={{0,2},{2,0},{4,6},{6,4},{8,10},{10,8},{12,14},{14,12},{16,18},{18,... | collective-permute-start | bytes 442376 | tf_op jit(solution)/shard_map/ppermute | solution.py:134
  46.4 2.6 %collective-permute-start.15 = (bf16[144,512]{1,0:T(8,128)(2,1)S(1)}, bf16[144,512]{1,0:T(8,128)(2,1)S(1)}, u32[]{:S(2)}, u32[]{:S(2)}) collective-permute-start(bf16[144,512]{1,0:T(8,128)(2,1)S(1)} %collective-permute-done.14.refs_14_), channel_id=1, source_target_pairs={{0,2},{2,0},{4,6},{6,4},{8,10},{10,8},{12,14},{14,12},{16,18},{18,... | collective-permute-start | bytes 442376 | tf_op jit(solution)/shard_map/ppermute | solution.py:134
  47.1 0.7 copy-start.39
  47.7 1.5 %collective-permute-start.7 = (bf16[144,512]{1,0:T(8,128)(2,1)S(1)}, bf16[144,512]{1,0:T(8,128)(2,1)S(1)}, u32[]{:S(2)}, u32[]{:S(2)}) collective-permute-start(bf16[144,512]{1,0:T(8,128)(2,1)S(1)} %collective-permute-done.6.refs_6_), channel_id=1, source_target_pairs={{0,2},{2,0},{4,6},{6,4},{8,10},{10,8},{12,14},{14,12},{16,18},{18,... | collective-permute-start | bytes 442376 | tf_op jit(solution)/shard_map/ppermute | solution.py:134
  49.2 0.9 copy-start.4
  50.2 0.9 copy-start.6
  51.1 0.9 copy-start.24
  52.0 0.9 copy-start.26
  52.9 0.9 copy-start.28
  53.8 0.9 copy-start.30
  54.7 0.9 copy-start.32
  55.6 0.9 copy-start.34
  56.5 0.9 copy-start.36
  57.4 0.9 copy-start.38
  58.4 0.9 copy-start.40
  59.3 26.6 %copy-start.5 = (bf16[144,512]{1,0:T(8,128)(2,1)S(1)}, bf16[144,512]{1,0:T(8,128)(2,1)}, u32[]{:S(2)}) copy-start(bf16[144,512]{1,0:T(8,128)(2,1)} %pack.2.refs_0_.raw) | copy-start | bytes 442372
  63.7 0.8 copy-start.10
  64.4 0.8 copy-start.12
  65.8 5.7 %copy-start.41 = (f32[24,1024]{1,0:T(8,128)}, f32[24,1024]{1,0:T(8,128)S(1)}, u32[]{:S(2)}) copy-start(f32[24,1024]{1,0:T(8,128)S(1)} %get-tuple-element.31.table) | copy-start | bytes 294916
  65.9 5.0 %collective-permute-start.16 = (f32[24,1024]{1,0:T(8,128)S(1)}, f32[24,1024]{1,0:T(8,128)S(1)}, u32[]{:S(2)}, u32[]{:S(2)}) collective-permute-start(f32[24,1024]{1,0:T(8,128)S(1)} %get-tuple-element.31.table), channel_id=1, source_target_pairs={{0,1},{1,0},{2,3},{3,2},{4,5},{5,4},{6,7},{7,6},{8,9},{9,8},{10,11... | collective-permute-start | bytes 294920 | tf_op jit(solution)/shard_map/ppermute | solution.py:134
  73.2 3.9 %collective-permute-start.17 = (f32[16,128]{1,0:T(8,128)}, f32[16,128]{1,0:T(8,128)S(1)}, u32[]{:S(2)}, u32[]{:S(2)}) collective-permute-start(f32[16,128]{1,0:T(8,128)} %get-tuple-element.34.sums), channel_id=1, source_target_pairs={{0,8},{2,10},{4,12},{6,14},{8,0},{10,2},{12,4},{14,6},{16,24},{18,... | collective-permute-start | bytes 24584 | tf_op jit(solution)/shard_map/ppermute | solution.py:134
  77.0 1.0 copy-start.13
  78.1 0.9 copy-start.14
  79.0 0.7 copy-start.42
  80.1 0.7 copy-start.16
  80.8 7.4 %collective-permute-start.22 = (bf16[128,512]{1,0:T(8,128)(2,1)S(1)}, bf16[128,512]{1,0:T(8,128)(2,1)S(1)}, u32[]{:S(2)}, u32[]{:S(2)}) collective-permute-start(bf16[128,512]{1,0:T(8,128)(2,1)S(1)} %get-tuple-element.45), channel_id=1, source_target_pairs={{0,16},{2,18},{4,20},{6,22},{8,24},{10,26},{12,28},{14,30},{16,0},... | collective-permute-start | bytes 393224 | tf_op jit(solution)/shard_map/ppermute | solution.py:134
  80.8 1.0 copy-start.11
  82.4 0.7 copy-start.15
  83.1 9.0 %collective-permute-start.18 = (bf16[128,512]{1,0:T(8,128)(2,1)S(1)}, bf16[128,512]{1,0:T(8,128)(2,1)S(1)}, u32[]{:S(2)}, u32[]{:S(2)}) collective-permute-start(bf16[128,512]{1,0:T(8,128)(2,1)S(1)} %get-tuple-element.38), channel_id=1, source_target_pairs={{0,8},{2,10},{4,12},{6,14},{8,0},{10,2},{12,4},{14,6},{16,24},{18,... | collective-permute-start | bytes 393224 | tf_op jit(solution)/shard_map/ppermute | solution.py:134
  84.3 10.5 %collective-permute-start.24 = (bf16[144,512]{1,0:T(8,128)(2,1)S(1)}, bf16[144,512]{1,0:T(8,128)(2,1)S(1)}, u32[]{:S(2)}, u32[]{:S(2)}) collective-permute-start(bf16[144,512]{1,0:T(8,128)(2,1)S(1)} %copy-done.7), channel_id=1, source_target_pairs={{0,1},{1,0},{2,3},{3,2},{4,5},{5,4},{6,7},{7,6},{8,9},{9,8},{10,11... | collective-permute-start | bytes 442376 | tf_op jit(solution)/shard_map/ppermute | solution.py:134
  85.9 22.9 %collective-permute-start.20 = (bf16[144,512]{1,0:T(8,128)(2,1)S(1)}, bf16[144,512]{1,0:T(8,128)(2,1)S(1)}, u32[]{:S(2)}, u32[]{:S(2)}) collective-permute-start(bf16[144,512]{1,0:T(8,128)(2,1)S(1)} %copy-done.5), channel_id=1, source_target_pairs={{0,1},{1,0},{2,3},{3,2},{4,5},{5,4},{6,7},{7,6},{8,9},{9,8},{10,11... | collective-permute-start | bytes 442376 | tf_op jit(solution)/shard_map/ppermute | solution.py:134
  90.5 5.7 %collective-permute-start.23 = (bf16[128,512]{1,0:T(8,128)(2,1)}, bf16[128,512]{1,0:T(8,128)(2,1)S(1)}, u32[]{:S(2)}, u32[]{:S(2)}) collective-permute-start(bf16[128,512]{1,0:T(8,128)(2,1)} %sum_pass.1.grad), channel_id=1, source_target_pairs={{0,1},{1,0},{2,3},{3,2},{4,5},{5,4},{6,7},{7,6},{8,9},{9,8},{10,11... | collective-permute-start | bytes 393224 | tf_op jit(solution)/shard_map/ppermute | solution.py:134
  94.4 14.4 %collective-permute-start.19 = (bf16[128,512]{1,0:T(8,128)(2,1)}, bf16[128,512]{1,0:T(8,128)(2,1)S(1)}, u32[]{:S(2)}, u32[]{:S(2)}) collective-permute-start(bf16[128,512]{1,0:T(8,128)(2,1)} %sum_query.1.grad), channel_id=1, source_target_pairs={{0,1},{1,0},{2,3},{3,2},{4,5},{5,4},{6,7},{7,6},{8,9},{9,8},{10,11... | collective-permute-start | bytes 393224 | tf_op jit(solution)/shard_map/ppermute | solution.py:134
  96.2 2.2 %copy-start.1 = (bf16[1024,2048]{1,0:T(8,128)(2,1)S(1)}, bf16[1024,2048]{1,0:T(8,128)(2,1)}, u32[]{:S(2)}) copy-start(bf16[1024,2048]{1,0:T(8,128)(2,1)} %w_in.5) | copy-start | bytes 12582916
  98.4 2.2 %copy-start.3 = (bf16[2048,1024]{1,0:T(8,128)(2,1)S(1)}, bf16[2048,1024]{1,0:T(8,128)(2,1)}, u32[]{:S(2)}) copy-start(bf16[2048,1024]{1,0:T(8,128)(2,1)} %w_out.5) | copy-start | bytes 12582916
  100.6 0.9 copy-start.9
  101.5 7.2 %copy-start.8 = (bf16[128,512]{1,0:T(8,128)(2,1)S(1)}, bf16[128,512]{1,0:T(8,128)(2,1)}, u32[]{:S(2)}) copy-start(bf16[128,512]{1,0:T(8,128)(2,1)} %sum_query.1.grad) | copy-start | bytes 393220
  105.7 0.7 copy-start.17
  106.4 7.3 %collective-permute-start.25 = (bf16[128,512]{1,0:T(8,128)(2,1)S(1)}, bf16[128,512]{1,0:T(8,128)(2,1)S(1)}, u32[]{:S(2)}, u32[]{:S(2)}) collective-permute-start(bf16[128,512]{1,0:T(8,128)(2,1)S(1)} %get-tuple-element.47), channel_id=1, source_target_pairs={{0,1},{1,0},{2,3},{3,2},{4,5},{5,4},{6,7},{7,6},{8,9},{9,8},{10,11... | collective-permute-start | bytes 393224 | tf_op jit(solution)/shard_map/ppermute | solution.py:134
  113.0 0.7 copy-start.19
  113.7 5.0 %collective-permute-start.21 = (bf16[128,512]{1,0:T(8,128)(2,1)S(1)}, bf16[128,512]{1,0:T(8,128)(2,1)S(1)}, u32[]{:S(2)}, u32[]{:S(2)}) collective-permute-start(bf16[128,512]{1,0:T(8,128)(2,1)S(1)} %get-tuple-element.41), channel_id=1, source_target_pairs={{0,1},{1,0},{2,3},{3,2},{4,5},{5,4},{6,7},{7,6},{8,9},{9,8},{10,11... | collective-permute-start | bytes 393224 | tf_op jit(solution)/shard_map/ppermute | solution.py:134
  (17 other events, 11.0 us)

commit v2 on v0

--- a/solution.py
+++ b/solution.py
@@ -1,12 +1,22 @@
+import functools
+
 import jax
 import jax.numpy as jnp
 from jax import lax
+from jax.experimental import pallas as pl
+from jax.experimental.pallas import tpu as pltpu
 from jax.sharding import PartitionSpec as P
 
 logit_scale = 50.0
 norm_eps = 1e-06
 root_half = 0.7071067811865476
 inv_root_two_pi = 0.3989422804014327
+f32, bf16 = jnp.float32, jnp.bfloat16
+nt = (((1,), (1,)), ((), ()))
+tn = (((0,), (0,)), ((), ()))
+vmem = pl.BlockSpec(memory_space=pltpu.VMEM)
+smem = pl.BlockSpec(memory_space=pltpu.SMEM)
+hbm = pl.BlockSpec(memory_space=pltpu.HBM)
 
 
 def gelu_value(values):
@@ -42,19 +52,20 @@
     grad_out = inv_norm * (
         grad_emb - unit_rows * jnp.sum(unit_rows * grad_emb, axis=1, keepdims=True)
     )
-    contract = (((1,), (1,)), ((), ()))
     grad_hidden = lax.dot_general(
-        grad_out.astype(jnp.bfloat16), w_out, contract, preferred_element_type=jnp.float32
+        grad_out.astype(jnp.bfloat16), w_out, nt, preferred_element_type=jnp.float32
     )
     grad_pre = (grad_hidden * gelu_slope(pre_act)).astype(jnp.bfloat16)
-    partial_in = lax.dot_general(grad_pre, w_in, contract, preferred_element_type=jnp.float32)
+    partial_in = lax.dot_general(grad_pre, w_in, nt, preferred_element_type=jnp.float32)
     summed = lax.psum_scatter(
         partial_in.astype(jnp.bfloat16), "mp", scatter_dimension=1, tiled=True
     ).astype(jnp.float32)
     return (summed + own_columns(grad_out)).astype(jnp.bfloat16)
 
 
-def shards(query_states, passage_states, w_in, w_out, neg_owner, neg_mask, served_rows, loss_scale):
+def general_shards(
+    query_states, passage_states, w_in, w_out, neg_owner, neg_mask, served_rows, loss_scale
+):
     owners = lax.axis_size("dp")
     row_count = query_states.shape[0]
     negatives = neg_owner.shape[1]
@@ -116,6 +127,450 @@
     return (grad_query_states, grad_passage_states)
 
 
+query_bits, pass_bits = (4, 2), (8, 1)
+
+
+def offsets(bits):
+    found = [0]
+    for bit in bits:
+        found = found + [at | bit for at in found]
+    return found
+
+
+query_at, pass_at = offsets(query_bits), offsets(pass_bits)
+
+
+def swap(values, axis, bit):
+    size = lax.axis_size(axis)
+    return lax.ppermute(values, axis, [(i, i ^ bit) for i in range(size)])
+
+
+def gather_blocks(block, bits):
+    blocks = [block]
+    for bit in bits:
+        blocks = blocks + [swap(values, "dp", bit) for values in blocks]
+    return blocks
+
+
+def halves(first, values):
+    width = values.shape[1] // 2
+    left, right = values[:, :width], values[:, width:]
+    return jnp.where(first, left, right), jnp.where(first, right, left)
+
+
+def eye_of(size):
+    return (
+        lax.broadcasted_iota(jnp.int32, (size, size), 0)
+        == lax.broadcasted_iota(jnp.int32, (size, size), 1)
+    ).astype(f32)
+
+
+def local(kernel, name, outs, operands, mebibytes=1, scratch=(), scalars=()):
+    return pl.pallas_call(
+        kernel,
+        in_specs=[smem] * len(scalars) + [vmem] * len(operands),
+        out_specs=[vmem] * len(outs),
+        out_shape=[pltpu.VMEM(shape, dtype) for shape, dtype in outs],
+        scratch_shapes=list(scratch),
+        compiler_params=pltpu.CompilerParams(vmem_limit_bytes=mebibytes << 20),
+        name=name,
+    )(*scalars, *[pltpu.with_memory_space_constraint(x, pltpu.VMEM) for x in operands])
+
+
+def encode_kernel(
+    tile, me, scale, xq, xp, w_in, w_out, owner, mask, served,
+    send_q, send_p, own_q, own_p, slope, slots_out, served_out, scale_out, w_in_kept, w_out_kept,
+    states, total, owner_held, mask_held, served_held, sems,
+):
+    rows = xq.shape[0]
+    tiles = w_in.shape[1] // tile
+    copies = [
+        pltpu.make_async_copy(xq, states.at[:rows, :], sems.at[0]),
+        pltpu.make_async_copy(xp, states.at[rows:, :], sems.at[1]),
+        pltpu.make_async_copy(owner, owner_held, sems.at[2]),
+        pltpu.make_async_copy(mask, mask_held, sems.at[3]),
+        pltpu.make_async_copy(served, served_held, sems.at[4]),
+    ]
+    for t in range(tiles):
+        at = slice(t * tile, (t + 1) * tile)
+        copies.append(pltpu.make_async_copy(w_in.at[:, at], w_in_kept.at[:, at], sems.at[5 + 2 * t]))
+        copies.append(pltpu.make_async_copy(w_out.at[at, :], w_out_kept.at[at, :], sems.at[6 + 2 * t]))
+    for copy in copies:
+        copy.start()
+    for copy in copies[2:5]:
+        copy.wait()
+    owners = slots_out.shape[0]
+    down = lax.broadcasted_iota(jnp.int32, (owners, rows), 0)
+    named = jnp.zeros((owners, rows), f32)
+    live = jnp.zeros((owners, rows), f32)
+    for j in range(owner.shape[0]):
+        hit = (owner_held[j : j + 1, :] == down).astype(f32)
+        named = named + hit
+        live = live + hit * mask_held[j : j + 1, :].astype(f32)
+    earlier = lax.broadcasted_iota(jnp.int32, (rows, rows), 0) < lax.broadcasted_iota(
+        jnp.int32, (rows, rows), 1
+    )
+    slot = jnp.dot(named.astype(bf16), earlier.astype(f32).astype(bf16), preferred_element_type=f32)
+    slots_out[...] = jnp.where(live > 0.5, slot, -1.0).astype(bf16)
+    served_out[...] = served_held[0].astype(f32).astype(bf16)
+    scale_out[...] = jnp.zeros_like(scale_out) + scale[0] * logit_scale
+    copies[0].wait()
+    copies[1].wait()
+    for t in range(tiles):
+        at = slice(t * tile, (t + 1) * tile)
+        copies[5 + 2 * t].wait()
+        pre = jnp.dot(states[...], w_in_kept[:, at], preferred_element_type=f32)
+        cdf = 0.5 * (1.0 + lax.erf(pre * root_half))
+        slope[:, at] = (cdf + pre * jnp.exp(-0.5 * pre * pre) * inv_root_two_pi).astype(bf16)
+        hidden = (pre * cdf).astype(bf16)
+        copies[6 + 2 * t].wait()
+        part = jnp.dot(hidden, w_out_kept[at, :], preferred_element_type=f32)
+        if t == 0:
+            total[...] = part
+        else:
+            total[...] += part
+    first = me[0] == 0
+    for at, send, own in ((0, send_q, own_q), (rows, send_p, own_p)):
+        mine, theirs = halves(first, total[at : at + rows, :])
+        send[...] = theirs.astype(bf16)
+        own[...] = mine + halves(first, states[at : at + rows, :].astype(f32))[0]
+
+
+def encode_both(me, scale, xq, xp, w_in, w_out, owner, mask, served):
+    rows, width = xq.shape
+    hidden = w_in.shape[1]
+    tile = min(512, hidden)
+    owners = served.shape[1]
+    half = (rows, width // 2)
+    operands = (xq, xp, w_in, w_out, owner.T, mask.T, served)
+    return pl.pallas_call(
+        functools.partial(encode_kernel, tile),
+        in_specs=[smem] * 2 + [hbm] * 7,
+        out_specs=[vmem] * 10,
+        out_shape=[
+            pltpu.VMEM(half, bf16),
+            pltpu.VMEM(half, bf16),
+            pltpu.VMEM(half, f32),
+            pltpu.VMEM(half, f32),
+            pltpu.VMEM((2 * rows, hidden), bf16),
+            pltpu.VMEM((owners, rows), bf16),
+            pltpu.VMEM((owners, served.shape[2]), bf16),
+            pltpu.VMEM((8, rows), f32),
+            pltpu.VMEM(w_in.shape, bf16),
+            pltpu.VMEM(w_out.shape, bf16),
+        ],
+        scratch_shapes=[
+            pltpu.VMEM((2 * rows, width), bf16),
+            pltpu.VMEM((2 * rows, width), f32),
+            pltpu.VMEM(owner.T.shape, jnp.int32),
+            pltpu.VMEM(mask.T.shape, jnp.int32),
+            pltpu.VMEM(served.shape, jnp.int32),
+            pltpu.SemaphoreType.DMA((5 + 2 * (hidden // tile),)),
+        ],
+        compiler_params=pltpu.CompilerParams(vmem_limit_bytes=8 << 20),
+        name="encode_both",
+    )(me, scale, *[pltpu.with_memory_space_constraint(x, pltpu.HBM) for x in operands])
+
+
+def pack_kernel(own, other, numbers, out):
+    rows = own.shape[0]
+    out[:rows, :] = (own[...] + other[...].astype(f32)).astype(bf16)
+    out[rows:, :] = jnp.zeros((out.shape[0] - rows, out.shape[1]), bf16)
+    out[rows:, : numbers.shape[1]] = numbers[...]
+
+
+def pack(own, other, numbers):
+    shape = (own.shape[0] + numbers.shape[0], own.shape[1])
+    return local(pack_kernel, "pack", [(shape, bf16)], (own, other, numbers))[0]
+
+
+def score_kernel(owners, rows, place, *refs):
+    nq, npass = len(query_at), len(pass_at)
+    q_refs, p_refs = refs[:nq], refs[nq : nq + npass]
+    table, valid, pick, q_all, p_all, slots, served = refs[nq + npass :]
+    for n, ref in enumerate(q_refs):
+        q_all[n * rows : (n + 1) * rows, :] = ref[:rows, :]
+        slots[n * owners : (n + 1) * owners, :] = ref[rows:, :rows].astype(f32)
+    for n, ref in enumerate(p_refs):
+        p_all[n * rows : (n + 1) * rows, :] = ref[:rows, :]
+        served[n * owners : (n + 1) * owners, :] = ref[rows:, :rows].astype(f32)
+    table[...] = jnp.zeros_like(table)
+    eye = eye_of(rows)
+    down = lax.broadcasted_iota(jnp.int32, (rows, rows), 0).astype(f32)
+    queries = q_all[...]
+    for b in range(nq):
+        block = q_all[b * rows : (b + 1) * rows, :].astype(f32)
+        square = jnp.sum(block * block, axis=1, keepdims=True)
+        table[2 * npass : 2 * npass + 1, b * rows : (b + 1) * rows] = jnp.sum(
+            eye * square, axis=0, keepdims=True
+        )
+    for a in range(npass):
+        part = p_all[a * rows : (a + 1) * rows, :]
+        block = part.astype(f32)
+        square = jnp.sum(block * block, axis=1, keepdims=True)
+        scores = lax.dot_general(part, queries, nt, preferred_element_type=f32)
+        if a == 0:
+            table[2 * npass + 1 : 2 * npass + 2, :rows] = jnp.sum(
+                eye * scores[:, :rows], axis=0, keepdims=True
+            )
+            table[2 * npass + 2 : 2 * npass + 3, :rows] = jnp.sum(
+                eye * square, axis=0, keepdims=True
+            )
+        for b in range(nq):
+            lanes = slice(b * rows, (b + 1) * rows)
+            row_of = served[pl.ds(a * owners + (place[0] ^ query_at[b]), 1), :]
+            slot_of = slots[pl.ds(b * owners + (place[0] ^ pass_at[a]), 1), :]
+            by_slot = (down == row_of).astype(f32).astype(bf16)
+            by_query = (down == slot_of).astype(f32).astype(bf16)
+            chosen = jnp.dot(by_slot, by_query, preferred_element_type=f32)
+            table[a : a + 1, lanes] = jnp.sum(chosen * scores[:, lanes], axis=0, keepdims=True)
+            table[npass + a : npass + a + 1, lanes] = jnp.sum(
+                chosen * square, axis=0, keepdims=True
+            )
+            valid[a : a + 1, lanes] = (slot_of >= 0.0).astype(f32)
+            pick[a * rows : (a + 1) * rows, lanes] = chosen.astype(bf16)
+
+
+def score(place, q_blocks, p_blocks, rows, owners):
+    nq, npass = len(query_at), len(pass_at)
+    width = q_blocks[0].shape[1]
+    return local(
+        functools.partial(score_kernel, owners, rows),
+        "score",
+        [
+            ((-(-(2 * npass + 3) // 8) * 8, nq * rows), f32),
+            ((npass, nq * rows), f32),
+            ((npass * rows, nq * rows), bf16),
+            ((nq * rows, width), bf16),
+            ((npass * rows, width), bf16),
+        ],
+        (*q_blocks, *p_blocks),
+        3,
+        [pltpu.VMEM((nq * owners, rows), f32), pltpu.VMEM((npass * owners, rows), f32)],
+        [place],
+    )
+
+
+def weigh_kernel(rows, table, other, valid, coefs, sums):
+    nq, npass = len(query_at), len(pass_at)
+    full = table[...] + other[...]
+    raw, square = full[:npass], full[npass : 2 * npass]
+    inv_q = lax.rsqrt(full[2 * npass : 2 * npass + 1] + norm_eps)
+    inv_pos = lax.rsqrt(full[2 * npass + 2 : 2 * npass + 3] + norm_eps)
+    inv_neg = lax.rsqrt(square + norm_eps)
+    exp_neg = valid[...] * jnp.exp(logit_scale * (raw * inv_q * inv_neg))
+    pos_score = full[2 * npass + 1 : 2 * npass + 2] * inv_q * inv_pos
+    coefs[...] = jnp.zeros_like(coefs)
+    coefs[:npass] = exp_neg
+    coefs[npass : 2 * npass] = exp_neg * inv_neg
+    coefs[2 * npass : 2 * npass + 1] = inv_q
+    coefs[2 * npass + 1 : 2 * npass + 2] = inv_pos
+    neg_sum = jnp.sum(exp_neg, axis=0, keepdims=True)
+    sums[...] = jnp.zeros_like(sums)
+    for n in range(nq):
+        sums[n : n + 1, :] = neg_sum[:, n * rows : (n + 1) * rows]
+    sums[nq : nq + 1, :] = jnp.exp(logit_scale * pos_score[:, :rows])
+
+
+def weigh(table, other, valid, rows):
+    return local(
+        functools.partial(weigh_kernel, rows),
+        "weigh",
+        [(table.shape, f32), ((2 * len(query_at), rows), f32)],
+        (table, other, valid),
+    )
+
+
+def add_sums_kernel(bit, sums, other, out):
+    nq = len(query_at)
+    for n, at in enumerate(query_at):
+        m = query_at.index(at ^ bit)
+        for k, l in ((n, m), (nq + n, nq + m)):
+            out[k : k + 1, :] = sums[k : k + 1, :] + other[l : l + 1, :]
+
+
+def spread_query_kernel(rows, coefs, pick, p_all, kept, sent):
+    npass = len(pass_at)
+    passages = p_all[...]
+    for b in range(len(query_at)):
+        lanes = slice(b * rows, (b + 1) * rows)
+        pieces = []
+        for a in range(npass):
+            piece = pick[a * rows : (a + 1) * rows, lanes].astype(f32)
+            piece = piece * coefs[npass + a : npass + a + 1, lanes]
+            pieces.append(piece.T.astype(bf16))
+        weights = jnp.concatenate(pieces, axis=1)
+        out, at = (kept, b) if b < len(query_at) // 2 else (sent, b - len(query_at) // 2)
+        out[at * rows : (at + 1) * rows, :] = jnp.dot(
+            weights, passages, preferred_element_type=f32
+        ).astype(out.dtype)
+
+
+def spread_pass_kernel(rows, scale, coefs, sums, pick, q_all, kept, sent):
+    nq, npass = len(query_at), len(pass_at)
+    total = sums[:nq] + sums[nq:]
+    share = scale[:nq] / total
+    pos = -share[:1] * sums[:1] * coefs[2 * npass : 2 * npass + 1, :rows]
+    share = jnp.concatenate([share[n : n + 1] for n in range(nq)], axis=1)
+    scaled = share * coefs[2 * npass : 2 * npass + 1]
+    queries = q_all[...]
+    for a in range(npass):
+        weights = pick[a * rows : (a + 1) * rows, :].astype(f32) * (coefs[a : a + 1] * scaled)
+        if a == 0:
+            weights = jnp.concatenate(
+                [weights[:, :rows] + eye_of(rows) * pos, weights[:, rows:]], axis=1
+            )
+        out, at = (kept, a) if a < npass // 2 else (sent, a - npass // 2)
+        out[at * rows : (at + 1) * rows, :] = jnp.dot(
+            weights.astype(bf16), queries, preferred_element_type=f32
+        ).astype(out.dtype)
+
+
+def spread(kernel, name, operands, rows, width, count):
+    half = (count // 2 * rows, width)
+    return local(functools.partial(kernel, rows), name, [(half, f32), (half, bf16)], operands, 3)
+
+
+def fold_kernel(own, other, kept, sent):
+    rows = kept.shape[0]
+    total = own[...] + other[...].astype(f32)
+    kept[...] = total[:rows]
+    sent[...] = total[rows:].astype(bf16)
+
+
+def fold(own, other, name):
+    half = (own.shape[0] // 2, own.shape[1])
+    return local(fold_kernel, name, [(half, f32), (half, bf16)], (own, other))
+
+
+def add_kernel(own, other, out):
+    out[...] = (own[...] + other[...].astype(f32)).astype(out.dtype)
+
+
+def grad_query_kernel(own, other, scale, sums, coefs, raw_pass, out):
+    nq, npass = len(query_at), len(pass_at)
+    rows = own.shape[0]
+    eye = eye_of(rows)
+    share = scale[:1] / (sums[:1] + sums[nq : nq + 1])
+    pos = sums[:1] * coefs[2 * npass + 1 : 2 * npass + 2, :rows]
+    share = jnp.sum(eye * share, axis=1, keepdims=True)
+    pos = jnp.sum(eye * pos, axis=1, keepdims=True)
+    total = own[...] + other[...].astype(f32) - pos * raw_pass[:rows, :].astype(f32)
+    out[...] = (share * total).astype(bf16)
+
+
+def decode_kernel(
+    tower, tile, me, grad, grad_other, raw, raw_other, slope, w_in, w_out, send, own, total
+):
+    first = me[0] == 0
+    rows, width = grad.shape
+
+    def joined(mine, theirs):
+        mine, theirs = mine.astype(f32), theirs.astype(f32)
+        return jnp.concatenate(
+            [jnp.where(first, mine, theirs), jnp.where(first, theirs, mine)], axis=1
+        )
+
+    grads = joined(grad[...], grad_other[...])
+    values = joined(raw[:rows, :], raw_other[:rows, :])
+    inv_norm = lax.rsqrt(jnp.sum(values * values, axis=1, keepdims=True) + norm_eps)
+    unit = values * inv_norm
+    grad_out = inv_norm * (grads - unit * jnp.sum(unit * grads, axis=1, keepdims=True))
+    own[...] = halves(first, grad_out)[0]
+    rounded = grad_out.astype(bf16)
+    for t in range(w_in.shape[1] // tile):
+        at = slice(t * tile, (t + 1) * tile)
+        hidden = lax.dot_general(rounded, w_out[at, :], nt, preferred_element_type=f32)
+        grad_pre = (hidden * slope[tower * rows : (tower + 1) * rows, at].astype(f32)).astype(bf16)
+        part = lax.dot_general(grad_pre, w_in[:, at], nt, preferred_element_type=f32)
+        if t == 0:
+            total[...] = part
+        else:
+            total[...] += part
+    mine, theirs = halves(first, total[...])
+    send[...] = theirs.astype(bf16)
+    own[...] += mine
+
+
+def decode_one(me, grad, grad_other, raw, raw_other, slope, tower, w_in, w_out):
+    rows, width = grad.shape[0], w_in.shape[0]
+    return local(
+        functools.partial(decode_kernel, tower, min(512, w_in.shape[1])),
+        "decode_one",
+        [(grad.shape, bf16), (grad.shape, f32)],
+        (grad, grad_other, raw, raw_other, slope, w_in, w_out),
+        3,
+        [pltpu.VMEM((rows, width), f32)],
+        [me],
+    )
+
+
+def finish(own, other, name):
+    return pl.pallas_call(
+        add_kernel,
+        in_specs=[vmem] * 2,
+        out_specs=vmem,
+        out_shape=jax.ShapeDtypeStruct(own.shape, bf16),
+        compiler_params=pltpu.CompilerParams(vmem_limit_bytes=1 << 20),
+        name=name,
+    )(*[pltpu.with_memory_space_constraint(x, pltpu.VMEM) for x in (own, other)])
+
+
+def paired_shards(
+    query_states, passage_states, w_in, w_out, neg_owner, neg_mask, served_rows, loss_scale
+):
+    rows = query_states.shape[0]
+    owners = served_rows.shape[1]
+    me = lax.axis_index("mp").astype(jnp.int32).reshape(1)
+    place = lax.axis_index("dp").astype(jnp.int32).reshape(1)
+    send_q, send_p, own_q, own_p, slope, slots, served, scale, w_in, w_out = encode_both(
+        me, loss_scale.reshape(1), query_states, passage_states, w_in, w_out, neg_owner, neg_mask, served_rows
+    )
+    raw_q = pack(own_q, swap(send_q, "mp", 1), slots)
+    raw_p = pack(own_p, swap(send_p, "mp", 1), served)
+    width = raw_q.shape[1]
+    q_blocks = gather_blocks(raw_q, query_bits)
+    p_blocks = gather_blocks(raw_p, pass_bits)
+    raw_q_other, raw_p_other = swap(raw_q, "mp", 1), swap(raw_p, "mp", 1)
+
+    table, valid, pick, q_all, p_all = score(place, q_blocks, p_blocks, rows, owners)
+    coefs, sums = weigh(table, swap(table, "mp", 1), valid, rows)
+    nq, npass = len(query_at), len(pass_at)
+    kept_q, sent_q = spread(
+        spread_query_kernel, "spread_query", (coefs, pick, p_all), rows, width, nq
+    )
+    for bit in query_bits:
+        sums = local(
+            functools.partial(add_sums_kernel, bit),
+            "add_sums",
+            [(sums.shape, f32)],
+            (sums, swap(sums, "dp", bit)),
+        )[0]
+    kept_p, sent_p = spread(
+        spread_pass_kernel, "spread_pass", (scale, coefs, sums, pick, q_all), rows, width, npass
+    )
+    half = ((rows, width), bf16)
+    kept_p, sent_p = fold(kept_p, swap(sent_p, "dp", pass_bits[1]), "fold_pass")
+    grad_p = local(add_kernel, "grad_pass", [half], (kept_p, swap(sent_p, "dp", pass_bits[0])))[0]
+    kept_q, sent_q = fold(kept_q, swap(sent_q, "dp", query_bits[1]), "fold_query")
+    grad_q = local(
+        grad_query_kernel,
+        "grad_query",
+        [half],
+        (kept_q, swap(sent_q, "dp", query_bits[0]), scale, sums, coefs, raw_p),
+    )[0]
+    send_q, own_q = decode_one(
+        me, grad_q, swap(grad_q, "mp", 1), raw_q, raw_q_other, slope, 0, w_in, w_out
+    )
+    send_p, own_p = decode_one(
+        me, grad_p, swap(grad_p, "mp", 1), raw_p, raw_p_other, slope, 1, w_in, w_out
+    )
+    return (
+        finish(own_q, swap(send_q, "mp", 1), "out_query"),
+        finish(own_p, swap(send_p, "mp", 1), "out_pass"),
+    )
+
+
 def solution(mesh):
     in_specs = (
         P("dp", None),
@@ -128,4 +583,7 @@
         P(),
     )
     out_specs = (P("dp", "mp"), P("dp", "mp"))
+    gathered = len(query_at) * len(pass_at)
+    paired = mesh.shape["mp"] == 2 and mesh.shape["dp"] == gathered
+    shards = paired_shards if paired else general_shards
     return jax.shard_map(shards, mesh=mesh, in_specs=in_specs, out_specs=out_specs, check_vma=False)

time: 224 us -> 79.6 us (0.36)
  waiting for transfers between devices: 104 us -> 28 us
  other arithmetic: 37.5 us -> 0 us
  matrix products: 25.5 us -> 0 us
  starting transfers between devices: 9.51 us -> 28.1 us
  blocking collectives: 18.4 us -> 0 us
  Pallas kernels: 0 us -> 15.8 us
  between operations: 14.8 us -> 1.4 us
  local copies, waits for them, and re-layouts: 13.4 us -> 6.17 us
    psum x1 -> x0, waiting for transfers between devices: 43 us -> none  [encode(): mixed_sum = lax.psum(partial_out, 'mp')]
    ppermute x0 -> x21, starting transfers between devices: none -> 28.1 us  [swap(): return lax.ppermute(values, axis, [(i, i ^ bit) for i in range(size)])]
    ppermute x0 -> x21, waiting for transfers between devices: none -> 28 us  [swap(): return lax.ppermute(values, axis, [(i, i ^ bit) for i in range(size)])]
    dot_general x7 -> x0, matrix products: 25.5 us -> none  [the longest x2 15.1 us: decode(): lax.dot_general(grad_pre, w_in, contract, preferred_element_type=jnp.floa...]
    all_gather x1 -> x0, waiting for transfers between devices: 23 us -> none  [shards(): every_emb = lax.all_gather(emb_pass, 'dp', axis=0, tiled=True)]
    all_to_all x2 -> x0, waiting for transfers between devices: 22.1 us -> none  [the longest x1 22.1 us: shards(): lax.all_to_all(outgoing_grad.reshape(owners, capacity, column_width), 'dp...]
    reduce_scatter x2 -> x0, waiting for transfers between devices: 16.2 us -> none  [decode(): lax.psum_scatter(partial_in.astype(jnp.bfloat16), 'mp', scatter_dimension...]
    pallas_call x0 -> x17, Pallas kernels: none -> 15.8 us  [the longest x14 8.94 us: local(): pl.pallas_call(kernel, in_specs=[smem] * len(scalars) + [vmem] * len(oper...]
  transfers between devices with their start and end apart: 6 -> 21, of which waited for: 5 -> 12; matrix products, arithmetic and copies ran while one was open for 21% -> 0% of each run, Pallas kernels for 0% -> 11%
where the time goes in v2:
time: 79.6 us; the launch traced here: 79.4 us
  starting transfers between devices  28.1 us (35%)
  waiting for transfers between devices  28 us (35%)
  Pallas kernels  15.8 us (20%)
  local copies, waits for them, and re-layouts  6.17 us (8%)
  between operations  1.4 us (2%)
    ppermute x21, starting transfers between devices, swap(): return lax.ppermute(values, axis, [(i, i ^ bit) for i in range(size)])  28.1 us
    ppermute x21, waiting for transfers between devices, swap(): return lax.ppermute(values, axis, [(i, i ^ bit) for i in range(size)])  28 us
    pallas_call x14, Pallas kernels, local(): pl.pallas_call(kernel, in_specs=[smem] * len(scalars) + [vmem] * len(oper...  8.94 us
    unnamed x8, local copies, waits for them, and re-layouts  6.17 us
    pallas_call x1, Pallas kernels, encode_both(): pl.pallas_call(functools.partial(encode_kernel, tile), in_specs=[smem] *...  5.51 us
  transfers between devices with their start and end apart: 21, of which 12 were waited for; matrix products, arithmetic and copies ran while one was open for 0% of the time, Pallas kernels for 11%

profile of v2, /device:TPU:0, one launch (start us, length us, event | category | flops | bytes accessed | tf_op | source)
XLA Modules:
  0.0 79.4 jit_solution(11547548121174038407)
XLA Ops:
  1.3 5.5 %encode_both.1 = (bf16[128,512]{1,0:T(8,128)(2,1)S(1)}, bf16[128,512]{1,0:T(8,128)(2,1)S(1)}, f32[128,512]{1,0:T(8,128)S(1)}, f32[128,512]{1,0:T(8,128)S(1)}, bf...) custom-call(s32[1]{0:T(128)} %bitcast.me, ...), custom_call_target="tpu_custom_call" | custom-call | tf_op jit(solution)/shard_map/encode_both/pallas_call | solution.py:246
  6.8 0.0 copy-start
  6.8 1.9 %copy-done = bf16[1024,2048]{1,0:T(8,128)(2,1)} copy-done((bf16[1024,2048]{1,0:T(8,128)(2,1)}, bf16[1024,2048]{1,0:T(8,128)(2,1)S(1)}, u32[]{:S(2)}) %copy-start) | copy-done | bytes 4194328
  8.8 0.0 copy-start.2
  8.8 2.0 %copy-done.2 = bf16[2048,1024]{1,0:T(8,128)(2,1)} copy-done((bf16[2048,1024]{1,0:T(8,128)(2,1)}, bf16[2048,1024]{1,0:T(8,128)(2,1)S(1)}, u32[]{:S(2)}) %copy-start.2) | copy-done | bytes 4194328
  10.8 3.0 %collective-permute-start.4 = (bf16[128,512]{1,0:T(8,128)(2,1)S(1)}, bf16[128,512]{1,0:T(8,128)(2,1)S(1)}, u32[]{:S(2)}, u32[]{:S(2)}) collective-permute-start(bf16[128,512]{1,0:T(8,128)(2,1)S(1)} %get-tuple-element.35), channel_id=1, source_target_pairs={{0,1},{1,0},{2,3},{3,2},{4,5},{5,4},{6,7},{7,6},{8,9},{9,8},{10,11... | collective-permute-start | bytes 393224 | tf_op jit(solution)/shard_map/ppermute | solution.py:145
  13.8 0.0 collective-permute-start
  13.8 4.3 %collective-permute-done.4.other = bf16[128,512]{1,0:T(8,128)(2,1)S(1)} collective-permute-done((bf16[128,512]{1,0:T(8,128)(2,1)S(1)}, bf16[128,512]{1,0:T(8,128)(2,1)S(1)}, u32[]{:S(2)}, u32[]{:S(2)}) %collective-permute-start.4) | collective-permute-done | bytes 131104 | tf_op jit(solution)/shard_map/ppermute | solution.py:145
  18.1 3.2 %collective-permute-start.5 = (bf16[144,512]{1,0:T(8,128)(2,1)S(1)}, bf16[144,512]{1,0:T(8,128)(2,1)S(1)}, u32[]{:S(2)}, u32[]{:S(2)}) collective-permute-start(bf16[144,512]{1,0:T(8,128)(2,1)S(1)} %pack.3.refs_4_.raw_pass.raw), channel_id=1, source_target_pairs={{0,16},{2,18},{4,20},{6,22},{8,24},{10,26},{12,28},{14,30},{16,0},... | collective-permute-start | bytes 442376 | tf_op jit(solution)/shard_map/ppermute | solution.py:145
  21.3 0.0 collective-permute-done.other
  21.4 1.6 %collective-permute-start.1 = (bf16[144,512]{1,0:T(8,128)(2,1)S(1)}, bf16[144,512]{1,0:T(8,128)(2,1)S(1)}, u32[]{:S(2)}, u32[]{:S(2)}) collective-permute-start(bf16[144,512]{1,0:T(8,128)(2,1)S(1)} %pack.2.refs_0_.raw), channel_id=1, source_target_pairs={{0,8},{2,10},{4,12},{6,14},{8,0},{10,2},{12,4},{14,6},{16,24},{18,... | collective-permute-start | bytes 442376 | tf_op jit(solution)/shard_map/ppermute | solution.py:145
  23.0 0.0 collective-permute-start.6
  23.0 1.5 %collective-permute-start.2 = (bf16[144,512]{1,0:T(8,128)(2,1)S(1)}, bf16[144,512]{1,0:T(8,128)(2,1)S(1)}, u32[]{:S(2)}, u32[]{:S(2)}) collective-permute-start(bf16[144,512]{1,0:T(8,128)(2,1)S(1)} %pack.2.refs_0_.raw), channel_id=1, source_target_pairs={{0,4},{2,6},{4,0},{6,2},{8,12},{10,14},{12,8},{14,10},{16,20},{18,... | collective-permute-start | bytes 442376 | tf_op jit(solution)/shard_map/ppermute | solution.py:145
  24.5 1.1 %collective-permute-done.5.refs_5_ = bf16[144,512]{1,0:T(8,128)(2,1)S(1)} collective-permute-done((bf16[144,512]{1,0:T(8,128)(2,1)S(1)}, bf16[144,512]{1,0:T(8,128)(2,1)S(1)}, u32[]{:S(2)}, u32[]{:S(2)}) %collective-permute-start.5) | collective-permute-done | bytes 147488 | tf_op jit(solution)/shard_map/ppermute | solution.py:145
  25.6 0.0 collective-permute-start.7
  25.6 1.7 %collective-permute-done.1.refs_1_ = bf16[144,512]{1,0:T(8,128)(2,1)S(1)} collective-permute-done((bf16[144,512]{1,0:T(8,128)(2,1)S(1)}, bf16[144,512]{1,0:T(8,128)(2,1)S(1)}, u32[]{:S(2)}, u32[]{:S(2)}) %collective-permute-start.1) | collective-permute-done | bytes 147488 | tf_op jit(solution)/shard_map/ppermute | solution.py:145
  27.3 1.3 %collective-permute-start.3 = (bf16[144,512]{1,0:T(8,128)(2,1)S(1)}, bf16[144,512]{1,0:T(8,128)(2,1)S(1)}, u32[]{:S(2)}, u32[]{:S(2)}) collective-permute-start(bf16[144,512]{1,0:T(8,128)(2,1)S(1)} %collective-permute-done.1.refs_1_), channel_id=1, source_target_pairs={{0,4},{2,6},{4,0},{6,2},{8,12},{10,14},{12,8},{14,10},{16,20},{18,... | collective-permute-start | bytes 442376 | tf_op jit(solution)/shard_map/ppermute | solution.py:145
  28.6 0.0 copy-start.1
  28.6 0.0 collective-permute-done.6.refs_6_
  28.6 1.0 %collective-permute-done.2.refs_2_ = bf16[144,512]{1,0:T(8,128)(2,1)S(1)} collective-permute-done((bf16[144,512]{1,0:T(8,128)(2,1)S(1)}, bf16[144,512]{1,0:T(8,128)(2,1)S(1)}, u32[]{:S(2)}, u32[]{:S(2)}) %collective-permute-start.2) | collective-permute-done | bytes 147488 | tf_op jit(solution)/shard_map/ppermute | solution.py:145
  29.6 0.0 collective-permute-done.7.refs_7_
  29.6 2.8 %collective-permute-done.3.refs_3_ = bf16[144,512]{1,0:T(8,128)(2,1)S(1)} collective-permute-done((bf16[144,512]{1,0:T(8,128)(2,1)S(1)}, bf16[144,512]{1,0:T(8,128)(2,1)S(1)}, u32[]{:S(2)}, u32[]{:S(2)}) %collective-permute-start.3) | collective-permute-done | bytes 147488 | tf_op jit(solution)/shard_map/ppermute | solution.py:145
  32.5 1.1 %score.1 = (f32[16,512]{1,0:T(8,128)S(1)}, f32[4,512]{1,0:T(4,128)S(1)}, bf16[512,512]{1,0:T(8,128)(2,1)S(1)}, bf16[512,512]{1,0:T(8,128)(2,1)S(1)}, bf16[512,512]{1,0:T(8,128)(2,1)S(1)}) custom-call(s32[1]{0:T(128)} %bitcast.1.place, bf16[144,512]{1,0:T(8,128)(2,1)S(1)} %pack.2.refs_0_.raw, bf16[144,512]{1,0:T(8,128)(2,1)S(1)} %collective-permute-done.1.refs_1_, ...), custom_call_target="tpu_custom_call" | custom-call | tf_op jit(solution)/shard_map/score/pallas_call | solution.py:169
  33.6 1.5 %collective-permute-start.8 = (f32[16,512]{1,0:T(8,128)S(1)}, f32[16,512]{1,0:T(8,128)S(1)}, u32[]{:S(2)}, u32[]{:S(2)}) collective-permute-start(f32[16,512]{1,0:T(8,128)S(1)} %get-tuple-element.37.table), channel_id=1, source_target_pairs={{0,1},{1,0},{2,3},{3,2},{4,5},{5,4},{6,7},{7,6},{8,9},{9,8},{10,11... | collective-permute-start | bytes 98312 | tf_op jit(solution)/shard_map/ppermute | solution.py:145
  35.1 2.5 %collective-permute-done.8.other = f32[16,512]{1,0:T(8,128)S(1)} collective-permute-done((f32[16,512]{1,0:T(8,128)S(1)}, f32[16,512]{1,0:T(8,128)S(1)}, u32[]{:S(2)}, u32[]{:S(2)}) %collective-permute-start.8) | collective-permute-done | bytes 32800 | tf_op jit(solution)/shard_map/ppermute | solution.py:145
  37.6 1.5 %collective-permute-start.11 = (f32[8,128]{1,0:T(8,128)S(1)}, f32[8,128]{1,0:T(8,128)S(1)}, u32[]{:S(2)}, u32[]{:S(2)}) collective-permute-start(f32[8,128]{1,0:T(8,128)S(1)} %get-tuple-element.47.sums), channel_id=1, source_target_pairs={{0,8},{2,10},{4,12},{6,14},{8,0},{10,2},{12,4},{14,6},{16,24},{18,... | collective-permute-start | bytes 12296 | tf_op jit(solution)/shard_map/ppermute | solution.py:145
  39.2 2.1 %collective-permute-done.11.other = f32[8,128]{1,0:T(8,128)S(1)} collective-permute-done((f32[8,128]{1,0:T(8,128)S(1)}, f32[8,128]{1,0:T(8,128)S(1)}, u32[]{:S(2)}, u32[]{:S(2)}) %collective-permute-start.11) | collective-permute-done | bytes 4128 | tf_op jit(solution)/shard_map/ppermute | solution.py:145
  41.3 1.4 %collective-permute-start.12 = (f32[8,128]{1,0:T(8,128)S(1)}, f32[8,128]{1,0:T(8,128)S(1)}, u32[]{:S(2)}, u32[]{:S(2)}) collective-permute-start(f32[8,128]{1,0:T(8,128)S(1)} %add_sums.2.sums), channel_id=1, source_target_pairs={{0,4},{2,6},{4,0},{6,2},{8,12},{10,14},{12,8},{14,10},{16,20},{18,... | collective-permute-start | bytes 12296 | tf_op jit(solution)/shard_map/ppermute | solution.py:145
  42.7 0.5 spread_query.1
  43.3 0.7 collective-permute-start.9
  43.9 1.1 %collective-permute-done.12.other = f32[8,128]{1,0:T(8,128)S(1)} collective-permute-done((f32[8,128]{1,0:T(8,128)S(1)}, f32[8,128]{1,0:T(8,128)S(1)}, u32[]{:S(2)}, u32[]{:S(2)}) %collective-permute-start.12) | collective-permute-done | bytes 4128 | tf_op jit(solution)/shard_map/ppermute | solution.py:145
  45.0 0.5 spread_pass.1
  45.5 0.1 collective-permute-start.16
  45.6 4.1 %collective-permute-done.9.other = bf16[256,512]{1,0:T(8,128)(2,1)S(1)} collective-permute-done((bf16[256,512]{1,0:T(8,128)(2,1)S(1)}, bf16[256,512]{1,0:T(8,128)(2,1)S(1)}, u32[]{:S(2)}, u32[]{:S(2)}) %collective-permute-start.9) | collective-permute-done | bytes 262176 | tf_op jit(solution)/shard_map/ppermute | solution.py:145
  49.7 1.6 %collective-permute-start.10 = (bf16[128,512]{1,0:T(8,128)(2,1)S(1)}, bf16[128,512]{1,0:T(8,128)(2,1)S(1)}, u32[]{:S(2)}, u32[]{:S(2)}) collective-permute-start(bf16[128,512]{1,0:T(8,128)(2,1)S(1)} %get-tuple-element.45), channel_id=1, source_target_pairs={{0,8},{2,10},{4,12},{6,14},{8,0},{10,2},{12,4},{14,6},{16,24},{18,... | collective-permute-start | bytes 393224 | tf_op jit(solution)/shard_map/ppermute | solution.py:145
  51.3 0.0 collective-permute-done.16.other
  51.3 0.1 fold_pass.1
  51.4 3.2 %collective-permute-start.17 = (bf16[128,512]{1,0:T(8,128)(2,1)S(1)}, bf16[128,512]{1,0:T(8,128)(2,1)S(1)}, u32[]{:S(2)}, u32[]{:S(2)}) collective-permute-start(bf16[128,512]{1,0:T(8,128)(2,1)S(1)} %get-tuple-element.57), channel_id=1, source_target_pairs={{0,16},{2,18},{4,20},{6,22},{8,24},{10,26},{12,28},{14,30},{16,0},... | collective-permute-start | bytes 393224 | tf_op jit(solution)/shard_map/ppermute | solution.py:145
  54.7 1.5 %collective-permute-start.14 = (bf16[144,512]{1,0:T(8,128)(2,1)S(1)}, bf16[144,512]{1,0:T(8,128)(2,1)S(1)}, u32[]{:S(2)}, u32[]{:S(2)}) collective-permute-start(bf16[144,512]{1,0:T(8,128)(2,1)S(1)} %pack.2.refs_0_.raw), channel_id=1, source_target_pairs={{0,1},{1,0},{2,3},{3,2},{4,5},{5,4},{6,7},{7,6},{8,9},{9,8},{10,11... | collective-permute-start | bytes 442376 | tf_op jit(solution)/shard_map/ppermute | solution.py:145
  56.2 0.5 collective-permute-start.19
  56.7 0.0 collective-permute-done.10.other
  56.7 0.1 grad_query.1.grad
  56.8 1.6 %collective-permute-start.13 = (bf16[128,512]{1,0:T(8,128)(2,1)S(1)}, bf16[128,512]{1,0:T(8,128)(2,1)S(1)}, u32[]{:S(2)}, u32[]{:S(2)}) collective-permute-start(bf16[128,512]{1,0:T(8,128)(2,1)S(1)} %grad_query.1.grad), channel_id=1, source_target_pairs={{0,1},{1,0},{2,3},{3,2},{4,5},{5,4},{6,7},{7,6},{8,9},{9,8},{10,11... | collective-permute-start | bytes 393224 | tf_op jit(solution)/shard_map/ppermute | solution.py:145
  58.4 0.6 collective-permute-done.17.other
  59.0 1.6 %collective-permute-start.18 = (bf16[128,512]{1,0:T(8,128)(2,1)S(1)}, bf16[128,512]{1,0:T(8,128)(2,1)S(1)}, u32[]{:S(2)}, u32[]{:S(2)}) collective-permute-start(bf16[128,512]{1,0:T(8,128)(2,1)S(1)} %grad_pass.1.grad), channel_id=1, source_target_pairs={{0,1},{1,0},{2,3},{3,2},{4,5},{5,4},{6,7},{7,6},{8,9},{9,8},{10,11... | collective-permute-start | bytes 393224 | tf_op jit(solution)/shard_map/ppermute | solution.py:145
  60.6 0.0 collective-permute-done.14.raw_other
  60.6 2.8 %collective-permute-done.13.grad_other = bf16[128,512]{1,0:T(8,128)(2,1)S(1)} collective-permute-done((bf16[128,512]{1,0:T(8,128)(2,1)S(1)}, bf16[128,512]{1,0:T(8,128)(2,1)S(1)}, u32[]{:S(2)}, u32[]{:S(2)}) %collective-permute-start.13) | collective-permute-done | bytes 131104 | tf_op jit(solution)/shard_map/ppermute | solution.py:145
  63.4 0.0 copy-done.1
  63.4 0.0 copy-start.3
  63.5 2.2 %copy-done.3 = bf16[2048,1024]{1,0:T(8,128)(2,1)S(1)} copy-done((bf16[2048,1024]{1,0:T(8,128)(2,1)S(1)}, bf16[2048,1024]{1,0:T(8,128)(2,1)}, u32[]{:S(2)}) %copy-start.3) | copy-done | bytes 4194328
  65.6 3.2 %decode_one.2 = (bf16[128,512]{1,0:T(8,128)(2,1)S(1)}, f32[128,512]{1,0:T(8,128)S(1)}) custom-call(s32[1]{0:T(128)} %bitcast.me, bf16[128,512]{1,0:T(8,128)(2,1)S(1)} %grad_query.1.grad, bf16[128,512]{1,0:T(8,128)(2,1)S(1)} %collective-permute-done.13.grad_other, bf16[144,512]{1,0:T(8,128)(2,1)S(1)} %pack.2.refs_0_.raw, ...), custom_call_target="tpu_custom_call" | custom-call | tf_op jit(solution)/shard_map/decode_one/pallas_call | solution.py:169
  68.9 1.6 %collective-permute-start.15 = (bf16[128,512]{1,0:T(8,128)(2,1)S(1)}, bf16[128,512]{1,0:T(8,128)(2,1)S(1)}, u32[]{:S(2)}, u32[]{:S(2)}) collective-permute-start(bf16[128,512]{1,0:T(8,128)(2,1)S(1)} %get-tuple-element.52), channel_id=1, source_target_pairs={{0,1},{1,0},{2,3},{3,2},{4,5},{5,4},{6,7},{7,6},{8,9},{9,8},{10,11... | collective-permute-start | bytes 393224 | tf_op jit(solution)/shard_map/ppermute | solution.py:145
  70.5 0.0 collective-permute-done.19.raw_other
  70.5 0.0 collective-permute-done.18.grad_other
  70.5 3.2 %decode_one.3 = (bf16[128,512]{1,0:T(8,128)(2,1)S(1)}, f32[128,512]{1,0:T(8,128)S(1)}) custom-call(s32[1]{0:T(128)} %bitcast.me, bf16[128,512]{1,0:T(8,128)(2,1)S(1)} %grad_pass.1.grad, bf16[128,512]{1,0:T(8,128)(2,1)S(1)} %collective-permute-done.18.grad_other, bf16[144,512]{1,0:T(8,128)(2,1)S(1)} %pack.3.refs_4_.raw_pass.raw, ...), custom_call_target="tpu_custom_call" | custom-call | tf_op jit(solution)/shard_map/decode_one/pallas_call | solution.py:169
  73.7 0.6 collective-permute-start.20
  74.3 0.0 collective-permute-done.15.other
  74.3 0.7 out_query.1
  75.0 3.8 %collective-permute-done.20.other = bf16[128,512]{1,0:T(8,128)(2,1)S(1)} collective-permute-done((bf16[128,512]{1,0:T(8,128)(2,1)S(1)}, bf16[128,512]{1,0:T(8,128)(2,1)S(1)}, u32[]{:S(2)}, u32[]{:S(2)}) %collective-permute-start.20) | collective-permute-done | bytes 131104 | tf_op jit(solution)/shard_map/ppermute | solution.py:145
  78.8 0.7 out_pass.1
  (7 shorter events, 0.2 us)
Async XLA Ops:
  6.8 2.0 %copy-start = (bf16[1024,2048]{1,0:T(8,128)(2,1)}, bf16[1024,2048]{1,0:T(8,128)(2,1)S(1)}, u32[]{:S(2)}) copy-start(bf16[1024,2048]{1,0:T(8,128)(2,1)S(1)} %get-tuple-element.49.w_in) | copy-start | bytes 12582916
  8.8 2.0 %copy-start.2 = (bf16[2048,1024]{1,0:T(8,128)(2,1)}, bf16[2048,1024]{1,0:T(8,128)(2,1)S(1)}, u32[]{:S(2)}) copy-start(bf16[2048,1024]{1,0:T(8,128)(2,1)S(1)} %get-tuple-element.50.w_out) | copy-start | bytes 12582916
  10.8 7.3 %collective-permute-start.4 = (bf16[128,512]{1,0:T(8,128)(2,1)S(1)}, bf16[128,512]{1,0:T(8,128)(2,1)S(1)}, u32[]{:S(2)}, u32[]{:S(2)}) collective-permute-start(bf16[128,512]{1,0:T(8,128)(2,1)S(1)} %get-tuple-element.35), channel_id=1, source_target_pairs={{0,1},{1,0},{2,3},{3,2},{4,5},{5,4},{6,7},{7,6},{8,9},{9,8},{10,11... | collective-permute-start | bytes 393224 | tf_op jit(solution)/shard_map/ppermute | solution.py:145
  13.8 7.6 %collective-permute-start = (bf16[128,512]{1,0:T(8,128)(2,1)S(1)}, bf16[128,512]{1,0:T(8,128)(2,1)S(1)}, u32[]{:S(2)}, u32[]{:S(2)}) collective-permute-start(bf16[128,512]{1,0:T(8,128)(2,1)S(1)} %get-tuple-element.32), channel_id=1, source_target_pairs={{0,1},{1,0},{2,3},{3,2},{4,5},{5,4},{6,7},{7,6},{8,9},{9,8},{10,11... | collective-permute-start | bytes 393224 | tf_op jit(solution)/shard_map/ppermute | solution.py:145
  18.1 7.5 %collective-permute-start.5 = (bf16[144,512]{1,0:T(8,128)(2,1)S(1)}, bf16[144,512]{1,0:T(8,128)(2,1)S(1)}, u32[]{:S(2)}, u32[]{:S(2)}) collective-permute-start(bf16[144,512]{1,0:T(8,128)(2,1)S(1)} %pack.3.refs_4_.raw_pass.raw), channel_id=1, source_target_pairs={{0,16},{2,18},{4,20},{6,22},{8,24},{10,26},{12,28},{14,30},{16,0},... | collective-permute-start | bytes 442376 | tf_op jit(solution)/shard_map/ppermute | solution.py:145
  21.4 6.0 %collective-permute-start.1 = (bf16[144,512]{1,0:T(8,128)(2,1)S(1)}, bf16[144,512]{1,0:T(8,128)(2,1)S(1)}, u32[]{:S(2)}, u32[]{:S(2)}) collective-permute-start(bf16[144,512]{1,0:T(8,128)(2,1)S(1)} %pack.2.refs_0_.raw), channel_id=1, source_target_pairs={{0,8},{2,10},{4,12},{6,14},{8,0},{10,2},{12,4},{14,6},{16,24},{18,... | collective-permute-start | bytes 442376 | tf_op jit(solution)/shard_map/ppermute | solution.py:145
  23.0 5.6 %collective-permute-start.6 = (bf16[144,512]{1,0:T(8,128)(2,1)S(1)}, bf16[144,512]{1,0:T(8,128)(2,1)S(1)}, u32[]{:S(2)}, u32[]{:S(2)}) collective-permute-start(bf16[144,512]{1,0:T(8,128)(2,1)S(1)} %pack.3.refs_4_.raw_pass.raw), channel_id=1, source_target_pairs={{0,2},{2,0},{4,6},{6,4},{8,10},{10,8},{12,14},{14,12},{16,18},{18,... | collective-permute-start | bytes 442376 | tf_op jit(solution)/shard_map/ppermute | solution.py:145
  23.0 6.6 %collective-permute-start.2 = (bf16[144,512]{1,0:T(8,128)(2,1)S(1)}, bf16[144,512]{1,0:T(8,128)(2,1)S(1)}, u32[]{:S(2)}, u32[]{:S(2)}) collective-permute-start(bf16[144,512]{1,0:T(8,128)(2,1)S(1)} %pack.2.refs_0_.raw), channel_id=1, source_target_pairs={{0,4},{2,6},{4,0},{6,2},{8,12},{10,14},{12,8},{14,10},{16,20},{18,... | collective-permute-start | bytes 442376 | tf_op jit(solution)/shard_map/ppermute | solution.py:145
  25.6 4.0 %collective-permute-start.7 = (bf16[144,512]{1,0:T(8,128)(2,1)S(1)}, bf16[144,512]{1,0:T(8,128)(2,1)S(1)}, u32[]{:S(2)}, u32[]{:S(2)}) collective-permute-start(bf16[144,512]{1,0:T(8,128)(2,1)S(1)} %collective-permute-done.5.refs_5_), channel_id=1, source_target_pairs={{0,2},{2,0},{4,6},{6,4},{8,10},{10,8},{12,14},{14,12},{16,18},{18,... | collective-permute-start | bytes 442376 | tf_op jit(solution)/shard_map/ppermute | solution.py:145
  27.3 5.1 %collective-permute-start.3 = (bf16[144,512]{1,0:T(8,128)(2,1)S(1)}, bf16[144,512]{1,0:T(8,128)(2,1)S(1)}, u32[]{:S(2)}, u32[]{:S(2)}) collective-permute-start(bf16[144,512]{1,0:T(8,128)(2,1)S(1)} %collective-permute-done.1.refs_1_), channel_id=1, source_target_pairs={{0,4},{2,6},{4,0},{6,2},{8,12},{10,14},{12,8},{14,10},{16,20},{18,... | collective-permute-start | bytes 442376 | tf_op jit(solution)/shard_map/ppermute | solution.py:145
  28.6 34.8 %copy-start.1 = (bf16[1024,2048]{1,0:T(8,128)(2,1)S(1)}, bf16[1024,2048]{1,0:T(8,128)(2,1)}, u32[]{:S(2)}) copy-start(bf16[1024,2048]{1,0:T(8,128)(2,1)} %copy-done) | copy-start | bytes 12582916
  33.6 4.0 %collective-permute-start.8 = (f32[16,512]{1,0:T(8,128)S(1)}, f32[16,512]{1,0:T(8,128)S(1)}, u32[]{:S(2)}, u32[]{:S(2)}) collective-permute-start(f32[16,512]{1,0:T(8,128)S(1)} %get-tuple-element.37.table), channel_id=1, source_target_pairs={{0,1},{1,0},{2,3},{3,2},{4,5},{5,4},{6,7},{7,6},{8,9},{9,8},{10,11... | collective-permute-start | bytes 98312 | tf_op jit(solution)/shard_map/ppermute | solution.py:145
  37.6 3.7 %collective-permute-start.11 = (f32[8,128]{1,0:T(8,128)S(1)}, f32[8,128]{1,0:T(8,128)S(1)}, u32[]{:S(2)}, u32[]{:S(2)}) collective-permute-start(f32[8,128]{1,0:T(8,128)S(1)} %get-tuple-element.47.sums), channel_id=1, source_target_pairs={{0,8},{2,10},{4,12},{6,14},{8,0},{10,2},{12,4},{14,6},{16,24},{18,... | collective-permute-start | bytes 12296 | tf_op jit(solution)/shard_map/ppermute | solution.py:145
  41.3 3.7 %collective-permute-start.12 = (f32[8,128]{1,0:T(8,128)S(1)}, f32[8,128]{1,0:T(8,128)S(1)}, u32[]{:S(2)}, u32[]{:S(2)}) collective-permute-start(f32[8,128]{1,0:T(8,128)S(1)} %add_sums.2.sums), channel_id=1, source_target_pairs={{0,4},{2,6},{4,0},{6,2},{8,12},{10,14},{12,8},{14,10},{16,20},{18,... | collective-permute-start | bytes 12296 | tf_op jit(solution)/shard_map/ppermute | solution.py:145
  43.3 6.4 %collective-permute-start.9 = (bf16[256,512]{1,0:T(8,128)(2,1)S(1)}, bf16[256,512]{1,0:T(8,128)(2,1)S(1)}, u32[]{:S(2)}, u32[]{:S(2)}) collective-permute-start(bf16[256,512]{1,0:T(8,128)(2,1)S(1)} %get-tuple-element.43), channel_id=1, source_target_pairs={{0,4},{2,6},{4,0},{6,2},{8,12},{10,14},{12,8},{14,10},{16,20},{18,... | collective-permute-start | bytes 786440 | tf_op jit(solution)/shard_map/ppermute | solution.py:145
  45.5 5.9 %collective-permute-start.16 = (bf16[256,512]{1,0:T(8,128)(2,1)S(1)}, bf16[256,512]{1,0:T(8,128)(2,1)S(1)}, u32[]{:S(2)}, u32[]{:S(2)}) collective-permute-start(bf16[256,512]{1,0:T(8,128)(2,1)S(1)} %get-tuple-element.55), channel_id=1, source_target_pairs={{0,2},{2,0},{4,6},{6,4},{8,10},{10,8},{12,14},{14,12},{16,18},{18,... | collective-permute-start | bytes 786440 | tf_op jit(solution)/shard_map/ppermute | solution.py:145
  49.7 6.9 %collective-permute-start.10 = (bf16[128,512]{1,0:T(8,128)(2,1)S(1)}, bf16[128,512]{1,0:T(8,128)(2,1)S(1)}, u32[]{:S(2)}, u32[]{:S(2)}) collective-permute-start(bf16[128,512]{1,0:T(8,128)(2,1)S(1)} %get-tuple-element.45), channel_id=1, source_target_pairs={{0,8},{2,10},{4,12},{6,14},{8,0},{10,2},{12,4},{14,6},{16,24},{18,... | collective-permute-start | bytes 393224 | tf_op jit(solution)/shard_map/ppermute | solution.py:145
  51.4 7.6 %collective-permute-start.17 = (bf16[128,512]{1,0:T(8,128)(2,1)S(1)}, bf16[128,512]{1,0:T(8,128)(2,1)S(1)}, u32[]{:S(2)}, u32[]{:S(2)}) collective-permute-start(bf16[128,512]{1,0:T(8,128)(2,1)S(1)} %get-tuple-element.57), channel_id=1, source_target_pairs={{0,16},{2,18},{4,20},{6,22},{8,24},{10,26},{12,28},{14,30},{16,0},... | collective-permute-start | bytes 393224 | tf_op jit(solution)/shard_map/ppermute | solution.py:145
  54.7 6.0 %collective-permute-start.14 = (bf16[144,512]{1,0:T(8,128)(2,1)S(1)}, bf16[144,512]{1,0:T(8,128)(2,1)S(1)}, u32[]{:S(2)}, u32[]{:S(2)}) collective-permute-start(bf16[144,512]{1,0:T(8,128)(2,1)S(1)} %pack.2.refs_0_.raw), channel_id=1, source_target_pairs={{0,1},{1,0},{2,3},{3,2},{4,5},{5,4},{6,7},{7,6},{8,9},{9,8},{10,11... | collective-permute-start | bytes 442376 | tf_op jit(solution)/shard_map/ppermute | solution.py:145
  56.2 14.3 %collective-permute-start.19 = (bf16[144,512]{1,0:T(8,128)(2,1)S(1)}, bf16[144,512]{1,0:T(8,128)(2,1)S(1)}, u32[]{:S(2)}, u32[]{:S(2)}) collective-permute-start(bf16[144,512]{1,0:T(8,128)(2,1)S(1)} %pack.3.refs_4_.raw_pass.raw), channel_id=1, source_target_pairs={{0,1},{1,0},{2,3},{3,2},{4,5},{5,4},{6,7},{7,6},{8,9},{9,8},{10,11... | collective-permute-start | bytes 442376 | tf_op jit(solution)/shard_map/ppermute | solution.py:145
  56.8 6.6 %collective-permute-start.13 = (bf16[128,512]{1,0:T(8,128)(2,1)S(1)}, bf16[128,512]{1,0:T(8,128)(2,1)S(1)}, u32[]{:S(2)}, u32[]{:S(2)}) collective-permute-start(bf16[128,512]{1,0:T(8,128)(2,1)S(1)} %grad_query.1.grad), channel_id=1, source_target_pairs={{0,1},{1,0},{2,3},{3,2},{4,5},{5,4},{6,7},{7,6},{8,9},{9,8},{10,11... | collective-permute-start | bytes 393224 | tf_op jit(solution)/shard_map/ppermute | solution.py:145
  59.0 11.4 %collective-permute-start.18 = (bf16[128,512]{1,0:T(8,128)(2,1)S(1)}, bf16[128,512]{1,0:T(8,128)(2,1)S(1)}, u32[]{:S(2)}, u32[]{:S(2)}) collective-permute-start(bf16[128,512]{1,0:T(8,128)(2,1)S(1)} %grad_pass.1.grad), channel_id=1, source_target_pairs={{0,1},{1,0},{2,3},{3,2},{4,5},{5,4},{6,7},{7,6},{8,9},{9,8},{10,11... | collective-permute-start | bytes 393224 | tf_op jit(solution)/shard_map/ppermute | solution.py:145
  63.4 2.2 %copy-start.3 = (bf16[2048,1024]{1,0:T(8,128)(2,1)S(1)}, bf16[2048,1024]{1,0:T(8,128)(2,1)}, u32[]{:S(2)}) copy-start(bf16[2048,1024]{1,0:T(8,128)(2,1)} %copy-done.2) | copy-start | bytes 12582916
  68.9 5.4 %collective-permute-start.15 = (bf16[128,512]{1,0:T(8,128)(2,1)S(1)}, bf16[128,512]{1,0:T(8,128)(2,1)S(1)}, u32[]{:S(2)}, u32[]{:S(2)}) collective-permute-start(bf16[128,512]{1,0:T(8,128)(2,1)S(1)} %get-tuple-element.52), channel_id=1, source_target_pairs={{0,1},{1,0},{2,3},{3,2},{4,5},{5,4},{6,7},{7,6},{8,9},{9,8},{10,11... | collective-permute-start | bytes 393224 | tf_op jit(solution)/shard_map/ppermute | solution.py:145
  73.7 5.0 %collective-permute-start.20 = (bf16[128,512]{1,0:T(8,128)(2,1)S(1)}, bf16[128,512]{1,0:T(8,128)(2,1)S(1)}, u32[]{:S(2)}, u32[]{:S(2)}) collective-permute-start(bf16[128,512]{1,0:T(8,128)(2,1)S(1)} %get-tuple-element.59), channel_id=1, source_target_pairs={{0,1},{1,0},{2,3},{3,2},{4,5},{5,4},{6,7},{7,6},{8,9},{9,8},{10,11... | collective-permute-start | bytes 393224 | tf_op jit(solution)/shard_map/ppermute | solution.py:145

commit v3 on v2

--- a/solution.py
+++ b/solution.py
@@ -173,13 +173,14 @@
         out_shape=[pltpu.VMEM(shape, dtype) for shape, dtype in outs],
         scratch_shapes=list(scratch),
         compiler_params=pltpu.CompilerParams(vmem_limit_bytes=mebibytes << 20),
+        cost_estimate=pl.CostEstimate(flops=1, bytes_accessed=1, transcendentals=0),
         name=name,
     )(*scalars, *[pltpu.with_memory_space_constraint(x, pltpu.VMEM) for x in operands])
 
 
 def encode_kernel(
-    tile, me, scale, xq, xp, w_in, w_out, owner, mask, served,
-    send_q, send_p, own_q, own_p, slope, slots_out, served_out, scale_out, w_in_kept, w_out_kept,
+    tile, me, place, scale, xq, xp, w_in, w_out, owner, mask, served,
+    send_q, send_p, own_q, own_p, pre_act, slots_out, served_out, scale_out, w_in_kept, w_out_kept,
     states, total, owner_held, mask_held, served_held, sems,
 ):
     rows = xq.shape[0]
@@ -221,7 +222,7 @@
         copies[5 + 2 * t].wait()
         pre = jnp.dot(states[...], w_in_kept[:, at], preferred_element_type=f32)
         cdf = 0.5 * (1.0 + lax.erf(pre * root_half))
-        slope[:, at] = (cdf + pre * jnp.exp(-0.5 * pre * pre) * inv_root_two_pi).astype(bf16)
+        pre_act[:, at] = pre
         hidden = (pre * cdf).astype(bf16)
         copies[6 + 2 * t].wait()
         part = jnp.dot(hidden, w_out_kept[at, :], preferred_element_type=f32)
@@ -236,7 +237,7 @@
         own[...] = mine + halves(first, states[at : at + rows, :].astype(f32))[0]
 
 
-def encode_both(me, scale, xq, xp, w_in, w_out, owner, mask, served):
+def encode_both(me, place, scale, xq, xp, w_in, w_out, owner, mask, served):
     rows, width = xq.shape
     hidden = w_in.shape[1]
     tile = min(512, hidden)
@@ -245,14 +246,14 @@
     operands = (xq, xp, w_in, w_out, owner.T, mask.T, served)
     return pl.pallas_call(
         functools.partial(encode_kernel, tile),
-        in_specs=[smem] * 2 + [hbm] * 7,
+        in_specs=[smem] * 3 + [hbm] * 7,
         out_specs=[vmem] * 10,
         out_shape=[
             pltpu.VMEM(half, bf16),
             pltpu.VMEM(half, bf16),
             pltpu.VMEM(half, f32),
             pltpu.VMEM(half, f32),
-            pltpu.VMEM((2 * rows, hidden), bf16),
+            pltpu.VMEM((2 * rows, hidden), f32),
             pltpu.VMEM((owners, rows), bf16),
             pltpu.VMEM((owners, served.shape[2]), bf16),
             pltpu.VMEM((8, rows), f32),
@@ -269,7 +270,18 @@
         ],
         compiler_params=pltpu.CompilerParams(vmem_limit_bytes=8 << 20),
         name="encode_both",
-    )(me, scale, *[pltpu.with_memory_space_constraint(x, pltpu.HBM) for x in operands])
+    )(me, place, scale, *[pltpu.with_memory_space_constraint(x, pltpu.HBM) for x in operands])
+
+
+def slope_kernel(pre_act, slope):
+    step = 32
+
+    def body(n, carry):
+        at = pl.ds(pl.multiple_of(n * step, step), step)
+        slope[at, :] = gelu_slope(pre_act[at, :]).astype(bf16)
+        return carry
+
+    lax.fori_loop(0, pre_act.shape[0] // step, body, 0)
 
 
 def pack_kernel(own, other, numbers, out):
@@ -308,13 +320,13 @@
         part = p_all[a * rows : (a + 1) * rows, :]
         block = part.astype(f32)
         square = jnp.sum(block * block, axis=1, keepdims=True)
+        table[2 * npass + 2 : 2 * npass + 3, a * rows : (a + 1) * rows] = jnp.sum(
+            eye * square, axis=0, keepdims=True
+        )
         scores = lax.dot_general(part, queries, nt, preferred_element_type=f32)
         if a == 0:
             table[2 * npass + 1 : 2 * npass + 2, :rows] = jnp.sum(
                 eye * scores[:, :rows], axis=0, keepdims=True
-            )
-            table[2 * npass + 2 : 2 * npass + 3, :rows] = jnp.sum(
-                eye * square, axis=0, keepdims=True
             )
         for b in range(nq):
             lanes = slice(b * rows, (b + 1) * rows)
@@ -356,43 +368,59 @@
     full = table[...] + other[...]
     raw, square = full[:npass], full[npass : 2 * npass]
     inv_q = lax.rsqrt(full[2 * npass : 2 * npass + 1] + norm_eps)
-    inv_pos = lax.rsqrt(full[2 * npass + 2 : 2 * npass + 3] + norm_eps)
+    inv_pass = lax.rsqrt(full[2 * npass + 2 : 2 * npass + 3] + norm_eps)
     inv_neg = lax.rsqrt(square + norm_eps)
-    exp_neg = valid[...] * jnp.exp(logit_scale * (raw * inv_q * inv_neg))
-    pos_score = full[2 * npass + 1 : 2 * npass + 2] * inv_q * inv_pos
+    neg_score = raw * inv_q * inv_neg
+    exp_neg = valid[...] * jnp.exp(logit_scale * neg_score)
+    pos_score = full[2 * npass + 1 : 2 * npass + 2] * inv_q * inv_pass
     coefs[...] = jnp.zeros_like(coefs)
     coefs[:npass] = exp_neg
     coefs[npass : 2 * npass] = exp_neg * inv_neg
-    coefs[2 * npass : 2 * npass + 1] = inv_q
-    coefs[2 * npass + 1 : 2 * npass + 2] = inv_pos
+    coefs[2 * npass : 3 * npass] = exp_neg * neg_score
+    coefs[3 * npass : 3 * npass + 1] = inv_q
+    coefs[3 * npass + 1 : 3 * npass + 2] = inv_pass
+    coefs[3 * npass + 2 : 3 * npass + 3] = pos_score
     neg_sum = jnp.sum(exp_neg, axis=0, keepdims=True)
+    neg_dot = jnp.sum(exp_neg * neg_score, axis=0, keepdims=True)
     sums[...] = jnp.zeros_like(sums)
     for n in range(nq):
         sums[n : n + 1, :] = neg_sum[:, n * rows : (n + 1) * rows]
+        sums[2 * nq + n : 2 * nq + n + 1, :] = neg_dot[:, n * rows : (n + 1) * rows]
     sums[nq : nq + 1, :] = jnp.exp(logit_scale * pos_score[:, :rows])
 
 
 def weigh(table, other, valid, rows):
+    nq, npass = len(query_at), len(pass_at)
     return local(
         functools.partial(weigh_kernel, rows),
         "weigh",
-        [(table.shape, f32), ((2 * len(query_at), rows), f32)],
+        [((-(-(3 * npass + 3) // 8) * 8, nq * rows), f32), ((-(-3 * nq // 8) * 8, rows), f32)],
         (table, other, valid),
     )
 
 
-def add_sums_kernel(bit, sums, other, out):
+def add_sums_kernel(bit, sums, other, *refs):
+    out = refs[-1]
     nq = len(query_at)
+    out[...] = sums[...]
     for n, at in enumerate(query_at):
         m = query_at.index(at ^ bit)
-        for k, l in ((n, m), (nq + n, nq + m)):
+        for first in (0, nq, 2 * nq):
+            k, l = first + n, first + m
             out[k : k + 1, :] = sums[k : k + 1, :] + other[l : l + 1, :]
+
+
+def exchange_sums(sums, bit, *after):
+    kernel = functools.partial(add_sums_kernel, bit)
+    return local(kernel, "add_sums", [(sums.shape, f32)], (sums, swap(sums, "dp", bit), *after))[0]
 
 
 def spread_query_kernel(rows, coefs, pick, p_all, kept, sent):
     npass = len(pass_at)
     passages = p_all[...]
-    for b in range(len(query_at)):
+    near = [b for b, at in enumerate(query_at) if not at & query_bits[0]]
+    far = [b for b, at in enumerate(query_at) if at & query_bits[0]]
+    for b in near + far:
         lanes = slice(b * rows, (b + 1) * rows)
         pieces = []
         for a in range(npass):
@@ -400,84 +428,132 @@
             piece = piece * coefs[npass + a : npass + a + 1, lanes]
             pieces.append(piece.T.astype(bf16))
         weights = jnp.concatenate(pieces, axis=1)
-        out, at = (kept, b) if b < len(query_at) // 2 else (sent, b - len(query_at) // 2)
-        out[at * rows : (at + 1) * rows, :] = jnp.dot(
-            weights, passages, preferred_element_type=f32
-        ).astype(out.dtype)
-
-
-def spread_pass_kernel(rows, scale, coefs, sums, pick, q_all, kept, sent):
+        values = jnp.dot(weights, passages, preferred_element_type=f32)
+        out, at = (kept, near.index(b)) if b in near else (sent, far.index(b))
+        out[at * rows : (at + 1) * rows, :] = values.astype(out.dtype)
+
+
+def spread_query(coefs, pick, p_all, rows):
+    half = (len(query_at) // 2 * rows, p_all.shape[1])
+    return local(
+        functools.partial(spread_query_kernel, rows),
+        "spread_query",
+        [(half, f32), (half, bf16)],
+        (coefs, pick, p_all),
+        3,
+    )
+
+
+def column_of(eye, row):
+    return jnp.sum(eye * row, axis=1, keepdims=True)
+
+
+def spread_pass_kernel(rows, scale, coefs, sums, pick, q_all, p_all, kept, *sent):
     nq, npass = len(query_at), len(pass_at)
-    total = sums[:nq] + sums[nq:]
-    share = scale[:nq] / total
-    pos = -share[:1] * sums[:1] * coefs[2 * npass : 2 * npass + 1, :rows]
+    eye = eye_of(rows)
+    share = scale[:nq] / (sums[:nq] + sums[nq : 2 * nq])
+    pos = -share[:1] * sums[:1]
     share = jnp.concatenate([share[n : n + 1] for n in range(nq)], axis=1)
-    scaled = share * coefs[2 * npass : 2 * npass + 1]
+    scaled = share * coefs[3 * npass : 3 * npass + 1]
     queries = q_all[...]
     for a in range(npass):
-        weights = pick[a * rows : (a + 1) * rows, :].astype(f32) * (coefs[a : a + 1] * scaled)
+        at = slice(a * rows, (a + 1) * rows)
+        chosen = pick[at, :]
+        weights = chosen.astype(f32) * (coefs[a : a + 1] * scaled)
+        product = share * coefs[2 * npass + a : 2 * npass + a + 1]
+        high = product.astype(bf16).astype(f32)
+        parts = jnp.concatenate([high, product - high, jnp.zeros((14, nq * rows), f32)], axis=0)
+        dots = lax.dot_general(parts.astype(bf16), chosen, nt, preferred_element_type=f32)
+        dot = jnp.sum(dots, axis=0, keepdims=True)
         if a == 0:
-            weights = jnp.concatenate(
-                [weights[:, :rows] + eye_of(rows) * pos, weights[:, rows:]], axis=1
-            )
-        out, at = (kept, a) if a < npass // 2 else (sent, a - npass // 2)
-        out[at * rows : (at + 1) * rows, :] = jnp.dot(
-            weights.astype(bf16), queries, preferred_element_type=f32
-        ).astype(out.dtype)
-
-
-def spread(kernel, name, operands, rows, width, count):
-    half = (count // 2 * rows, width)
-    return local(functools.partial(kernel, rows), name, [(half, f32), (half, bf16)], operands, 3)
-
-
-def fold_kernel(own, other, kept, sent):
+            own = pos * coefs[3 * npass : 3 * npass + 1, :rows]
+            weights = jnp.concatenate([weights[:, :rows] + eye * own, weights[:, rows:]], axis=1)
+            dot = dot + pos * coefs[3 * npass + 2 : 3 * npass + 3, :rows]
+        values = jnp.dot(weights.astype(bf16), queries, preferred_element_type=f32)
+        along = column_of(eye, dot * coefs[3 * npass + 1 : 3 * npass + 2, at])
+        values = values - along * p_all[at, :].astype(f32)
+        if a < npass // 2:
+            kept[at, :] = values
+        else:
+            sent[a - npass // 2][...] = values.astype(bf16)
+
+
+def spread_pass(scale, coefs, sums, pick, q_all, p_all, rows):
+    half, width = len(pass_at) // 2, q_all.shape[1]
+    kept, *sent = local(
+        functools.partial(spread_pass_kernel, rows),
+        "spread_pass",
+        [((half * rows, width), f32)] + [((rows, width), bf16)] * half,
+        (scale, coefs, sums, pick, q_all, p_all),
+        3,
+    )
+    return kept, sent
+
+
+def fold_pass_kernel(own, first, second, kept, sent):
+    rows = kept.shape[0]
+    kept[...] = own[:rows, :] + first[...].astype(f32)
+    sent[...] = (own[rows:, :] + second[...].astype(f32)).astype(bf16)
+
+
+def fold_pass(own, first, second):
+    half = (own.shape[0] // 2, own.shape[1])
+    return local(fold_pass_kernel, "fold_pass", [(half, f32), (half, bf16)], (own, first, second))
+
+
+def fold_query_kernel(own, other, kept, sent):
     rows = kept.shape[0]
     total = own[...] + other[...].astype(f32)
     kept[...] = total[:rows]
     sent[...] = total[rows:].astype(bf16)
 
 
-def fold(own, other, name):
+def fold_query(own, other):
     half = (own.shape[0] // 2, own.shape[1])
-    return local(fold_kernel, name, [(half, f32), (half, bf16)], (own, other))
+    return local(fold_query_kernel, "fold_query", [(half, f32), (half, bf16)], (own, other))
 
 
 def add_kernel(own, other, out):
     out[...] = (own[...] + other[...].astype(f32)).astype(out.dtype)
 
 
-def grad_query_kernel(own, other, scale, sums, coefs, raw_pass, out):
+def grad_query_kernel(own, other, scale, sums, coefs, raw, raw_pass, grad, rounded):
     nq, npass = len(query_at), len(pass_at)
     rows = own.shape[0]
     eye = eye_of(rows)
+    inv_norm = coefs[3 * npass : 3 * npass + 1, :rows]
     share = scale[:1] / (sums[:1] + sums[nq : nq + 1])
-    pos = sums[:1] * coefs[2 * npass + 1 : 2 * npass + 2, :rows]
-    share = jnp.sum(eye * share, axis=1, keepdims=True)
-    pos = jnp.sum(eye * pos, axis=1, keepdims=True)
-    total = own[...] + other[...].astype(f32) - pos * raw_pass[:rows, :].astype(f32)
-    out[...] = (share * total).astype(bf16)
-
-
-def decode_kernel(
-    tower, tile, me, grad, grad_other, raw, raw_other, slope, w_in, w_out, send, own, total
-):
+    pos = sums[:1] * coefs[3 * npass + 1 : 3 * npass + 2, :rows]
+    dot = share * (sums[2 * nq : 2 * nq + 1] - sums[:1] * coefs[3 * npass + 2 : 3 * npass + 3, :rows])
+    total = own[...] + other[...].astype(f32)
+    total = total - column_of(eye, pos) * raw_pass[:rows, :].astype(f32)
+    values = column_of(eye, share * inv_norm) * total
+    values = values - column_of(eye, dot * inv_norm * inv_norm) * raw[:rows, :].astype(f32)
+    grad[...] = values
+    rounded[...] = values.astype(bf16)
+
+
+def grad_pass_kernel(own, other, coefs, after, grad, rounded):
+    npass = len(pass_at)
+    rows = own.shape[0]
+    inv_norm = column_of(eye_of(rows), coefs[3 * npass + 1 : 3 * npass + 2, :rows])
+    values = inv_norm * (own[...] + other[...].astype(f32))
+    grad[...] = values
+    rounded[...] = values.astype(bf16)
+
+
+def grad_out(kernel, name, own, operands):
+    return local(kernel, name, [(own.shape, f32), (own.shape, bf16)], (own, *operands))
+
+
+def decode_kernel(tower, tile, me, grad, mine, theirs, slope, w_in, w_out, *refs):
+    send, own, total = refs[-3:]
     first = me[0] == 0
-    rows, width = grad.shape
-
-    def joined(mine, theirs):
-        mine, theirs = mine.astype(f32), theirs.astype(f32)
-        return jnp.concatenate(
-            [jnp.where(first, mine, theirs), jnp.where(first, theirs, mine)], axis=1
-        )
-
-    grads = joined(grad[...], grad_other[...])
-    values = joined(raw[:rows, :], raw_other[:rows, :])
-    inv_norm = lax.rsqrt(jnp.sum(values * values, axis=1, keepdims=True) + norm_eps)
-    unit = values * inv_norm
-    grad_out = inv_norm * (grads - unit * jnp.sum(unit * grads, axis=1, keepdims=True))
-    own[...] = halves(first, grad_out)[0]
-    rounded = grad_out.astype(bf16)
+    rows = grad.shape[0]
+    mine, theirs = mine[...], theirs[...]
+    rounded = jnp.concatenate(
+        [jnp.where(first, mine, theirs), jnp.where(first, theirs, mine)], axis=1
+    )
     for t in range(w_in.shape[1] // tile):
         at = slice(t * tile, (t + 1) * tile)
         hidden = lax.dot_general(rounded, w_out[at, :], nt, preferred_element_type=f32)
@@ -489,16 +565,16 @@
             total[...] += part
     mine, theirs = halves(first, total[...])
     send[...] = theirs.astype(bf16)
-    own[...] += mine
-
-
-def decode_one(me, grad, grad_other, raw, raw_other, slope, tower, w_in, w_out):
+    own[...] = grad[...] + mine
+
+
+def decode_one(me, grad, rounded, slope, tower, w_in, w_out, *after):
     rows, width = grad.shape[0], w_in.shape[0]
     return local(
         functools.partial(decode_kernel, tower, min(512, w_in.shape[1])),
         "decode_one",
         [(grad.shape, bf16), (grad.shape, f32)],
-        (grad, grad_other, raw, raw_other, slope, w_in, w_out),
+        (grad, rounded, swap(rounded, "mp", 1), slope, w_in, w_out, *after),
         3,
         [pltpu.VMEM((rows, width), f32)],
         [me],
@@ -523,48 +599,37 @@
     owners = served_rows.shape[1]
     me = lax.axis_index("mp").astype(jnp.int32).reshape(1)
     place = lax.axis_index("dp").astype(jnp.int32).reshape(1)
-    send_q, send_p, own_q, own_p, slope, slots, served, scale, w_in, w_out = encode_both(
-        me, loss_scale.reshape(1), query_states, passage_states, w_in, w_out, neg_owner, neg_mask, served_rows
-    )
+    send_q, send_p, own_q, own_p, pre_act, slots, served, scale, w_in, w_out = encode_both(
+        me, place, loss_scale.reshape(1), query_states, passage_states, w_in, w_out, neg_owner, neg_mask, served_rows
+    )
+    slope = local(slope_kernel, "slope", [(pre_act.shape, bf16)], (pre_act,))[0]
     raw_q = pack(own_q, swap(send_q, "mp", 1), slots)
     raw_p = pack(own_p, swap(send_p, "mp", 1), served)
-    width = raw_q.shape[1]
+    p_blocks = gather_blocks(raw_p, pass_bits)
     q_blocks = gather_blocks(raw_q, query_bits)
-    p_blocks = gather_blocks(raw_p, pass_bits)
-    raw_q_other, raw_p_other = swap(raw_q, "mp", 1), swap(raw_p, "mp", 1)
 
     table, valid, pick, q_all, p_all = score(place, q_blocks, p_blocks, rows, owners)
     coefs, sums = weigh(table, swap(table, "mp", 1), valid, rows)
-    nq, npass = len(query_at), len(pass_at)
-    kept_q, sent_q = spread(
-        spread_query_kernel, "spread_query", (coefs, pick, p_all), rows, width, nq
-    )
-    for bit in query_bits:
-        sums = local(
-            functools.partial(add_sums_kernel, bit),
-            "add_sums",
-            [(sums.shape, f32)],
-            (sums, swap(sums, "dp", bit)),
-        )[0]
-    kept_p, sent_p = spread(
-        spread_pass_kernel, "spread_pass", (scale, coefs, sums, pick, q_all), rows, width, npass
-    )
-    half = ((rows, width), bf16)
-    kept_p, sent_p = fold(kept_p, swap(sent_p, "dp", pass_bits[1]), "fold_pass")
-    grad_p = local(add_kernel, "grad_pass", [half], (kept_p, swap(sent_p, "dp", pass_bits[0])))[0]
-    kept_q, sent_q = fold(kept_q, swap(sent_q, "dp", query_bits[1]), "fold_query")
-    grad_q = local(
+    kept_q, sent_q = spread_query(coefs, pick, p_all, rows)
+    sums = exchange_sums(sums, query_bits[1], sent_q)
+    sums = exchange_sums(sums, query_bits[0])
+    kept_p, sent_p = spread_pass(scale, coefs, sums, pick, q_all, p_all, rows)
+    kept_p, sent_p = fold_pass(kept_p, *[swap(x, "dp", pass_bits[1]) for x in sent_p])
+    kept_q, sent_q = fold_query(kept_q, swap(sent_q, "dp", query_bits[0]))
+    grad_q, round_q = grad_out(
         grad_query_kernel,
         "grad_query",
-        [half],
-        (kept_q, swap(sent_q, "dp", query_bits[0]), scale, sums, coefs, raw_p),
-    )[0]
-    send_q, own_q = decode_one(
-        me, grad_q, swap(grad_q, "mp", 1), raw_q, raw_q_other, slope, 0, w_in, w_out
-    )
-    send_p, own_p = decode_one(
-        me, grad_p, swap(grad_p, "mp", 1), raw_p, raw_p_other, slope, 1, w_in, w_out
-    )
+        kept_q,
+        (swap(sent_q, "dp", query_bits[1]), scale, sums, coefs, raw_q, raw_p),
+    )
+    grad_p, round_p = grad_out(
+        grad_pass_kernel,
+        "grad_pass",
+        kept_p,
+        (swap(sent_p, "dp", pass_bits[0]), coefs, round_q),
+    )
+    send_q, own_q = decode_one(me, grad_q, round_q, slope, 0, w_in, w_out)
+    send_p, own_p = decode_one(me, grad_p, round_p, slope, 1, w_in, w_out, send_q)
     return (
         finish(own_q, swap(send_q, "mp", 1), "out_query"),
         finish(own_p, swap(send_p, "mp", 1), "out_pass"),

time: 79.6 us -> 68.4 us (0.86)
  local copies, waits for them, and re-layouts: 6.17 us -> 0 us
  waiting for transfers between devices: 28 us -> 24.4 us
  starting transfers between devices: 28.1 us -> 26.4 us
    unnamed x8 -> x0, local copies, waits for them, and re-layouts: 6.17 us -> none
    ppermute x21 -> x20, waiting for transfers between devices: 28 us -> 24.4 us  [swap(): return lax.ppermute(values, axis, [(i, i ^ bit) for i in range(size)])]
    ppermute x21 -> x20, starting transfers between devices: 28.1 us -> 26.4 us  [swap(): return lax.ppermute(values, axis, [(i, i ^ bit) for i in range(size)])]
    pallas_call x14 -> x15, Pallas kernels: 8.94 us -> 9.64 us  [local(): pl.pallas_call(kernel, in_specs=[smem] * len(scalars) + [vmem] * len(oper...]
  transfers between devices with their start and end apart: 21 -> 20, of which waited for: 12 -> 9; matrix products, arithmetic and copies ran while one was open for 0% -> 0% of each run, Pallas kernels for 11% -> 13%
where the time goes in v3:
time: 68.4 us; the launch traced here: 68.3 us
  starting transfers between devices  26.4 us (39%)
  waiting for transfers between devices  24.4 us (36%)
  Pallas kernels  16.1 us (24%)
  between operations  1.42 us (2%)
    ppermute x20, starting transfers between devices, swap(): return lax.ppermute(values, axis, [(i, i ^ bit) for i in range(size)])  26.4 us
    ppermute x20, waiting for transfers between devices, swap(): return lax.ppermute(values, axis, [(i, i ^ bit) for i in range(size)])  24.4 us
    pallas_call x15, Pallas kernels, local(): pl.pallas_call(kernel, in_specs=[smem] * len(scalars) + [vmem] * len(oper...  9.64 us
    pallas_call x1, Pallas kernels, encode_both(): pl.pallas_call(functools.partial(encode_kernel, tile), in_specs=[smem] *...  5.05 us
  transfers between devices with their start and end apart: 20, of which 9 were waited for; matrix products, arithmetic and copies ran while one was open for 0% of the time, Pallas kernels for 13%

profile of v3, /device:TPU:0, one launch (start us, length us, event | category | flops | bytes accessed | tf_op | source)
XLA Modules:
  0.0 68.3 jit_solution(15652349909903214874)
XLA Ops:
  1.3 5.1 %encode_both.1 = (bf16[128,512]{1,0:T(8,128)(2,1)S(1)}, bf16[128,512]{1,0:T(8,128)(2,1)S(1)}, f32[128,512]{1,0:T(8,128)S(1)}, f32[128,512]{1,0:T(8,128)S(1)}, f3...) custom-call(s32[1]{0:T(128)} %bitcast.me, ...), custom_call_target="tpu_custom_call" | custom-call | tf_op jit(solution)/shard_map/encode_both/pallas_call | solution.py:247
  6.3 3.0 %collective-permute-start = (bf16[128,512]{1,0:T(8,128)(2,1)S(1)}, bf16[128,512]{1,0:T(8,128)(2,1)S(1)}, u32[]{:S(2)}, u32[]{:S(2)}) collective-permute-start(bf16[128,512]{1,0:T(8,128)(2,1)S(1)} %get-tuple-element.37), channel_id=1, source_target_pairs={{0,1},{1,0},{2,3},{3,2},{4,5},{5,4},{6,7},{7,6},{8,9},{9,8},{10,11... | collective-permute-start | bytes 393224 | tf_op jit(solution)/shard_map/ppermute | solution.py:145
  9.4 0.1 collective-permute-start.4
  9.5 4.2 %collective-permute-done.other = bf16[128,512]{1,0:T(8,128)(2,1)S(1)} collective-permute-done((bf16[128,512]{1,0:T(8,128)(2,1)S(1)}, bf16[128,512]{1,0:T(8,128)(2,1)S(1)}, u32[]{:S(2)}, u32[]{:S(2)}) %collective-permute-start) | collective-permute-done | bytes 131104 | tf_op jit(solution)/shard_map/ppermute | solution.py:145
  13.7 2.2 %collective-permute-start.1 = (bf16[144,512]{1,0:T(8,128)(2,1)S(1)}, bf16[144,512]{1,0:T(8,128)(2,1)S(1)}, u32[]{:S(2)}, u32[]{:S(2)}) collective-permute-start(bf16[144,512]{1,0:T(8,128)(2,1)S(1)} %pack.2.refs_0_.raw), channel_id=1, source_target_pairs={{0,8},{2,10},{4,12},{6,14},{8,0},{10,2},{12,4},{14,6},{16,24},{18,... | collective-permute-start | bytes 442376 | tf_op jit(solution)/shard_map/ppermute | solution.py:145
  15.9 0.0 collective-permute-done.4.other
  16.0 2.7 %collective-permute-start.5 = (bf16[144,512]{1,0:T(8,128)(2,1)S(1)}, bf16[144,512]{1,0:T(8,128)(2,1)S(1)}, u32[]{:S(2)}, u32[]{:S(2)}) collective-permute-start(bf16[144,512]{1,0:T(8,128)(2,1)S(1)} %pack.3.refs_4_.raw_pass), channel_id=1, source_target_pairs={{0,16},{2,18},{4,20},{6,22},{8,24},{10,26},{12,28},{14,30},{16,0},... | collective-permute-start | bytes 442376 | tf_op jit(solution)/shard_map/ppermute | solution.py:145
  18.6 1.5 %collective-permute-start.2 = (bf16[144,512]{1,0:T(8,128)(2,1)S(1)}, bf16[144,512]{1,0:T(8,128)(2,1)S(1)}, u32[]{:S(2)}, u32[]{:S(2)}) collective-permute-start(bf16[144,512]{1,0:T(8,128)(2,1)S(1)} %pack.2.refs_0_.raw), channel_id=1, source_target_pairs={{0,4},{2,6},{4,0},{6,2},{8,12},{10,14},{12,8},{14,10},{16,20},{18,... | collective-permute-start | bytes 442376 | tf_op jit(solution)/shard_map/ppermute | solution.py:145
  20.1 0.0 collective-permute-start.6
  20.1 0.0 collective-permute-done.1.refs_1_
  20.1 2.4 %collective-permute-start.3 = (bf16[144,512]{1,0:T(8,128)(2,1)S(1)}, bf16[144,512]{1,0:T(8,128)(2,1)S(1)}, u32[]{:S(2)}, u32[]{:S(2)}) collective-permute-start(bf16[144,512]{1,0:T(8,128)(2,1)S(1)} %collective-permute-done.1.refs_1_), channel_id=1, source_target_pairs={{0,4},{2,6},{4,0},{6,2},{8,12},{10,14},{12,8},{14,10},{16,20},{18,... | collective-permute-start | bytes 442376 | tf_op jit(solution)/shard_map/ppermute | solution.py:145
  22.5 2.3 %collective-permute-done.5.refs_5_ = bf16[144,512]{1,0:T(8,128)(2,1)S(1)} collective-permute-done((bf16[144,512]{1,0:T(8,128)(2,1)S(1)}, bf16[144,512]{1,0:T(8,128)(2,1)S(1)}, u32[]{:S(2)}, u32[]{:S(2)}) %collective-permute-start.5) | collective-permute-done | bytes 147488 | tf_op jit(solution)/shard_map/ppermute | solution.py:145
  24.9 0.0 collective-permute-start.7
  24.9 0.0 collective-permute-done.2.refs_2_
  24.9 0.0 collective-permute-done.6.refs_6_
  24.9 2.0 %collective-permute-done.3.refs_3_ = bf16[144,512]{1,0:T(8,128)(2,1)S(1)} collective-permute-done((bf16[144,512]{1,0:T(8,128)(2,1)S(1)}, bf16[144,512]{1,0:T(8,128)(2,1)S(1)}, u32[]{:S(2)}, u32[]{:S(2)}) %collective-permute-start.3) | collective-permute-done | bytes 147488 | tf_op jit(solution)/shard_map/ppermute | solution.py:145
  26.9 0.0 collective-permute-done.7.refs_7_
  26.9 1.1 %score.1 = (f32[16,512]{1,0:T(8,128)S(1)}, f32[4,512]{1,0:T(4,128)S(1)}, bf16[512,512]{1,0:T(8,128)(2,1)S(1)}, bf16[512,512]{1,0:T(8,128)(2,1)S(1)}, bf16[512,512]{1,0:T(8,128)(2,1)S(1)}) custom-call(s32[1]{0:T(128)} %bitcast.1.place, bf16[144,512]{1,0:T(8,128)(2,1)S(1)} %pack.2.refs_0_.raw, bf16[144,512]{1,0:T(8,128)(2,1)S(1)} %collective-permute-done.1.refs_1_, ...), custom_call_target="tpu_custom_call" | custom-call | flops 1 | bytes 1 | tf_op jit(solution)/shard_map/score/pallas_call | solution.py:169
  28.1 1.6 %collective-permute-start.8 = (f32[16,512]{1,0:T(8,128)S(1)}, f32[16,512]{1,0:T(8,128)S(1)}, u32[]{:S(2)}, u32[]{:S(2)}) collective-permute-start(f32[16,512]{1,0:T(8,128)S(1)} %get-tuple-element.42.table), channel_id=1, source_target_pairs={{0,1},{1,0},{2,3},{3,2},{4,5},{5,4},{6,7},{7,6},{8,9},{9,8},{10,11... | collective-permute-start | bytes 98312 | tf_op jit(solution)/shard_map/ppermute | solution.py:145
  29.6 2.4 %collective-permute-done.8.other = f32[16,512]{1,0:T(8,128)S(1)} collective-permute-done((f32[16,512]{1,0:T(8,128)S(1)}, f32[16,512]{1,0:T(8,128)S(1)}, u32[]{:S(2)}, u32[]{:S(2)}) %collective-permute-start.8) | collective-permute-done | bytes 32800 | tf_op jit(solution)/shard_map/ppermute | solution.py:145
  32.1 0.5 spread_query.1
  32.6 1.6 %collective-permute-start.9 = (bf16[256,512]{1,0:T(8,128)(2,1)S(1)}, bf16[256,512]{1,0:T(8,128)(2,1)S(1)}, u32[]{:S(2)}, u32[]{:S(2)}) collective-permute-start(bf16[256,512]{1,0:T(8,128)(2,1)S(1)} %get-tuple-element.48.refs_0_), channel_id=1, source_target_pairs={{0,8},{2,10},{4,12},{6,14},{8,0},{10,2},{12,4},{14,6},{16,24},{18,... | collective-permute-start | bytes 786440 | tf_op jit(solution)/shard_map/ppermute | solution.py:145
  34.2 1.5 %collective-permute-start.11 = (f32[16,128]{1,0:T(8,128)S(1)}, f32[16,128]{1,0:T(8,128)S(1)}, u32[]{:S(2)}, u32[]{:S(2)}) collective-permute-start(f32[16,128]{1,0:T(8,128)S(1)} %get-tuple-element.52.sums), channel_id=1, source_target_pairs={{0,4},{2,6},{4,0},{6,2},{8,12},{10,14},{12,8},{14,10},{16,20},{18,... | collective-permute-start | bytes 24584 | tf_op jit(solution)/shard_map/ppermute | solution.py:145
  35.7 2.2 %collective-permute-done.11.other = f32[16,128]{1,0:T(8,128)S(1)} collective-permute-done((f32[16,128]{1,0:T(8,128)S(1)}, f32[16,128]{1,0:T(8,128)S(1)}, u32[]{:S(2)}, u32[]{:S(2)}) %collective-permute-start.11) | collective-permute-done | bytes 8224 | tf_op jit(solution)/shard_map/ppermute | solution.py:145
  37.9 0.5 collective-permute-start.12
  38.4 3.2 %collective-permute-done.12.other = f32[16,128]{1,0:T(8,128)S(1)} collective-permute-done((f32[16,128]{1,0:T(8,128)S(1)}, f32[16,128]{1,0:T(8,128)S(1)}, u32[]{:S(2)}, u32[]{:S(2)}) %collective-permute-start.12) | collective-permute-done | bytes 8224 | tf_op jit(solution)/shard_map/ppermute | solution.py:145
  41.6 0.6 spread_pass.1
  42.2 0.1 collective-permute-start.15
  42.3 0.5 collective-permute-start.16
  42.8 0.0 collective-permute-done.9.other
  42.9 1.6 %collective-permute-start.10 = (bf16[128,512]{1,0:T(8,128)(2,1)S(1)}, bf16[128,512]{1,0:T(8,128)(2,1)S(1)}, u32[]{:S(2)}, u32[]{:S(2)}) collective-permute-start(bf16[128,512]{1,0:T(8,128)(2,1)S(1)} %get-tuple-element.50), channel_id=1, source_target_pairs={{0,4},{2,6},{4,0},{6,2},{8,12},{10,14},{12,8},{14,10},{16,20},{18,... | collective-permute-start | bytes 393224 | tf_op jit(solution)/shard_map/ppermute | solution.py:145
  44.4 0.0 collective-permute-done.15.first
  44.4 0.0 collective-permute-done.16.second
  44.4 0.1 fold_pass.1
  44.5 1.8 %collective-permute-start.17 = (bf16[128,512]{1,0:T(8,128)(2,1)S(1)}, bf16[128,512]{1,0:T(8,128)(2,1)S(1)}, u32[]{:S(2)}, u32[]{:S(2)}) collective-permute-start(bf16[128,512]{1,0:T(8,128)(2,1)S(1)} %get-tuple-element.65), channel_id=1, source_target_pairs={{0,16},{2,18},{4,20},{6,22},{8,24},{10,26},{12,28},{14,30},{16,0},... | collective-permute-start | bytes 393224 | tf_op jit(solution)/shard_map/ppermute | solution.py:145
  46.3 2.1 %collective-permute-done.10.other = bf16[128,512]{1,0:T(8,128)(2,1)S(1)} collective-permute-done((bf16[128,512]{1,0:T(8,128)(2,1)S(1)}, bf16[128,512]{1,0:T(8,128)(2,1)S(1)}, u32[]{:S(2)}, u32[]{:S(2)}) %collective-permute-start.10) | collective-permute-done | bytes 131104 | tf_op jit(solution)/shard_map/ppermute | solution.py:145
  48.4 0.2 grad_query.1
  48.6 1.6 %collective-permute-start.13 = (bf16[128,512]{1,0:T(8,128)(2,1)S(1)}, bf16[128,512]{1,0:T(8,128)(2,1)S(1)}, u32[]{:S(2)}, u32[]{:S(2)}) collective-permute-start(bf16[128,512]{1,0:T(8,128)(2,1)S(1)} %get-tuple-element.54.mine.after), channel_id=1, source_target_pairs={{0,1},{1,0},{2,3},{3,2},{4,5},{5,4},{6,7},{7,6},{8,9},{9,8},{10,11... | collective-permute-start | bytes 393224 | tf_op jit(solution)/shard_map/ppermute | solution.py:145
  50.2 3.2 %collective-permute-done.17.other = bf16[128,512]{1,0:T(8,128)(2,1)S(1)} collective-permute-done((bf16[128,512]{1,0:T(8,128)(2,1)S(1)}, bf16[128,512]{1,0:T(8,128)(2,1)S(1)}, u32[]{:S(2)}, u32[]{:S(2)}) %collective-permute-start.17) | collective-permute-done | bytes 131104 | tf_op jit(solution)/shard_map/ppermute | solution.py:145
  53.4 0.1 grad_pass.1
  53.5 1.6 %collective-permute-start.18 = (bf16[128,512]{1,0:T(8,128)(2,1)S(1)}, bf16[128,512]{1,0:T(8,128)(2,1)S(1)}, u32[]{:S(2)}, u32[]{:S(2)}) collective-permute-start(bf16[128,512]{1,0:T(8,128)(2,1)S(1)} %get-tuple-element.67.mine), channel_id=1, source_target_pairs={{0,1},{1,0},{2,3},{3,2},{4,5},{5,4},{6,7},{7,6},{8,9},{9,8},{10,11... | collective-permute-start | bytes 393224 | tf_op jit(solution)/shard_map/ppermute | solution.py:145
  55.1 0.8 %slope.1 = bf16[256,2048]{1,0:T(8,128)(2,1)S(1)} custom-call(f32[256,2048]{1,0:T(8,128)S(1)} %get-tuple-element.55.pre_act), custom_call_target="tpu_custom_call" | custom-call | flops 1 | bytes 1 | tf_op jit(solution)/shard_map/slope/pallas_call | solution.py:169
  55.9 0.0 collective-permute-done.13.theirs
  56.0 3.0 %decode_one.2 = (bf16[128,512]{1,0:T(8,128)(2,1)S(1)}, f32[128,512]{1,0:T(8,128)S(1)}) custom-call(s32[1]{0:T(128)} %bitcast.me, f32[128,512]{1,0:T(8,128)S(1)} %get-tuple-element.53.grad, bf16[128,512]{1,0:T(8,128)(2,1)S(1)} %get-tuple-element.54.mine.after, bf16[128,512]{1,0:T(8,128)(2,1)S(1)} %collective-permute-done.13.theirs, ...), custom_call_target="tpu_custom_call" | custom-call | flops 1 | bytes 1 | tf_op jit(solution)/shard_map/decode_one/pallas_call | solution.py:169
  59.0 0.6 collective-permute-start.14
  59.6 0.0 collective-permute-done.18.theirs
  59.6 3.0 %decode_one.3 = (bf16[128,512]{1,0:T(8,128)(2,1)S(1)}, f32[128,512]{1,0:T(8,128)S(1)}) custom-call(s32[1]{0:T(128)} %bitcast.me, f32[128,512]{1,0:T(8,128)S(1)} %get-tuple-element.66.grad, bf16[128,512]{1,0:T(8,128)(2,1)S(1)} %get-tuple-element.67.mine, bf16[128,512]{1,0:T(8,128)(2,1)S(1)} %collective-permute-done.18.theirs, bf16[256,2048]{1,0:T(8,128)(2,1)S(1)} %slope.1, ...), custom_call_target="tpu_custom_call" | custom-call | flops 1 | bytes 1 | tf_op jit(solution)/shard_map/decode_one/pallas_call | solution.py:169
  62.6 1.6 %collective-permute-start.19 = (bf16[128,512]{1,0:T(8,128)(2,1)S(1)}, bf16[128,512]{1,0:T(8,128)(2,1)S(1)}, u32[]{:S(2)}, u32[]{:S(2)}) collective-permute-start(bf16[128,512]{1,0:T(8,128)(2,1)S(1)} %get-tuple-element.69), channel_id=1, source_target_pairs={{0,1},{1,0},{2,3},{3,2},{4,5},{5,4},{6,7},{7,6},{8,9},{9,8},{10,11... | collective-permute-start | bytes 393224 | tf_op jit(solution)/shard_map/ppermute | solution.py:145
  64.2 0.0 collective-permute-done.14.other
  64.2 0.7 out_query.1
  64.9 2.7 %collective-permute-done.19.other = bf16[128,512]{1,0:T(8,128)(2,1)S(1)} collective-permute-done((bf16[128,512]{1,0:T(8,128)(2,1)S(1)}, bf16[128,512]{1,0:T(8,128)(2,1)S(1)}, u32[]{:S(2)}, u32[]{:S(2)}) %collective-permute-start.19) | collective-permute-done | bytes 131104 | tf_op jit(solution)/shard_map/ppermute | solution.py:145
  67.6 0.7 out_pass.1
  (6 shorter events, 0.2 us)
Async XLA Ops:
  6.3 7.4 %collective-permute-start = (bf16[128,512]{1,0:T(8,128)(2,1)S(1)}, bf16[128,512]{1,0:T(8,128)(2,1)S(1)}, u32[]{:S(2)}, u32[]{:S(2)}) collective-permute-start(bf16[128,512]{1,0:T(8,128)(2,1)S(1)} %get-tuple-element.37), channel_id=1, source_target_pairs={{0,1},{1,0},{2,3},{3,2},{4,5},{5,4},{6,7},{7,6},{8,9},{9,8},{10,11... | collective-permute-start | bytes 393224 | tf_op jit(solution)/shard_map/ppermute | solution.py:145
  9.4 6.5 %collective-permute-start.4 = (bf16[128,512]{1,0:T(8,128)(2,1)S(1)}, bf16[128,512]{1,0:T(8,128)(2,1)S(1)}, u32[]{:S(2)}, u32[]{:S(2)}) collective-permute-start(bf16[128,512]{1,0:T(8,128)(2,1)S(1)} %get-tuple-element.40), channel_id=1, source_target_pairs={{0,1},{1,0},{2,3},{3,2},{4,5},{5,4},{6,7},{7,6},{8,9},{9,8},{10,11... | collective-permute-start | bytes 393224 | tf_op jit(solution)/shard_map/ppermute | solution.py:145
  13.7 6.4 %collective-permute-start.1 = (bf16[144,512]{1,0:T(8,128)(2,1)S(1)}, bf16[144,512]{1,0:T(8,128)(2,1)S(1)}, u32[]{:S(2)}, u32[]{:S(2)}) collective-permute-start(bf16[144,512]{1,0:T(8,128)(2,1)S(1)} %pack.2.refs_0_.raw), channel_id=1, source_target_pairs={{0,8},{2,10},{4,12},{6,14},{8,0},{10,2},{12,4},{14,6},{16,24},{18,... | collective-permute-start | bytes 442376 | tf_op jit(solution)/shard_map/ppermute | solution.py:145
  16.0 8.9 %collective-permute-start.5 = (bf16[144,512]{1,0:T(8,128)(2,1)S(1)}, bf16[144,512]{1,0:T(8,128)(2,1)S(1)}, u32[]{:S(2)}, u32[]{:S(2)}) collective-permute-start(bf16[144,512]{1,0:T(8,128)(2,1)S(1)} %pack.3.refs_4_.raw_pass), channel_id=1, source_target_pairs={{0,16},{2,18},{4,20},{6,22},{8,24},{10,26},{12,28},{14,30},{16,0},... | collective-permute-start | bytes 442376 | tf_op jit(solution)/shard_map/ppermute | solution.py:145
  18.6 6.3 %collective-permute-start.2 = (bf16[144,512]{1,0:T(8,128)(2,1)S(1)}, bf16[144,512]{1,0:T(8,128)(2,1)S(1)}, u32[]{:S(2)}, u32[]{:S(2)}) collective-permute-start(bf16[144,512]{1,0:T(8,128)(2,1)S(1)} %pack.2.refs_0_.raw), channel_id=1, source_target_pairs={{0,4},{2,6},{4,0},{6,2},{8,12},{10,14},{12,8},{14,10},{16,20},{18,... | collective-permute-start | bytes 442376 | tf_op jit(solution)/shard_map/ppermute | solution.py:145
  20.1 4.8 %collective-permute-start.6 = (bf16[144,512]{1,0:T(8,128)(2,1)S(1)}, bf16[144,512]{1,0:T(8,128)(2,1)S(1)}, u32[]{:S(2)}, u32[]{:S(2)}) collective-permute-start(bf16[144,512]{1,0:T(8,128)(2,1)S(1)} %pack.3.refs_4_.raw_pass), channel_id=1, source_target_pairs={{0,2},{2,0},{4,6},{6,4},{8,10},{10,8},{12,14},{14,12},{16,18},{18,... | collective-permute-start | bytes 442376 | tf_op jit(solution)/shard_map/ppermute | solution.py:145
  20.1 6.8 %collective-permute-start.3 = (bf16[144,512]{1,0:T(8,128)(2,1)S(1)}, bf16[144,512]{1,0:T(8,128)(2,1)S(1)}, u32[]{:S(2)}, u32[]{:S(2)}) collective-permute-start(bf16[144,512]{1,0:T(8,128)(2,1)S(1)} %collective-permute-done.1.refs_1_), channel_id=1, source_target_pairs={{0,4},{2,6},{4,0},{6,2},{8,12},{10,14},{12,8},{14,10},{16,20},{18,... | collective-permute-start | bytes 442376 | tf_op jit(solution)/shard_map/ppermute | solution.py:145
  24.9 2.0 %collective-permute-start.7 = (bf16[144,512]{1,0:T(8,128)(2,1)S(1)}, bf16[144,512]{1,0:T(8,128)(2,1)S(1)}, u32[]{:S(2)}, u32[]{:S(2)}) collective-permute-start(bf16[144,512]{1,0:T(8,128)(2,1)S(1)} %collective-permute-done.5.refs_5_), channel_id=1, source_target_pairs={{0,2},{2,0},{4,6},{6,4},{8,10},{10,8},{12,14},{14,12},{16,18},{18,... | collective-permute-start | bytes 442376 | tf_op jit(solution)/shard_map/ppermute | solution.py:145
  28.1 4.0 %collective-permute-start.8 = (f32[16,512]{1,0:T(8,128)S(1)}, f32[16,512]{1,0:T(8,128)S(1)}, u32[]{:S(2)}, u32[]{:S(2)}) collective-permute-start(f32[16,512]{1,0:T(8,128)S(1)} %get-tuple-element.42.table), channel_id=1, source_target_pairs={{0,1},{1,0},{2,3},{3,2},{4,5},{5,4},{6,7},{7,6},{8,9},{9,8},{10,11... | collective-permute-start | bytes 98312 | tf_op jit(solution)/shard_map/ppermute | solution.py:145
  32.6 10.2 %collective-permute-start.9 = (bf16[256,512]{1,0:T(8,128)(2,1)S(1)}, bf16[256,512]{1,0:T(8,128)(2,1)S(1)}, u32[]{:S(2)}, u32[]{:S(2)}) collective-permute-start(bf16[256,512]{1,0:T(8,128)(2,1)S(1)} %get-tuple-element.48.refs_0_), channel_id=1, source_target_pairs={{0,8},{2,10},{4,12},{6,14},{8,0},{10,2},{12,4},{14,6},{16,24},{18,... | collective-permute-start | bytes 786440 | tf_op jit(solution)/shard_map/ppermute | solution.py:145
  34.2 3.7 %collective-permute-start.11 = (f32[16,128]{1,0:T(8,128)S(1)}, f32[16,128]{1,0:T(8,128)S(1)}, u32[]{:S(2)}, u32[]{:S(2)}) collective-permute-start(f32[16,128]{1,0:T(8,128)S(1)} %get-tuple-element.52.sums), channel_id=1, source_target_pairs={{0,4},{2,6},{4,0},{6,2},{8,12},{10,14},{12,8},{14,10},{16,20},{18,... | collective-permute-start | bytes 24584 | tf_op jit(solution)/shard_map/ppermute | solution.py:145
  37.9 3.7 %collective-permute-start.12 = (f32[16,128]{1,0:T(8,128)S(1)}, f32[16,128]{1,0:T(8,128)S(1)}, u32[]{:S(2)}, u32[]{:S(2)}) collective-permute-start(f32[16,128]{1,0:T(8,128)S(1)} %add_sums.2.sums), channel_id=1, source_target_pairs={{0,8},{2,10},{4,12},{6,14},{8,0},{10,2},{12,4},{14,6},{16,24},{18,... | collective-permute-start | bytes 24584 | tf_op jit(solution)/shard_map/ppermute | solution.py:145
  42.2 2.2 %collective-permute-start.15 = (bf16[128,512]{1,0:T(8,128)(2,1)S(1)}, bf16[128,512]{1,0:T(8,128)(2,1)S(1)}, u32[]{:S(2)}, u32[]{:S(2)}) collective-permute-start(bf16[128,512]{1,0:T(8,128)(2,1)S(1)} %get-tuple-element.62), channel_id=1, source_target_pairs={{0,2},{2,0},{4,6},{6,4},{8,10},{10,8},{12,14},{14,12},{16,18},{18,... | collective-permute-start | bytes 393224 | tf_op jit(solution)/shard_map/ppermute | solution.py:145
  42.3 2.1 %collective-permute-start.16 = (bf16[128,512]{1,0:T(8,128)(2,1)S(1)}, bf16[128,512]{1,0:T(8,128)(2,1)S(1)}, u32[]{:S(2)}, u32[]{:S(2)}) collective-permute-start(bf16[128,512]{1,0:T(8,128)(2,1)S(1)} %get-tuple-element.63), channel_id=1, source_target_pairs={{0,2},{2,0},{4,6},{6,4},{8,10},{10,8},{12,14},{14,12},{16,18},{18,... | collective-permute-start | bytes 393224 | tf_op jit(solution)/shard_map/ppermute | solution.py:145
  42.9 5.5 %collective-permute-start.10 = (bf16[128,512]{1,0:T(8,128)(2,1)S(1)}, bf16[128,512]{1,0:T(8,128)(2,1)S(1)}, u32[]{:S(2)}, u32[]{:S(2)}) collective-permute-start(bf16[128,512]{1,0:T(8,128)(2,1)S(1)} %get-tuple-element.50), channel_id=1, source_target_pairs={{0,4},{2,6},{4,0},{6,2},{8,12},{10,14},{12,8},{14,10},{16,20},{18,... | collective-permute-start | bytes 393224 | tf_op jit(solution)/shard_map/ppermute | solution.py:145
  44.5 8.9 %collective-permute-start.17 = (bf16[128,512]{1,0:T(8,128)(2,1)S(1)}, bf16[128,512]{1,0:T(8,128)(2,1)S(1)}, u32[]{:S(2)}, u32[]{:S(2)}) collective-permute-start(bf16[128,512]{1,0:T(8,128)(2,1)S(1)} %get-tuple-element.65), channel_id=1, source_target_pairs={{0,16},{2,18},{4,20},{6,22},{8,24},{10,26},{12,28},{14,30},{16,0},... | collective-permute-start | bytes 393224 | tf_op jit(solution)/shard_map/ppermute | solution.py:145
  48.6 7.4 %collective-permute-start.13 = (bf16[128,512]{1,0:T(8,128)(2,1)S(1)}, bf16[128,512]{1,0:T(8,128)(2,1)S(1)}, u32[]{:S(2)}, u32[]{:S(2)}) collective-permute-start(bf16[128,512]{1,0:T(8,128)(2,1)S(1)} %get-tuple-element.54.mine.after), channel_id=1, source_target_pairs={{0,1},{1,0},{2,3},{3,2},{4,5},{5,4},{6,7},{7,6},{8,9},{9,8},{10,11... | collective-permute-start | bytes 393224 | tf_op jit(solution)/shard_map/ppermute | solution.py:145
  53.5 6.1 %collective-permute-start.18 = (bf16[128,512]{1,0:T(8,128)(2,1)S(1)}, bf16[128,512]{1,0:T(8,128)(2,1)S(1)}, u32[]{:S(2)}, u32[]{:S(2)}) collective-permute-start(bf16[128,512]{1,0:T(8,128)(2,1)S(1)} %get-tuple-element.67.mine), channel_id=1, source_target_pairs={{0,1},{1,0},{2,3},{3,2},{4,5},{5,4},{6,7},{7,6},{8,9},{9,8},{10,11... | collective-permute-start | bytes 393224 | tf_op jit(solution)/shard_map/ppermute | solution.py:145
  59.0 5.2 %collective-permute-start.14 = (bf16[128,512]{1,0:T(8,128)(2,1)S(1)}, bf16[128,512]{1,0:T(8,128)(2,1)S(1)}, u32[]{:S(2)}, u32[]{:S(2)}) collective-permute-start(bf16[128,512]{1,0:T(8,128)(2,1)S(1)} %get-tuple-element.59.refs_0_), channel_id=1, source_target_pairs={{0,1},{1,0},{2,3},{3,2},{4,5},{5,4},{6,7},{7,6},{8,9},{9,8},{10,11... | collective-permute-start | bytes 393224 | tf_op jit(solution)/shard_map/ppermute | solution.py:145
  62.6 5.0 %collective-permute-start.19 = (bf16[128,512]{1,0:T(8,128)(2,1)S(1)}, bf16[128,512]{1,0:T(8,128)(2,1)S(1)}, u32[]{:S(2)}, u32[]{:S(2)}) collective-permute-start(bf16[128,512]{1,0:T(8,128)(2,1)S(1)} %get-tuple-element.69), channel_id=1, source_target_pairs={{0,1},{1,0},{2,3},{3,2},{4,5},{5,4},{6,7},{7,6},{8,9},{9,8},{10,11... | collective-permute-start | bytes 393224 | tf_op jit(solution)/shard_map/ppermute | solution.py:145

commit v4 on v3

--- a/solution.py
+++ b/solution.py
@@ -127,7 +127,7 @@
     return (grad_query_states, grad_passage_states)
 
 
-query_bits, pass_bits = (4, 2), (8, 1)
+query_bits, pass_bits = (8, 1), (4, 2)
 
 
 def offsets(bits):
@@ -181,7 +181,7 @@
 def encode_kernel(
     tile, me, place, scale, xq, xp, w_in, w_out, owner, mask, served,
     send_q, send_p, own_q, own_p, pre_act, slots_out, served_out, scale_out, w_in_kept, w_out_kept,
-    states, total, owner_held, mask_held, served_held, sems,
+    states, hidden, total, owner_held, mask_held, served_held, sems,
 ):
     rows = xq.shape[0]
     tiles = w_in.shape[1] // tile
@@ -194,8 +194,12 @@
     ]
     for t in range(tiles):
         at = slice(t * tile, (t + 1) * tile)
-        copies.append(pltpu.make_async_copy(w_in.at[:, at], w_in_kept.at[:, at], sems.at[5 + 2 * t]))
-        copies.append(pltpu.make_async_copy(w_out.at[at, :], w_out_kept.at[at, :], sems.at[6 + 2 * t]))
+        copies.append(pltpu.make_async_copy(w_in.at[:, at], w_in_kept.at[:, at], sems.at[5 + t]))
+    for t in range(tiles):
+        at = slice(t * tile, (t + 1) * tile)
+        copies.append(
+            pltpu.make_async_copy(w_out.at[at, :], w_out_kept.at[at, :], sems.at[5 + tiles + t])
+        )
     for copy in copies:
         copy.start()
     for copy in copies[2:5]:
@@ -219,13 +223,15 @@
     copies[1].wait()
     for t in range(tiles):
         at = slice(t * tile, (t + 1) * tile)
-        copies[5 + 2 * t].wait()
+        copies[5 + t].wait()
         pre = jnp.dot(states[...], w_in_kept[:, at], preferred_element_type=f32)
         cdf = 0.5 * (1.0 + lax.erf(pre * root_half))
         pre_act[:, at] = pre
-        hidden = (pre * cdf).astype(bf16)
-        copies[6 + 2 * t].wait()
-        part = jnp.dot(hidden, w_out_kept[at, :], preferred_element_type=f32)
+        hidden[:, at] = (pre * cdf).astype(bf16)
+    for t in range(tiles):
+        at = slice(t * tile, (t + 1) * tile)
+        copies[5 + tiles + t].wait()
+        part = jnp.dot(hidden[:, at], w_out_kept[at, :], preferred_element_type=f32)
         if t == 0:
             total[...] = part
         else:
@@ -262,6 +268,7 @@
         ],
         scratch_shapes=[
             pltpu.VMEM((2 * rows, width), bf16),
+            pltpu.VMEM((2 * rows, hidden), bf16),
             pltpu.VMEM((2 * rows, width), f32),
             pltpu.VMEM(owner.T.shape, jnp.int32),
             pltpu.VMEM(mask.T.shape, jnp.int32),
@@ -284,16 +291,32 @@
     lax.fori_loop(0, pre_act.shape[0] // step, body, 0)
 
 
-def pack_kernel(own, other, numbers, out):
+def flip_kernel(weights, out):
+    rows, columns = weights.shape
+    size = 256
+    eye = eye_of(size).astype(bf16)
+    for i in range(0, rows, size):
+        for j in range(0, columns, size):
+            out[j : j + size, i : i + size] = lax.dot_general(
+                eye, weights[i : i + size, j : j + size], nt, preferred_element_type=f32
+            ).astype(bf16)
+
+
+def flip(weights, name):
+    return local(flip_kernel, name, [(weights.shape[::-1], bf16)], (weights,), 2)[0]
+
+
+def pack_kernel(own, other, numbers, *refs):
+    out = refs[-1]
     rows = own.shape[0]
     out[:rows, :] = (own[...] + other[...].astype(f32)).astype(bf16)
     out[rows:, :] = jnp.zeros((out.shape[0] - rows, out.shape[1]), bf16)
     out[rows:, : numbers.shape[1]] = numbers[...]
 
 
-def pack(own, other, numbers):
+def pack(own, other, numbers, *after):
     shape = (own.shape[0] + numbers.shape[0], own.shape[1])
-    return local(pack_kernel, "pack", [(shape, bf16)], (own, other, numbers))[0]
+    return local(pack_kernel, "pack", [(shape, bf16)], (own, other, numbers, *after))[0]
 
 
 def score_kernel(owners, rows, place, *refs):
@@ -418,8 +441,8 @@
 def spread_query_kernel(rows, coefs, pick, p_all, kept, sent):
     npass = len(pass_at)
     passages = p_all[...]
-    near = [b for b, at in enumerate(query_at) if not at & query_bits[0]]
-    far = [b for b, at in enumerate(query_at) if at & query_bits[0]]
+    near = [b for b, at in enumerate(query_at) if not at & query_bits[1]]
+    far = [b for b, at in enumerate(query_at) if at & query_bits[1]]
     for b in near + far:
         lanes = slice(b * rows, (b + 1) * rows)
         pieces = []
@@ -472,33 +495,22 @@
         values = jnp.dot(weights.astype(bf16), queries, preferred_element_type=f32)
         along = column_of(eye, dot * coefs[3 * npass + 1 : 3 * npass + 2, at])
         values = values - along * p_all[at, :].astype(f32)
-        if a < npass // 2:
-            kept[at, :] = values
+        if a == 0:
+            kept[...] = values
         else:
-            sent[a - npass // 2][...] = values.astype(bf16)
+            sent[a - 1][...] = values.astype(bf16)
 
 
 def spread_pass(scale, coefs, sums, pick, q_all, p_all, rows):
-    half, width = len(pass_at) // 2, q_all.shape[1]
+    block = (rows, q_all.shape[1])
     kept, *sent = local(
         functools.partial(spread_pass_kernel, rows),
         "spread_pass",
-        [((half * rows, width), f32)] + [((rows, width), bf16)] * half,
+        [(block, f32)] + [(block, bf16)] * (len(pass_at) - 1),
         (scale, coefs, sums, pick, q_all, p_all),
         3,
     )
     return kept, sent
-
-
-def fold_pass_kernel(own, first, second, kept, sent):
-    rows = kept.shape[0]
-    kept[...] = own[:rows, :] + first[...].astype(f32)
-    sent[...] = (own[rows:, :] + second[...].astype(f32)).astype(bf16)
-
-
-def fold_pass(own, first, second):
-    half = (own.shape[0] // 2, own.shape[1])
-    return local(fold_pass_kernel, "fold_pass", [(half, f32), (half, bf16)], (own, first, second))
 
 
 def fold_query_kernel(own, other, kept, sent):
@@ -511,10 +523,6 @@
 def fold_query(own, other):
     half = (own.shape[0] // 2, own.shape[1])
     return local(fold_query_kernel, "fold_query", [(half, f32), (half, bf16)], (own, other))
-
-
-def add_kernel(own, other, out):
-    out[...] = (own[...] + other[...].astype(f32)).astype(out.dtype)
 
 
 def grad_query_kernel(own, other, scale, sums, coefs, raw, raw_pass, grad, rounded):
@@ -533,11 +541,12 @@
     rounded[...] = values.astype(bf16)
 
 
-def grad_pass_kernel(own, other, coefs, after, grad, rounded):
+def grad_pass_kernel(own, first, second, third, coefs, after, grad, rounded):
     npass = len(pass_at)
     rows = own.shape[0]
     inv_norm = column_of(eye_of(rows), coefs[3 * npass + 1 : 3 * npass + 2, :rows])
-    values = inv_norm * (own[...] + other[...].astype(f32))
+    others = first[...].astype(f32) + second[...].astype(f32) + third[...].astype(f32)
+    values = inv_norm * (own[...] + others)
     grad[...] = values
     rounded[...] = values.astype(bf16)
 
@@ -554,11 +563,11 @@
     rounded = jnp.concatenate(
         [jnp.where(first, mine, theirs), jnp.where(first, theirs, mine)], axis=1
     )
-    for t in range(w_in.shape[1] // tile):
+    for t in range(w_in.shape[0] // tile):
         at = slice(t * tile, (t + 1) * tile)
-        hidden = lax.dot_general(rounded, w_out[at, :], nt, preferred_element_type=f32)
+        hidden = jnp.dot(rounded, w_out[:, at], preferred_element_type=f32)
         grad_pre = (hidden * slope[tower * rows : (tower + 1) * rows, at].astype(f32)).astype(bf16)
-        part = lax.dot_general(grad_pre, w_in[:, at], nt, preferred_element_type=f32)
+        part = jnp.dot(grad_pre, w_in[at, :], preferred_element_type=f32)
         if t == 0:
             total[...] = part
         else:
@@ -569,27 +578,33 @@
 
 
 def decode_one(me, grad, rounded, slope, tower, w_in, w_out, *after):
-    rows, width = grad.shape[0], w_in.shape[0]
+    hidden, width = w_in.shape
     return local(
-        functools.partial(decode_kernel, tower, min(512, w_in.shape[1])),
+        functools.partial(decode_kernel, tower, min(512, hidden)),
         "decode_one",
         [(grad.shape, bf16), (grad.shape, f32)],
         (grad, rounded, swap(rounded, "mp", 1), slope, w_in, w_out, *after),
         3,
-        [pltpu.VMEM((rows, width), f32)],
+        [pltpu.VMEM((grad.shape[0], width), f32)],
         [me],
     )
 
 
-def finish(own, other, name):
+def finish_kernel(own, other, *refs):
+    out, done = refs[-2:]
+    out[...] = (own[...] + other[...].astype(f32)).astype(bf16)
+    done[...] = jnp.zeros_like(done)
+
+
+def finish(own, other, name, *after):
     return pl.pallas_call(
-        add_kernel,
-        in_specs=[vmem] * 2,
-        out_specs=vmem,
-        out_shape=jax.ShapeDtypeStruct(own.shape, bf16),
+        finish_kernel,
+        in_specs=[vmem] * (2 + len(after)),
+        out_specs=[vmem] * 2,
+        out_shape=[jax.ShapeDtypeStruct(own.shape, bf16), pltpu.VMEM((8, 128), f32)],
         compiler_params=pltpu.CompilerParams(vmem_limit_bytes=1 << 20),
         name=name,
-    )(*[pltpu.with_memory_space_constraint(x, pltpu.VMEM) for x in (own, other)])
+    )(*[pltpu.with_memory_space_constraint(x, pltpu.VMEM) for x in (own, other, *after)])
 
 
 def paired_shards(
@@ -603,7 +618,8 @@
         me, place, loss_scale.reshape(1), query_states, passage_states, w_in, w_out, neg_owner, neg_mask, served_rows
     )
     slope = local(slope_kernel, "slope", [(pre_act.shape, bf16)], (pre_act,))[0]
-    raw_q = pack(own_q, swap(send_q, "mp", 1), slots)
+    w_in, w_out = flip(w_in, "flip_in"), flip(w_out, "flip_out")
+    raw_q = pack(own_q, swap(send_q, "mp", 1), slots, slope, w_in, w_out)
     raw_p = pack(own_p, swap(send_p, "mp", 1), served)
     p_blocks = gather_blocks(raw_p, pass_bits)
     q_blocks = gather_blocks(raw_q, query_bits)
@@ -612,28 +628,27 @@
     coefs, sums = weigh(table, swap(table, "mp", 1), valid, rows)
     kept_q, sent_q = spread_query(coefs, pick, p_all, rows)
     sums = exchange_sums(sums, query_bits[1], sent_q)
-    sums = exchange_sums(sums, query_bits[0])
+    kept_q, sent_q = fold_query(kept_q, swap(sent_q, "dp", query_bits[1]))
+    sums = exchange_sums(sums, query_bits[0], sent_q)
     kept_p, sent_p = spread_pass(scale, coefs, sums, pick, q_all, p_all, rows)
-    kept_p, sent_p = fold_pass(kept_p, *[swap(x, "dp", pass_bits[1]) for x in sent_p])
-    kept_q, sent_q = fold_query(kept_q, swap(sent_q, "dp", query_bits[0]))
+    others_p = [swap(x, "dp", at) for x, at in zip(sent_p, pass_at[1:])]
     grad_q, round_q = grad_out(
         grad_query_kernel,
         "grad_query",
         kept_q,
-        (swap(sent_q, "dp", query_bits[1]), scale, sums, coefs, raw_q, raw_p),
+        (swap(sent_q, "dp", query_bits[0]), scale, sums, coefs, raw_q, raw_p),
     )
     grad_p, round_p = grad_out(
         grad_pass_kernel,
         "grad_pass",
         kept_p,
-        (swap(sent_p, "dp", pass_bits[0]), coefs, round_q),
+        (*others_p, coefs, round_q),
     )
     send_q, own_q = decode_one(me, grad_q, round_q, slope, 0, w_in, w_out)
     send_p, own_p = decode_one(me, grad_p, round_p, slope, 1, w_in, w_out, send_q)
-    return (
-        finish(own_q, swap(send_q, "mp", 1), "out_query"),
-        finish(own_p, swap(send_p, "mp", 1), "out_pass"),
-    )
+    out_q, done_q = finish(own_q, swap(send_q, "mp", 1), "out_query")
+    out_p, _ = finish(own_p, swap(send_p, "mp", 1), "out_pass", done_q)
+    return (out_q, out_p)
 
 
 def solution(mesh):

time: 68.4 us -> 65 us (0.950); the launches traced: 68.3 us -> 64.1 us
  waiting for transfers between devices: 24.4 us -> 19.8 us
    ppermute x20, waiting for transfers between devices: 24.4 us -> 19.8 us  [swap(): return lax.ppermute(values, axis, [(i, i ^ bit) for i in range(size)])]
    pallas_call x15 -> x16, Pallas kernels: 9.64 us -> 9.61 us  [local(): pl.pallas_call(kernel, in_specs=[smem] * len(scalars) + [vmem] * len(oper...]
  transfers between devices with their start and end apart: 20 -> 20, of which waited for: 9 -> 13; matrix products, arithmetic and copies ran while one was open for 0% -> 0% of each run, Pallas kernels for 13% -> 13%
where the time goes in v4:
time: 65 us; the launch traced here: 64.1 us
  starting transfers between devices  26.9 us (41%)
  waiting for transfers between devices  19.8 us (30%)
  Pallas kernels  16 us (25%)
  between operations  1.41 us (2%)
    ppermute x20, starting transfers between devices, swap(): return lax.ppermute(values, axis, [(i, i ^ bit) for i in range(size)])  26.9 us
    ppermute x20, waiting for transfers between devices, swap(): return lax.ppermute(values, axis, [(i, i ^ bit) for i in range(size)])  19.8 us
    pallas_call x16, Pallas kernels, local(): pl.pallas_call(kernel, in_specs=[smem] * len(scalars) + [vmem] * len(oper...  9.61 us
    pallas_call x1, Pallas kernels, encode_both(): pl.pallas_call(functools.partial(encode_kernel, tile), in_specs=[smem] *...  5.05 us
    pallas_call x2, Pallas kernels, finish(): pl.pallas_call(finish_kernel, in_specs=[vmem] * (2 + len(after)), out_spe...  1.36 us
  transfers between devices with their start and end apart: 20, of which 13 were waited for; matrix products, arithmetic and copies ran while one was open for 0% of the time, Pallas kernels for 13%

profile of v4, /device:TPU:0, one launch (start us, length us, event | category | flops | bytes accessed | tf_op | source)
XLA Modules:
  0.0 64.1 jit_solution(643335856644361067)
XLA Ops:
  1.3 5.1 %encode_both.1 = (bf16[128,512]{1,0:T(8,128)(2,1)S(1)}, bf16[128,512]{1,0:T(8,128)(2,1)S(1)}, f32[128,512]{1,0:T(8,128)S(1)}, f32[128,512]{1,0:T(8,128)S(1)}, f3...) custom-call(s32[1]{0:T(128)} %bitcast.me, ...), custom_call_target="tpu_custom_call" | custom-call | tf_op jit(solution)/shard_map/encode_both/pallas_call | solution.py:253
  6.3 3.0 %collective-permute-start = (bf16[128,512]{1,0:T(8,128)(2,1)S(1)}, bf16[128,512]{1,0:T(8,128)(2,1)S(1)}, u32[]{:S(2)}, u32[]{:S(2)}) collective-permute-start(bf16[128,512]{1,0:T(8,128)(2,1)S(1)} %get-tuple-element.39), channel_id=1, source_target_pairs={{0,1},{1,0},{2,3},{3,2},{4,5},{5,4},{6,7},{7,6},{8,9},{9,8},{10,11... | collective-permute-start | bytes 393224 | tf_op jit(solution)/shard_map/ppermute | solution.py:145
  9.4 0.1 collective-permute-start.4
  9.5 0.8 %slope.1.refs_0_ = bf16[256,2048]{1,0:T(8,128)(2,1)S(1)} custom-call(f32[256,2048]{1,0:T(8,128)S(1)} %get-tuple-element.41.pre_act), custom_call_target="tpu_custom_call" | custom-call | flops 1 | bytes 1 | tf_op jit(solution)/shard_map/slope/pallas_call | solution.py:169
  10.3 1.3 %flip_in.1.refs_1_.w_in = bf16[2048,1024]{1,0:T(8,128)(2,1)S(1)} custom-call(bf16[1024,2048]{1,0:T(8,128)(2,1)S(1)} %get-tuple-element.42.weights), custom_call_target="tpu_custom_call" | custom-call | flops 1 | bytes 1 | tf_op jit(solution)/shard_map/flip_in/pallas_call | solution.py:169
  11.6 1.3 %flip_out.1.refs_2_.w_out = bf16[1024,2048]{1,0:T(8,128)(2,1)S(1)} custom-call(bf16[2048,1024]{1,0:T(8,128)(2,1)S(1)} %get-tuple-element.43.weights), custom_call_target="tpu_custom_call" | custom-call | flops 1 | bytes 1 | tf_op jit(solution)/shard_map/flip_out/pallas_call | solution.py:169
  12.9 0.8 %collective-permute-done.other = bf16[128,512]{1,0:T(8,128)(2,1)S(1)} collective-permute-done((bf16[128,512]{1,0:T(8,128)(2,1)S(1)}, bf16[128,512]{1,0:T(8,128)(2,1)S(1)}, u32[]{:S(2)}, u32[]{:S(2)}) %collective-permute-start) | collective-permute-done | bytes 131104 | tf_op jit(solution)/shard_map/ppermute | solution.py:145
  13.7 3.2 %collective-permute-start.1 = (bf16[144,512]{1,0:T(8,128)(2,1)S(1)}, bf16[144,512]{1,0:T(8,128)(2,1)S(1)}, u32[]{:S(2)}, u32[]{:S(2)}) collective-permute-start(bf16[144,512]{1,0:T(8,128)(2,1)S(1)} %pack.2.refs_0_.raw), channel_id=1, source_target_pairs={{0,16},{2,18},{4,20},{6,22},{8,24},{10,26},{12,28},{14,30},{16,0},... | collective-permute-start | bytes 442376 | tf_op jit(solution)/shard_map/ppermute | solution.py:145
  16.9 0.0 collective-permute-done.4.other
  17.0 1.6 %collective-permute-start.5 = (bf16[144,512]{1,0:T(8,128)(2,1)S(1)}, bf16[144,512]{1,0:T(8,128)(2,1)S(1)}, u32[]{:S(2)}, u32[]{:S(2)}) collective-permute-start(bf16[144,512]{1,0:T(8,128)(2,1)S(1)} %pack.3.refs_4_.raw_pass), channel_id=1, source_target_pairs={{0,8},{2,10},{4,12},{6,14},{8,0},{10,2},{12,4},{14,6},{16,24},{18,... | collective-permute-start | bytes 442376 | tf_op jit(solution)/shard_map/ppermute | solution.py:145
  18.6 0.0 collective-permute-start.2
  18.6 1.5 %collective-permute-start.6 = (bf16[144,512]{1,0:T(8,128)(2,1)S(1)}, bf16[144,512]{1,0:T(8,128)(2,1)S(1)}, u32[]{:S(2)}, u32[]{:S(2)}) collective-permute-start(bf16[144,512]{1,0:T(8,128)(2,1)S(1)} %pack.3.refs_4_.raw_pass), channel_id=1, source_target_pairs={{0,4},{2,6},{4,0},{6,2},{8,12},{10,14},{12,8},{14,10},{16,20},{18,... | collective-permute-start | bytes 442376 | tf_op jit(solution)/shard_map/ppermute | solution.py:145
  20.1 1.9 %collective-permute-done.1.refs_1_ = bf16[144,512]{1,0:T(8,128)(2,1)S(1)} collective-permute-done((bf16[144,512]{1,0:T(8,128)(2,1)S(1)}, bf16[144,512]{1,0:T(8,128)(2,1)S(1)}, u32[]{:S(2)}, u32[]{:S(2)}) %collective-permute-start.1) | collective-permute-done | bytes 147488 | tf_op jit(solution)/shard_map/ppermute | solution.py:145
  22.1 0.0 collective-permute-start.3
  22.1 0.9 %collective-permute-done.5.refs_5_ = bf16[144,512]{1,0:T(8,128)(2,1)S(1)} collective-permute-done((bf16[144,512]{1,0:T(8,128)(2,1)S(1)}, bf16[144,512]{1,0:T(8,128)(2,1)S(1)}, u32[]{:S(2)}, u32[]{:S(2)}) %collective-permute-start.5) | collective-permute-done | bytes 147488 | tf_op jit(solution)/shard_map/ppermute | solution.py:145
  22.9 1.5 %collective-permute-start.7 = (bf16[144,512]{1,0:T(8,128)(2,1)S(1)}, bf16[144,512]{1,0:T(8,128)(2,1)S(1)}, u32[]{:S(2)}, u32[]{:S(2)}) collective-permute-start(bf16[144,512]{1,0:T(8,128)(2,1)S(1)} %collective-permute-done.5.refs_5_), channel_id=1, source_target_pairs={{0,4},{2,6},{4,0},{6,2},{8,12},{10,14},{12,8},{14,10},{16,20},{18,... | collective-permute-start | bytes 442376 | tf_op jit(solution)/shard_map/ppermute | solution.py:145
  24.5 0.0 collective-permute-done.2.refs_2_
  24.5 0.4 collective-permute-done.6.refs_6_
  24.9 0.0 collective-permute-done.3.refs_3_
  24.9 3.4 %collective-permute-done.7.refs_7_ = bf16[144,512]{1,0:T(8,128)(2,1)S(1)} collective-permute-done((bf16[144,512]{1,0:T(8,128)(2,1)S(1)}, bf16[144,512]{1,0:T(8,128)(2,1)S(1)}, u32[]{:S(2)}, u32[]{:S(2)}) %collective-permute-start.7) | collective-permute-done | bytes 147488 | tf_op jit(solution)/shard_map/ppermute | solution.py:145
  28.3 1.1 %score.1 = (f32[16,512]{1,0:T(8,128)S(1)}, f32[4,512]{1,0:T(4,128)S(1)}, bf16[512,512]{1,0:T(8,128)(2,1)S(1)}, bf16[512,512]{1,0:T(8,128)(2,1)S(1)}, bf16[512,512]{1,0:T(8,128)(2,1)S(1)}) custom-call(s32[1]{0:T(128)} %bitcast.1.place, bf16[144,512]{1,0:T(8,128)(2,1)S(1)} %pack.2.refs_0_.raw, bf16[144,512]{1,0:T(8,128)(2,1)S(1)} %collective-permute-done.1.refs_1_, ...), custom_call_target="tpu_custom_call" | custom-call | flops 1 | bytes 1 | tf_op jit(solution)/shard_map/score/pallas_call | solution.py:169
  29.5 1.6 %collective-permute-start.8 = (f32[16,512]{1,0:T(8,128)S(1)}, f32[16,512]{1,0:T(8,128)S(1)}, u32[]{:S(2)}, u32[]{:S(2)}) collective-permute-start(f32[16,512]{1,0:T(8,128)S(1)} %get-tuple-element.47.table), channel_id=1, source_target_pairs={{0,1},{1,0},{2,3},{3,2},{4,5},{5,4},{6,7},{7,6},{8,9},{9,8},{10,11... | collective-permute-start | bytes 98312 | tf_op jit(solution)/shard_map/ppermute | solution.py:145
  31.1 2.4 %collective-permute-done.8.other = f32[16,512]{1,0:T(8,128)S(1)} collective-permute-done((f32[16,512]{1,0:T(8,128)S(1)}, f32[16,512]{1,0:T(8,128)S(1)}, u32[]{:S(2)}, u32[]{:S(2)}) %collective-permute-start.8) | collective-permute-done | bytes 32800 | tf_op jit(solution)/shard_map/ppermute | solution.py:145
  33.5 0.5 spread_query.1
  34.0 0.1 collective-permute-start.9
  34.1 0.5 collective-permute-start.11
  34.6 1.0 %collective-permute-done.11.other = f32[16,128]{1,0:T(8,128)S(1)} collective-permute-done((f32[16,128]{1,0:T(8,128)S(1)}, f32[16,128]{1,0:T(8,128)S(1)}, u32[]{:S(2)}, u32[]{:S(2)}) %collective-permute-start.11) | collective-permute-done | bytes 8224 | tf_op jit(solution)/shard_map/ppermute | solution.py:145
  35.6 2.4 %collective-permute-start.12 = (f32[16,128]{1,0:T(8,128)S(1)}, f32[16,128]{1,0:T(8,128)S(1)}, u32[]{:S(2)}, u32[]{:S(2)}) collective-permute-start(f32[16,128]{1,0:T(8,128)S(1)} %add_sums.2.sums), channel_id=1, source_target_pairs={{0,16},{2,18},{4,20},{6,22},{8,24},{10,26},{12,28},{14,30},{16,0},... | collective-permute-start | bytes 24584 | tf_op jit(solution)/shard_map/ppermute | solution.py:145
  38.0 0.0 collective-permute-done.9.other
  38.0 0.7 %collective-permute-start.10 = (bf16[128,512]{1,0:T(8,128)(2,1)S(1)}, bf16[128,512]{1,0:T(8,128)(2,1)S(1)}, u32[]{:S(2)}, u32[]{:S(2)}) collective-permute-start(bf16[128,512]{1,0:T(8,128)(2,1)S(1)} %get-tuple-element.55.refs_0_), channel_id=1, source_target_pairs={{0,16},{2,18},{4,20},{6,22},{8,24},{10,26},{12,28},{14,30},{16,0},... | collective-permute-start | bytes 393224 | tf_op jit(solution)/shard_map/ppermute | solution.py:145
  38.7 1.5 %collective-permute-done.12.other = f32[16,128]{1,0:T(8,128)S(1)} collective-permute-done((f32[16,128]{1,0:T(8,128)S(1)}, f32[16,128]{1,0:T(8,128)S(1)}, u32[]{:S(2)}, u32[]{:S(2)}) %collective-permute-start.12) | collective-permute-done | bytes 8224 | tf_op jit(solution)/shard_map/ppermute | solution.py:145
  40.2 0.6 spread_pass.1
  40.9 2.0 %collective-permute-start.15 = (bf16[128,512]{1,0:T(8,128)(2,1)S(1)}, bf16[128,512]{1,0:T(8,128)(2,1)S(1)}, u32[]{:S(2)}, u32[]{:S(2)}) collective-permute-start(bf16[128,512]{1,0:T(8,128)(2,1)S(1)} %get-tuple-element.65), channel_id=1, source_target_pairs={{0,8},{2,10},{4,12},{6,14},{8,0},{10,2},{12,4},{14,6},{16,24},{18,... | collective-permute-start | bytes 393224 | tf_op jit(solution)/shard_map/ppermute | solution.py:145
  42.8 1.6 %collective-permute-start.16 = (bf16[128,512]{1,0:T(8,128)(2,1)S(1)}, bf16[128,512]{1,0:T(8,128)(2,1)S(1)}, u32[]{:S(2)}, u32[]{:S(2)}) collective-permute-start(bf16[128,512]{1,0:T(8,128)(2,1)S(1)} %get-tuple-element.66), channel_id=1, source_target_pairs={{0,4},{2,6},{4,0},{6,2},{8,12},{10,14},{12,8},{14,10},{16,20},{18,... | collective-permute-start | bytes 393224 | tf_op jit(solution)/shard_map/ppermute | solution.py:145
  44.4 0.0 collective-permute-start.17
  44.4 2.8 %collective-permute-done.10.other = bf16[128,512]{1,0:T(8,128)(2,1)S(1)} collective-permute-done((bf16[128,512]{1,0:T(8,128)(2,1)S(1)}, bf16[128,512]{1,0:T(8,128)(2,1)S(1)}, u32[]{:S(2)}, u32[]{:S(2)}) %collective-permute-start.10) | collective-permute-done | bytes 131104 | tf_op jit(solution)/shard_map/ppermute | solution.py:145
  47.3 0.2 grad_query.1
  47.4 1.6 %collective-permute-start.13 = (bf16[128,512]{1,0:T(8,128)(2,1)S(1)}, bf16[128,512]{1,0:T(8,128)(2,1)S(1)}, u32[]{:S(2)}, u32[]{:S(2)}) collective-permute-start(bf16[128,512]{1,0:T(8,128)(2,1)S(1)} %get-tuple-element.59.mine.after), channel_id=1, source_target_pairs={{0,1},{1,0},{2,3},{3,2},{4,5},{5,4},{6,7},{7,6},{8,9},{9,8},{10,11... | collective-permute-start | bytes 393224 | tf_op jit(solution)/shard_map/ppermute | solution.py:145
  49.0 0.0 collective-permute-done.15.first
  49.0 0.4 collective-permute-done.16.second
  49.4 1.5 %collective-permute-done.17.third = bf16[128,512]{1,0:T(8,128)(2,1)S(1)} collective-permute-done((bf16[128,512]{1,0:T(8,128)(2,1)S(1)}, bf16[128,512]{1,0:T(8,128)(2,1)S(1)}, u32[]{:S(2)}, u32[]{:S(2)}) %collective-permute-start.17) | collective-permute-done | bytes 131104 | tf_op jit(solution)/shard_map/ppermute | solution.py:145
  50.9 0.1 grad_pass.1
  51.0 1.5 %collective-permute-start.18 = (bf16[128,512]{1,0:T(8,128)(2,1)S(1)}, bf16[128,512]{1,0:T(8,128)(2,1)S(1)}, u32[]{:S(2)}, u32[]{:S(2)}) collective-permute-start(bf16[128,512]{1,0:T(8,128)(2,1)S(1)} %get-tuple-element.69.mine), channel_id=1, source_target_pairs={{0,1},{1,0},{2,3},{3,2},{4,5},{5,4},{6,7},{7,6},{8,9},{9,8},{10,11... | collective-permute-start | bytes 393224 | tf_op jit(solution)/shard_map/ppermute | solution.py:145
  52.5 0.0 collective-permute-done.13.theirs
  52.5 1.7 %decode_one.2 = (bf16[128,512]{1,0:T(8,128)(2,1)S(1)}, f32[128,512]{1,0:T(8,128)S(1)}) custom-call(s32[1]{0:T(128)} %bitcast.me, f32[128,512]{1,0:T(8,128)S(1)} %get-tuple-element.58.grad, bf16[128,512]{1,0:T(8,128)(2,1)S(1)} %get-tuple-element.59.mine.after, bf16[128,512]{1,0:T(8,128)(2,1)S(1)} %collective-permute-done.13.theirs, ...), custom_call_target="tpu_custom_call" | custom-call | flops 1 | bytes 1 | tf_op jit(solution)/shard_map/decode_one/pallas_call | solution.py:169
  54.3 1.5 %collective-permute-start.14 = (bf16[128,512]{1,0:T(8,128)(2,1)S(1)}, bf16[128,512]{1,0:T(8,128)(2,1)S(1)}, u32[]{:S(2)}, u32[]{:S(2)}) collective-permute-start(bf16[128,512]{1,0:T(8,128)(2,1)S(1)} %get-tuple-element.61.refs_0_), channel_id=1, source_target_pairs={{0,1},{1,0},{2,3},{3,2},{4,5},{5,4},{6,7},{7,6},{8,9},{9,8},{10,11... | collective-permute-start | bytes 393224 | tf_op jit(solution)/shard_map/ppermute | solution.py:145
  55.8 0.3 collective-permute-done.18.theirs
  56.1 1.8 %decode_one.3 = (bf16[128,512]{1,0:T(8,128)(2,1)S(1)}, f32[128,512]{1,0:T(8,128)S(1)}) custom-call(s32[1]{0:T(128)} %bitcast.me, f32[128,512]{1,0:T(8,128)S(1)} %get-tuple-element.68.grad, bf16[128,512]{1,0:T(8,128)(2,1)S(1)} %get-tuple-element.69.mine, bf16[128,512]{1,0:T(8,128)(2,1)S(1)} %collective-permute-done.18.theirs, ...), custom_call_target="tpu_custom_call" | custom-call | flops 1 | bytes 1 | tf_op jit(solution)/shard_map/decode_one/pallas_call | solution.py:169
  57.9 2.5 %collective-permute-start.19 = (bf16[128,512]{1,0:T(8,128)(2,1)S(1)}, bf16[128,512]{1,0:T(8,128)(2,1)S(1)}, u32[]{:S(2)}, u32[]{:S(2)}) collective-permute-start(bf16[128,512]{1,0:T(8,128)(2,1)S(1)} %get-tuple-element.71), channel_id=1, source_target_pairs={{0,1},{1,0},{2,3},{3,2},{4,5},{5,4},{6,7},{7,6},{8,9},{9,8},{10,11... | collective-permute-start | bytes 393224 | tf_op jit(solution)/shard_map/ppermute | solution.py:145
  60.4 0.0 collective-permute-done.14.other
  60.4 0.7 %out_query.1 = (bf16[128,512]{1,0:T(8,128)(2,1)}, f32[8,128]{1,0:T(8,128)S(1)}) custom-call(f32[128,512]{1,0:T(8,128)S(1)} %get-tuple-element.60.own, bf16[128,512]{1,0:T(8,128)(2,1)S(1)} %collective-permute-done.14.other), custom_call_target="tpu_custom_call" | custom-call | tf_op jit(solution)/shard_map/out_query/pallas_call | solution.py:600
  61.1 2.3 %collective-permute-done.19.other = bf16[128,512]{1,0:T(8,128)(2,1)S(1)} collective-permute-done((bf16[128,512]{1,0:T(8,128)(2,1)S(1)}, bf16[128,512]{1,0:T(8,128)(2,1)S(1)}, u32[]{:S(2)}, u32[]{:S(2)}) %collective-permute-start.19) | collective-permute-done | bytes 131104 | tf_op jit(solution)/shard_map/ppermute | solution.py:145
  63.4 0.7 %out_pass.1 = (bf16[128,512]{1,0:T(8,128)(2,1)}, f32[8,128]{1,0:T(8,128)}) custom-call(f32[128,512]{1,0:T(8,128)S(1)} %get-tuple-element.70.own, bf16[128,512]{1,0:T(8,128)(2,1)S(1)} %collective-permute-done.19.other, f32[8,128]{1,0:T(8,128)S(1)} %get-tuple-element.72.refs_0_), custom_call_target="tpu_custom_call" | custom-call | tf_op jit(solution)/shard_map/out_pass/pallas_call | solution.py:600
  (6 shorter events, 0.2 us)
Async XLA Ops:
  6.3 7.4 %collective-permute-start = (bf16[128,512]{1,0:T(8,128)(2,1)S(1)}, bf16[128,512]{1,0:T(8,128)(2,1)S(1)}, u32[]{:S(2)}, u32[]{:S(2)}) collective-permute-start(bf16[128,512]{1,0:T(8,128)(2,1)S(1)} %get-tuple-element.39), channel_id=1, source_target_pairs={{0,1},{1,0},{2,3},{3,2},{4,5},{5,4},{6,7},{7,6},{8,9},{9,8},{10,11... | collective-permute-start | bytes 393224 | tf_op jit(solution)/shard_map/ppermute | solution.py:145
  9.4 7.6 %collective-permute-start.4 = (bf16[128,512]{1,0:T(8,128)(2,1)S(1)}, bf16[128,512]{1,0:T(8,128)(2,1)S(1)}, u32[]{:S(2)}, u32[]{:S(2)}) collective-permute-start(bf16[128,512]{1,0:T(8,128)(2,1)S(1)} %get-tuple-element.45), channel_id=1, source_target_pairs={{0,1},{1,0},{2,3},{3,2},{4,5},{5,4},{6,7},{7,6},{8,9},{9,8},{10,11... | collective-permute-start | bytes 393224 | tf_op jit(solution)/shard_map/ppermute | solution.py:145
  13.7 8.3 %collective-permute-start.1 = (bf16[144,512]{1,0:T(8,128)(2,1)S(1)}, bf16[144,512]{1,0:T(8,128)(2,1)S(1)}, u32[]{:S(2)}, u32[]{:S(2)}) collective-permute-start(bf16[144,512]{1,0:T(8,128)(2,1)S(1)} %pack.2.refs_0_.raw), channel_id=1, source_target_pairs={{0,16},{2,18},{4,20},{6,22},{8,24},{10,26},{12,28},{14,30},{16,0},... | collective-permute-start | bytes 442376 | tf_op jit(solution)/shard_map/ppermute | solution.py:145
  17.0 6.0 %collective-permute-start.5 = (bf16[144,512]{1,0:T(8,128)(2,1)S(1)}, bf16[144,512]{1,0:T(8,128)(2,1)S(1)}, u32[]{:S(2)}, u32[]{:S(2)}) collective-permute-start(bf16[144,512]{1,0:T(8,128)(2,1)S(1)} %pack.3.refs_4_.raw_pass), channel_id=1, source_target_pairs={{0,8},{2,10},{4,12},{6,14},{8,0},{10,2},{12,4},{14,6},{16,24},{18,... | collective-permute-start | bytes 442376 | tf_op jit(solution)/shard_map/ppermute | solution.py:145
  18.6 5.8 %collective-permute-start.2 = (bf16[144,512]{1,0:T(8,128)(2,1)S(1)}, bf16[144,512]{1,0:T(8,128)(2,1)S(1)}, u32[]{:S(2)}, u32[]{:S(2)}) collective-permute-start(bf16[144,512]{1,0:T(8,128)(2,1)S(1)} %pack.2.refs_0_.raw), channel_id=1, source_target_pairs={{0,2},{2,0},{4,6},{6,4},{8,10},{10,8},{12,14},{14,12},{16,18},{18,... | collective-permute-start | bytes 442376 | tf_op jit(solution)/shard_map/ppermute | solution.py:145
  18.6 6.3 %collective-permute-start.6 = (bf16[144,512]{1,0:T(8,128)(2,1)S(1)}, bf16[144,512]{1,0:T(8,128)(2,1)S(1)}, u32[]{:S(2)}, u32[]{:S(2)}) collective-permute-start(bf16[144,512]{1,0:T(8,128)(2,1)S(1)} %pack.3.refs_4_.raw_pass), channel_id=1, source_target_pairs={{0,4},{2,6},{4,0},{6,2},{8,12},{10,14},{12,8},{14,10},{16,20},{18,... | collective-permute-start | bytes 442376 | tf_op jit(solution)/shard_map/ppermute | solution.py:145
  22.1 2.8 %collective-permute-start.3 = (bf16[144,512]{1,0:T(8,128)(2,1)S(1)}, bf16[144,512]{1,0:T(8,128)(2,1)S(1)}, u32[]{:S(2)}, u32[]{:S(2)}) collective-permute-start(bf16[144,512]{1,0:T(8,128)(2,1)S(1)} %collective-permute-done.1.refs_1_), channel_id=1, source_target_pairs={{0,2},{2,0},{4,6},{6,4},{8,10},{10,8},{12,14},{14,12},{16,18},{18,... | collective-permute-start | bytes 442376 | tf_op jit(solution)/shard_map/ppermute | solution.py:145
  22.9 5.4 %collective-permute-start.7 = (bf16[144,512]{1,0:T(8,128)(2,1)S(1)}, bf16[144,512]{1,0:T(8,128)(2,1)S(1)}, u32[]{:S(2)}, u32[]{:S(2)}) collective-permute-start(bf16[144,512]{1,0:T(8,128)(2,1)S(1)} %collective-permute-done.5.refs_5_), channel_id=1, source_target_pairs={{0,4},{2,6},{4,0},{6,2},{8,12},{10,14},{12,8},{14,10},{16,20},{18,... | collective-permute-start | bytes 442376 | tf_op jit(solution)/shard_map/ppermute | solution.py:145
  29.5 4.0 %collective-permute-start.8 = (f32[16,512]{1,0:T(8,128)S(1)}, f32[16,512]{1,0:T(8,128)S(1)}, u32[]{:S(2)}, u32[]{:S(2)}) collective-permute-start(f32[16,512]{1,0:T(8,128)S(1)} %get-tuple-element.47.table), channel_id=1, source_target_pairs={{0,1},{1,0},{2,3},{3,2},{4,5},{5,4},{6,7},{7,6},{8,9},{9,8},{10,11... | collective-permute-start | bytes 98312 | tf_op jit(solution)/shard_map/ppermute | solution.py:145
  34.0 4.0 %collective-permute-start.9 = (bf16[256,512]{1,0:T(8,128)(2,1)S(1)}, bf16[256,512]{1,0:T(8,128)(2,1)S(1)}, u32[]{:S(2)}, u32[]{:S(2)}) collective-permute-start(bf16[256,512]{1,0:T(8,128)(2,1)S(1)} %get-tuple-element.53.refs_0_), channel_id=1, source_target_pairs={{0,2},{2,0},{4,6},{6,4},{8,10},{10,8},{12,14},{14,12},{16,18},{18,... | collective-permute-start | bytes 786440 | tf_op jit(solution)/shard_map/ppermute | solution.py:145
  34.1 1.5 %collective-permute-start.11 = (f32[16,128]{1,0:T(8,128)S(1)}, f32[16,128]{1,0:T(8,128)S(1)}, u32[]{:S(2)}, u32[]{:S(2)}) collective-permute-start(f32[16,128]{1,0:T(8,128)S(1)} %get-tuple-element.57.sums), channel_id=1, source_target_pairs={{0,2},{2,0},{4,6},{6,4},{8,10},{10,8},{12,14},{14,12},{16,18},{18,... | collective-permute-start | bytes 24584 | tf_op jit(solution)/shard_map/ppermute | solution.py:145
  35.6 4.6 %collective-permute-start.12 = (f32[16,128]{1,0:T(8,128)S(1)}, f32[16,128]{1,0:T(8,128)S(1)}, u32[]{:S(2)}, u32[]{:S(2)}) collective-permute-start(f32[16,128]{1,0:T(8,128)S(1)} %add_sums.2.sums), channel_id=1, source_target_pairs={{0,16},{2,18},{4,20},{6,22},{8,24},{10,26},{12,28},{14,30},{16,0},... | collective-permute-start | bytes 24584 | tf_op jit(solution)/shard_map/ppermute | solution.py:145
  38.0 9.2 %collective-permute-start.10 = (bf16[128,512]{1,0:T(8,128)(2,1)S(1)}, bf16[128,512]{1,0:T(8,128)(2,1)S(1)}, u32[]{:S(2)}, u32[]{:S(2)}) collective-permute-start(bf16[128,512]{1,0:T(8,128)(2,1)S(1)} %get-tuple-element.55.refs_0_), channel_id=1, source_target_pairs={{0,16},{2,18},{4,20},{6,22},{8,24},{10,26},{12,28},{14,30},{16,0},... | collective-permute-start | bytes 393224 | tf_op jit(solution)/shard_map/ppermute | solution.py:145
  40.9 8.1 %collective-permute-start.15 = (bf16[128,512]{1,0:T(8,128)(2,1)S(1)}, bf16[128,512]{1,0:T(8,128)(2,1)S(1)}, u32[]{:S(2)}, u32[]{:S(2)}) collective-permute-start(bf16[128,512]{1,0:T(8,128)(2,1)S(1)} %get-tuple-element.65), channel_id=1, source_target_pairs={{0,8},{2,10},{4,12},{6,14},{8,0},{10,2},{12,4},{14,6},{16,24},{18,... | collective-permute-start | bytes 393224 | tf_op jit(solution)/shard_map/ppermute | solution.py:145
  42.8 6.5 %collective-permute-start.16 = (bf16[128,512]{1,0:T(8,128)(2,1)S(1)}, bf16[128,512]{1,0:T(8,128)(2,1)S(1)}, u32[]{:S(2)}, u32[]{:S(2)}) collective-permute-start(bf16[128,512]{1,0:T(8,128)(2,1)S(1)} %get-tuple-element.66), channel_id=1, source_target_pairs={{0,4},{2,6},{4,0},{6,2},{8,12},{10,14},{12,8},{14,10},{16,20},{18,... | collective-permute-start | bytes 393224 | tf_op jit(solution)/shard_map/ppermute | solution.py:145
  44.4 6.5 %collective-permute-start.17 = (bf16[128,512]{1,0:T(8,128)(2,1)S(1)}, bf16[128,512]{1,0:T(8,128)(2,1)S(1)}, u32[]{:S(2)}, u32[]{:S(2)}) collective-permute-start(bf16[128,512]{1,0:T(8,128)(2,1)S(1)} %get-tuple-element.67), channel_id=1, source_target_pairs={{0,12},{2,14},{4,8},{6,10},{8,4},{10,6},{12,0},{14,2},{16,28},{18,... | collective-permute-start | bytes 393224 | tf_op jit(solution)/shard_map/ppermute | solution.py:145
  47.4 5.1 %collective-permute-start.13 = (bf16[128,512]{1,0:T(8,128)(2,1)S(1)}, bf16[128,512]{1,0:T(8,128)(2,1)S(1)}, u32[]{:S(2)}, u32[]{:S(2)}) collective-permute-start(bf16[128,512]{1,0:T(8,128)(2,1)S(1)} %get-tuple-element.59.mine.after), channel_id=1, source_target_pairs={{0,1},{1,0},{2,3},{3,2},{4,5},{5,4},{6,7},{7,6},{8,9},{9,8},{10,11... | collective-permute-start | bytes 393224 | tf_op jit(solution)/shard_map/ppermute | solution.py:145
  51.0 5.1 %collective-permute-start.18 = (bf16[128,512]{1,0:T(8,128)(2,1)S(1)}, bf16[128,512]{1,0:T(8,128)(2,1)S(1)}, u32[]{:S(2)}, u32[]{:S(2)}) collective-permute-start(bf16[128,512]{1,0:T(8,128)(2,1)S(1)} %get-tuple-element.69.mine), channel_id=1, source_target_pairs={{0,1},{1,0},{2,3},{3,2},{4,5},{5,4},{6,7},{7,6},{8,9},{9,8},{10,11... | collective-permute-start | bytes 393224 | tf_op jit(solution)/shard_map/ppermute | solution.py:145
  54.3 6.1 %collective-permute-start.14 = (bf16[128,512]{1,0:T(8,128)(2,1)S(1)}, bf16[128,512]{1,0:T(8,128)(2,1)S(1)}, u32[]{:S(2)}, u32[]{:S(2)}) collective-permute-start(bf16[128,512]{1,0:T(8,128)(2,1)S(1)} %get-tuple-element.61.refs_0_), channel_id=1, source_target_pairs={{0,1},{1,0},{2,3},{3,2},{4,5},{5,4},{6,7},{7,6},{8,9},{9,8},{10,11... | collective-permute-start | bytes 393224 | tf_op jit(solution)/shard_map/ppermute | solution.py:145
  57.9 5.5 %collective-permute-start.19 = (bf16[128,512]{1,0:T(8,128)(2,1)S(1)}, bf16[128,512]{1,0:T(8,128)(2,1)S(1)}, u32[]{:S(2)}, u32[]{:S(2)}) collective-permute-start(bf16[128,512]{1,0:T(8,128)(2,1)S(1)} %get-tuple-element.71), channel_id=1, source_target_pairs={{0,1},{1,0},{2,3},{3,2},{4,5},{5,4},{6,7},{7,6},{8,9},{9,8},{10,11... | collective-permute-start | bytes 393224 | tf_op jit(solution)/shard_map/ppermute | solution.py:145

commit v5 on v4

--- a/solution.py
+++ b/solution.py
@@ -165,44 +165,122 @@
     ).astype(f32)
 
 
-def local(kernel, name, outs, operands, mebibytes=1, scratch=(), scalars=()):
+def local(kernel, name, outs, operands, mebibytes=1, scratch=(), scalars=(), aliases=None):
     return pl.pallas_call(
         kernel,
         in_specs=[smem] * len(scalars) + [vmem] * len(operands),
         out_specs=[vmem] * len(outs),
         out_shape=[pltpu.VMEM(shape, dtype) for shape, dtype in outs],
         scratch_shapes=list(scratch),
+        input_output_aliases=aliases or {},
         compiler_params=pltpu.CompilerParams(vmem_limit_bytes=mebibytes << 20),
         cost_estimate=pl.CostEstimate(flops=1, bytes_accessed=1, transcendentals=0),
         name=name,
     )(*scalars, *[pltpu.with_memory_space_constraint(x, pltpu.VMEM) for x in operands])
 
 
-def encode_kernel(
-    tile, me, place, scale, xq, xp, w_in, w_out, owner, mask, served,
-    send_q, send_p, own_q, own_p, pre_act, slots_out, served_out, scale_out, w_in_kept, w_out_kept,
-    states, hidden, total, owner_held, mask_held, served_held, sems,
+def encode_far_kernel(
+    tile, me, place, scale, xq, xp, w_in, w_out,
+    send_q, send_p, states, hidden, pre_act, scale_out, w_in_kept, w_out_far, total, sems,
 ):
     rows = xq.shape[0]
     tiles = w_in.shape[1] // tile
+    half = w_out_far.shape[1]
+    far = pl.ds(pl.multiple_of((1 - me[0]) * half, 128), half)
+    slices = [slice(t * tile, (t + 1) * tile) for t in range(tiles)]
     copies = [
         pltpu.make_async_copy(xq, states.at[:rows, :], sems.at[0]),
         pltpu.make_async_copy(xp, states.at[rows:, :], sems.at[1]),
-        pltpu.make_async_copy(owner, owner_held, sems.at[2]),
-        pltpu.make_async_copy(mask, mask_held, sems.at[3]),
-        pltpu.make_async_copy(served, served_held, sems.at[4]),
     ]
-    for t in range(tiles):
-        at = slice(t * tile, (t + 1) * tile)
-        copies.append(pltpu.make_async_copy(w_in.at[:, at], w_in_kept.at[:, at], sems.at[5 + t]))
-    for t in range(tiles):
-        at = slice(t * tile, (t + 1) * tile)
+    for t, at in enumerate(slices):
+        copies.append(pltpu.make_async_copy(w_in.at[:, at], w_in_kept.at[:, at], sems.at[2 + t]))
+    for t, at in enumerate(slices):
         copies.append(
-            pltpu.make_async_copy(w_out.at[at, :], w_out_kept.at[at, :], sems.at[5 + tiles + t])
+            pltpu.make_async_copy(w_out.at[at, far], w_out_far.at[at, :], sems.at[2 + tiles + t])
         )
     for copy in copies:
         copy.start()
-    for copy in copies[2:5]:
+    scale_out[...] = jnp.zeros_like(scale_out) + scale[0] * logit_scale
+
+    def up(t):
+        copies[2 + t].wait()
+        return jnp.dot(states[...], w_in_kept[:, slices[t]], preferred_element_type=f32)
+
+    def down(t):
+        copies[2 + tiles + t].wait()
+        return jnp.dot(hidden[:, slices[t]], w_out_far[slices[t], :], preferred_element_type=f32)
+
+    copies[0].wait()
+    copies[1].wait()
+    for t, at in enumerate(slices):
+        pre = up(t)
+        pre_act[:, at] = pre
+        cdf = 0.5 * (1.0 + lax.erf(pre * root_half))
+        hidden[:, at] = (pre * cdf).astype(bf16)
+    for t in range(tiles):
+        part = down(t)
+        if t == 0:
+            total[...] = part
+        elif t < tiles - 1:
+            total[...] += part
+        else:
+            part = total[...] + part
+    send_q[...] = part[:rows].astype(bf16)
+    send_p[...] = part[rows:].astype(bf16)
+
+
+def in_hbm(*values):
+    return [pltpu.with_memory_space_constraint(x, pltpu.HBM) for x in values]
+
+
+def encode_far(me, place, scale, xq, xp, w_in, w_out):
+    rows, width = xq.shape
+    hidden = w_in.shape[1]
+    tile = min(512, hidden)
+    half = (rows, width // 2)
+    return pl.pallas_call(
+        functools.partial(encode_far_kernel, tile),
+        in_specs=[smem] * 3 + [hbm] * 4,
+        out_specs=[vmem] * 8,
+        out_shape=[
+            pltpu.VMEM(half, bf16),
+            pltpu.VMEM(half, bf16),
+            pltpu.VMEM((2 * rows, width), bf16),
+            pltpu.VMEM((2 * rows, hidden), bf16),
+            pltpu.VMEM((2 * rows, hidden), f32),
+            pltpu.VMEM((8, rows), f32),
+            pltpu.VMEM(w_in.shape, bf16),
+            pltpu.VMEM((hidden, width // 2), bf16),
+        ],
+        scratch_shapes=[
+            pltpu.VMEM((2 * rows, width // 2), f32),
+            pltpu.SemaphoreType.DMA((2 + 2 * (hidden // tile),)),
+        ],
+        compiler_params=pltpu.CompilerParams(vmem_limit_bytes=8 << 20),
+        name="encode_far",
+    )(me, place, scale, *in_hbm(xq, xp, w_in, w_out))
+
+
+def encode_near_kernel(
+    tile, me, w_out, owner, mask, served, hidden, states,
+    own_q, own_p, w_out_near, slots_out, served_out, total, owner_held, mask_held, served_held, sems,
+):
+    rows, half = own_q.shape
+    tiles = hidden.shape[1] // tile
+    near = pl.ds(pl.multiple_of(me[0] * half, 128), half)
+    copies = []
+    for t in range(tiles):
+        at = slice(t * tile, (t + 1) * tile)
+        copies.append(pltpu.make_async_copy(w_out.at[at, near], w_out_near.at[at, :], sems.at[t]))
+    numbers = [
+        pltpu.make_async_copy(owner, owner_held, sems.at[tiles]),
+        pltpu.make_async_copy(mask, mask_held, sems.at[tiles + 1]),
+        pltpu.make_async_copy(served, served_held, sems.at[tiles + 2]),
+    ]
+    for copy in numbers + copies:
+        copy.start()
+    total[...] = halves(me[0] == 0, states[...].astype(f32))[0]
+    for copy in numbers:
         copy.wait()
     owners = slots_out.shape[0]
     down = lax.broadcasted_iota(jnp.int32, (owners, rows), 0)
@@ -218,66 +296,45 @@
     slot = jnp.dot(named.astype(bf16), earlier.astype(f32).astype(bf16), preferred_element_type=f32)
     slots_out[...] = jnp.where(live > 0.5, slot, -1.0).astype(bf16)
     served_out[...] = served_held[0].astype(f32).astype(bf16)
-    scale_out[...] = jnp.zeros_like(scale_out) + scale[0] * logit_scale
-    copies[0].wait()
-    copies[1].wait()
     for t in range(tiles):
         at = slice(t * tile, (t + 1) * tile)
-        copies[5 + t].wait()
-        pre = jnp.dot(states[...], w_in_kept[:, at], preferred_element_type=f32)
-        cdf = 0.5 * (1.0 + lax.erf(pre * root_half))
-        pre_act[:, at] = pre
-        hidden[:, at] = (pre * cdf).astype(bf16)
-    for t in range(tiles):
-        at = slice(t * tile, (t + 1) * tile)
-        copies[5 + tiles + t].wait()
-        part = jnp.dot(hidden[:, at], w_out_kept[at, :], preferred_element_type=f32)
-        if t == 0:
-            total[...] = part
-        else:
-            total[...] += part
-    first = me[0] == 0
-    for at, send, own in ((0, send_q, own_q), (rows, send_p, own_p)):
-        mine, theirs = halves(first, total[at : at + rows, :])
-        send[...] = theirs.astype(bf16)
-        own[...] = mine + halves(first, states[at : at + rows, :].astype(f32))[0]
-
-
-def encode_both(me, place, scale, xq, xp, w_in, w_out, owner, mask, served):
-    rows, width = xq.shape
-    hidden = w_in.shape[1]
-    tile = min(512, hidden)
+        copies[t].wait()
+        total[...] += jnp.dot(hidden[:, at], w_out_near[at, :], preferred_element_type=f32)
+    own_q[...] = total[:rows, :]
+    own_p[...] = total[rows:, :]
+
+
+def encode_near(me, w_out, owner, mask, served, hidden, states):
+    rows, width = states.shape[0] // 2, states.shape[1]
     owners = served.shape[1]
+    tile = min(512, hidden.shape[1])
     half = (rows, width // 2)
-    operands = (xq, xp, w_in, w_out, owner.T, mask.T, served)
     return pl.pallas_call(
-        functools.partial(encode_kernel, tile),
-        in_specs=[smem] * 3 + [hbm] * 7,
-        out_specs=[vmem] * 10,
+        functools.partial(encode_near_kernel, tile),
+        in_specs=[smem] + [hbm] * 4 + [vmem] * 2,
+        out_specs=[vmem] * 5,
         out_shape=[
-            pltpu.VMEM(half, bf16),
-            pltpu.VMEM(half, bf16),
             pltpu.VMEM(half, f32),
             pltpu.VMEM(half, f32),
-            pltpu.VMEM((2 * rows, hidden), f32),
+            pltpu.VMEM((w_out.shape[0], width // 2), bf16),
             pltpu.VMEM((owners, rows), bf16),
             pltpu.VMEM((owners, served.shape[2]), bf16),
-            pltpu.VMEM((8, rows), f32),
-            pltpu.VMEM(w_in.shape, bf16),
-            pltpu.VMEM(w_out.shape, bf16),
         ],
         scratch_shapes=[
-            pltpu.VMEM((2 * rows, width), bf16),
-            pltpu.VMEM((2 * rows, hidden), bf16),
-            pltpu.VMEM((2 * rows, width), f32),
+            pltpu.VMEM((2 * rows, width // 2), f32),
             pltpu.VMEM(owner.T.shape, jnp.int32),
             pltpu.VMEM(mask.T.shape, jnp.int32),
             pltpu.VMEM(served.shape, jnp.int32),
-            pltpu.SemaphoreType.DMA((5 + 2 * (hidden // tile),)),
+            pltpu.SemaphoreType.DMA((hidden.shape[1] // tile + 3,)),
         ],
-        compiler_params=pltpu.CompilerParams(vmem_limit_bytes=8 << 20),
-        name="encode_both",
-    )(me, place, scale, *[pltpu.with_memory_space_constraint(x, pltpu.HBM) for x in operands])
+        compiler_params=pltpu.CompilerParams(vmem_limit_bytes=3 << 20),
+        cost_estimate=pl.CostEstimate(flops=1, bytes_accessed=1, transcendentals=0),
+        name="encode_near",
+    )(
+        me,
+        *in_hbm(w_out, owner.T, mask.T, served),
+        *[pltpu.with_memory_space_constraint(x, pltpu.VMEM) for x in (hidden, states)],
+    )
 
 
 def slope_kernel(pre_act, slope):
@@ -306,6 +363,24 @@
     return local(flip_kernel, name, [(weights.shape[::-1], bf16)], (weights,), 2)[0]
 
 
+def flip_rows_kernel(far, me, weights, out):
+    half, columns = out.shape[1], out.shape[0]
+    size = 256
+    eye = eye_of(size).astype(bf16)
+    first = (1 - me[0] if far else me[0]) * half
+    for i in range(0, half, size):
+        rows = pl.ds(pl.multiple_of(first + i, size), size)
+        for j in range(0, columns, size):
+            out[j : j + size, i : i + size] = lax.dot_general(
+                eye, weights[rows, j : j + size], nt, preferred_element_type=f32
+            ).astype(bf16)
+
+
+def flip_rows(me, weights, far, name):
+    out = ((weights.shape[1], weights.shape[0] // 2), bf16)
+    return local(functools.partial(flip_rows_kernel, far), name, [out], (weights,), 2, scalars=[me])[0]
+
+
 def pack_kernel(own, other, numbers, *refs):
     out = refs[-1]
     rows = own.shape[0]
@@ -319,74 +394,95 @@
     return local(pack_kernel, "pack", [(shape, bf16)], (own, other, numbers, *after))[0]
 
 
-def score_kernel(owners, rows, place, *refs):
-    nq, npass = len(query_at), len(pass_at)
-    q_refs, p_refs = refs[:nq], refs[nq : nq + npass]
-    table, valid, pick, q_all, p_all, slots, served = refs[nq + npass :]
-    for n, ref in enumerate(q_refs):
-        q_all[n * rows : (n + 1) * rows, :] = ref[:rows, :]
-        slots[n * owners : (n + 1) * owners, :] = ref[rows:, :rows].astype(f32)
-    for n, ref in enumerate(p_refs):
-        p_all[n * rows : (n + 1) * rows, :] = ref[:rows, :]
-        served[n * owners : (n + 1) * owners, :] = ref[rows:, :rows].astype(f32)
-    table[...] = jnp.zeros_like(table)
+def score_block(a, owners, rows, place, ref, q_all, slots, table, valid, pick, p_all, served):
+    npass = len(pass_at)
+    p_all[a * rows : (a + 1) * rows, :] = ref[:rows, :]
+    served[...] = ref[rows:, :rows].astype(f32)
     eye = eye_of(rows)
     down = lax.broadcasted_iota(jnp.int32, (rows, rows), 0).astype(f32)
-    queries = q_all[...]
-    for b in range(nq):
-        block = q_all[b * rows : (b + 1) * rows, :].astype(f32)
+    part = ref[:rows, :]
+    block = part.astype(f32)
+    square = jnp.sum(block * block, axis=1, keepdims=True)
+    table[2 * npass + 2 : 2 * npass + 3, a * rows : (a + 1) * rows] = jnp.sum(
+        eye * square, axis=0, keepdims=True
+    )
+    scores = lax.dot_general(part, q_all[...], nt, preferred_element_type=f32)
+    if a == 0:
+        table[2 * npass + 1 : 2 * npass + 2, :rows] = jnp.sum(
+            eye * scores[:, :rows], axis=0, keepdims=True
+        )
+    for b, at in enumerate(query_at):
+        lanes = slice(b * rows, (b + 1) * rows)
+        row_of = served[pl.ds(place[0] ^ at, 1), :]
+        slot_of = slots[pl.ds(b * owners + (place[0] ^ pass_at[a]), 1), :]
+        by_slot = (down == row_of).astype(f32).astype(bf16)
+        by_query = (down == slot_of).astype(f32).astype(bf16)
+        chosen = jnp.dot(by_slot, by_query, preferred_element_type=f32)
+        table[a : a + 1, lanes] = jnp.sum(chosen * scores[:, lanes], axis=0, keepdims=True)
+        table[npass + a : npass + a + 1, lanes] = jnp.sum(chosen * square, axis=0, keepdims=True)
+        valid[a : a + 1, lanes] = (slot_of >= 0.0).astype(f32)
+        pick[a * rows : (a + 1) * rows, lanes] = chosen.astype(bf16)
+
+
+def score_early_kernel(owners, rows, place, *refs):
+    nq, npass = len(query_at), len(pass_at)
+    q_refs, p_refs = refs[:nq], refs[nq : nq + npass - 1]
+    table, valid, pick, p_all, q_all, slots = refs[-7:-1]
+    served = refs[-1]
+    table[...] = jnp.zeros_like(table)
+    for n, ref in enumerate(q_refs):
+        lanes = slice(n * rows, (n + 1) * rows)
+        q_all[lanes, :] = ref[:rows, :]
+        slots[n * owners : (n + 1) * owners, :] = ref[rows:, :rows].astype(f32)
+        block = ref[:rows, :].astype(f32)
         square = jnp.sum(block * block, axis=1, keepdims=True)
-        table[2 * npass : 2 * npass + 1, b * rows : (b + 1) * rows] = jnp.sum(
-            eye * square, axis=0, keepdims=True
+        table[2 * npass : 2 * npass + 1, lanes] = jnp.sum(
+            eye_of(rows) * square, axis=0, keepdims=True
         )
-    for a in range(npass):
-        part = p_all[a * rows : (a + 1) * rows, :]
-        block = part.astype(f32)
-        square = jnp.sum(block * block, axis=1, keepdims=True)
-        table[2 * npass + 2 : 2 * npass + 3, a * rows : (a + 1) * rows] = jnp.sum(
-            eye * square, axis=0, keepdims=True
-        )
-        scores = lax.dot_general(part, queries, nt, preferred_element_type=f32)
-        if a == 0:
-            table[2 * npass + 1 : 2 * npass + 2, :rows] = jnp.sum(
-                eye * scores[:, :rows], axis=0, keepdims=True
-            )
-        for b in range(nq):
-            lanes = slice(b * rows, (b + 1) * rows)
-            row_of = served[pl.ds(a * owners + (place[0] ^ query_at[b]), 1), :]
-            slot_of = slots[pl.ds(b * owners + (place[0] ^ pass_at[a]), 1), :]
-            by_slot = (down == row_of).astype(f32).astype(bf16)
-            by_query = (down == slot_of).astype(f32).astype(bf16)
-            chosen = jnp.dot(by_slot, by_query, preferred_element_type=f32)
-            table[a : a + 1, lanes] = jnp.sum(chosen * scores[:, lanes], axis=0, keepdims=True)
-            table[npass + a : npass + a + 1, lanes] = jnp.sum(
-                chosen * square, axis=0, keepdims=True
-            )
-            valid[a : a + 1, lanes] = (slot_of >= 0.0).astype(f32)
-            pick[a * rows : (a + 1) * rows, lanes] = chosen.astype(bf16)
-
-
-def score(place, q_blocks, p_blocks, rows, owners):
+    for a, ref in enumerate(p_refs):
+        score_block(a, owners, rows, place, ref, q_all, slots, table, valid, pick, p_all, served)
+
+
+def score_last_kernel(owners, rows, place, ref, q_all, slots, *refs):
+    table, valid, pick, p_all, served = refs[-5:]
+    last = len(pass_at) - 1
+    score_block(last, owners, rows, place, ref, q_all, slots, table, valid, pick, p_all, served)
+
+
+def score(place, q_blocks, p_blocks, rows, owners, *after):
     nq, npass = len(query_at), len(pass_at)
     width = q_blocks[0].shape[1]
-    return local(
-        functools.partial(score_kernel, owners, rows),
-        "score",
-        [
-            ((-(-(2 * npass + 3) // 8) * 8, nq * rows), f32),
-            ((npass, nq * rows), f32),
-            ((npass * rows, nq * rows), bf16),
-            ((nq * rows, width), bf16),
-            ((npass * rows, width), bf16),
-        ],
-        (*q_blocks, *p_blocks),
+    outs = [
+        ((-(-(2 * npass + 3) // 8) * 8, nq * rows), f32),
+        ((8, nq * rows), f32),
+        ((npass * rows, nq * rows), bf16),
+        ((npass * rows, width), bf16),
+    ]
+    scratch = [pltpu.VMEM((owners, rows), f32)]
+    *parts, q_all, slots = local(
+        functools.partial(score_early_kernel, owners, rows),
+        "score_early",
+        outs + [((nq * rows, width), bf16), ((nq * owners, rows), f32)],
+        (*q_blocks, *p_blocks[:-1], *after),
         3,
-        [pltpu.VMEM((nq * owners, rows), f32), pltpu.VMEM((npass * owners, rows), f32)],
+        scratch,
         [place],
     )
-
-
-def weigh_kernel(rows, table, other, valid, coefs, sums):
+    parts = local(
+        functools.partial(score_last_kernel, owners, rows),
+        "score_last",
+        outs,
+        (p_blocks[-1], q_all, slots, *parts),
+        3,
+        scratch,
+        [place],
+        {4 + n: n for n in range(len(parts))},
+    )
+    return (*parts, q_all)
+
+
+def weigh_kernel(rows, table, other, valid, *refs):
+    coefs, sums = refs[-2:]
     nq, npass = len(query_at), len(pass_at)
     full = table[...] + other[...]
     raw, square = full[:npass], full[npass : 2 * npass]
@@ -394,7 +490,7 @@
     inv_pass = lax.rsqrt(full[2 * npass + 2 : 2 * npass + 3] + norm_eps)
     inv_neg = lax.rsqrt(square + norm_eps)
     neg_score = raw * inv_q * inv_neg
-    exp_neg = valid[...] * jnp.exp(logit_scale * neg_score)
+    exp_neg = valid[:npass] * jnp.exp(logit_scale * neg_score)
     pos_score = full[2 * npass + 1 : 2 * npass + 2] * inv_q * inv_pass
     coefs[...] = jnp.zeros_like(coefs)
     coefs[:npass] = exp_neg
@@ -412,13 +508,13 @@
     sums[nq : nq + 1, :] = jnp.exp(logit_scale * pos_score[:, :rows])
 
 
-def weigh(table, other, valid, rows):
+def weigh(table, other, valid, rows, *after):
     nq, npass = len(query_at), len(pass_at)
     return local(
         functools.partial(weigh_kernel, rows),
         "weigh",
         [((-(-(3 * npass + 3) // 8) * 8, nq * rows), f32), ((-(-3 * nq // 8) * 8, rows), f32)],
-        (table, other, valid),
+        (table, other, valid, *after),
     )
 
 
@@ -438,12 +534,12 @@
     return local(kernel, "add_sums", [(sums.shape, f32)], (sums, swap(sums, "dp", bit), *after))[0]
 
 
-def spread_query_kernel(rows, coefs, pick, p_all, kept, sent):
+def spread_query_kernel(rows, far, coefs, pick, p_all, *refs):
+    out = refs[-1]
     npass = len(pass_at)
     passages = p_all[...]
-    near = [b for b, at in enumerate(query_at) if not at & query_bits[1]]
-    far = [b for b, at in enumerate(query_at) if at & query_bits[1]]
-    for b in near + far:
+    blocks = [b for b, at in enumerate(query_at) if bool(at & query_bits[1]) == far]
+    for n, b in enumerate(blocks):
         lanes = slice(b * rows, (b + 1) * rows)
         pieces = []
         for a in range(npass):
@@ -452,26 +548,25 @@
             pieces.append(piece.T.astype(bf16))
         weights = jnp.concatenate(pieces, axis=1)
         values = jnp.dot(weights, passages, preferred_element_type=f32)
-        out, at = (kept, near.index(b)) if b in near else (sent, far.index(b))
-        out[at * rows : (at + 1) * rows, :] = values.astype(out.dtype)
-
-
-def spread_query(coefs, pick, p_all, rows):
+        out[n * rows : (n + 1) * rows, :] = values.astype(out.dtype)
+
+
+def spread_query(coefs, pick, p_all, rows, far, *after):
     half = (len(query_at) // 2 * rows, p_all.shape[1])
     return local(
-        functools.partial(spread_query_kernel, rows),
+        functools.partial(spread_query_kernel, rows, far),
         "spread_query",
-        [(half, f32), (half, bf16)],
-        (coefs, pick, p_all),
+        [(half, bf16 if far else f32)],
+        (coefs, pick, p_all, *after),
         3,
-    )
+    )[0]
 
 
 def column_of(eye, row):
     return jnp.sum(eye * row, axis=1, keepdims=True)
 
 
-def spread_pass_kernel(rows, scale, coefs, sums, pick, q_all, p_all, kept, *sent):
+def spread_pass_kernel(rows, blocks, scale, coefs, sums, pick, q_all, p_all, *outs):
     nq, npass = len(query_at), len(pass_at)
     eye = eye_of(rows)
     share = scale[:nq] / (sums[:nq] + sums[nq : 2 * nq])
@@ -479,7 +574,7 @@
     share = jnp.concatenate([share[n : n + 1] for n in range(nq)], axis=1)
     scaled = share * coefs[3 * npass : 3 * npass + 1]
     queries = q_all[...]
-    for a in range(npass):
+    for out, a in zip(outs, blocks):
         at = slice(a * rows, (a + 1) * rows)
         chosen = pick[at, :]
         weights = chosen.astype(f32) * (coefs[a : a + 1] * scaled)
@@ -495,22 +590,18 @@
         values = jnp.dot(weights.astype(bf16), queries, preferred_element_type=f32)
         along = column_of(eye, dot * coefs[3 * npass + 1 : 3 * npass + 2, at])
         values = values - along * p_all[at, :].astype(f32)
-        if a == 0:
-            kept[...] = values
-        else:
-            sent[a - 1][...] = values.astype(bf16)
-
-
-def spread_pass(scale, coefs, sums, pick, q_all, p_all, rows):
+        out[...] = values.astype(out.dtype)
+
+
+def spread_pass(scale, coefs, sums, pick, q_all, p_all, rows, blocks, dtype):
     block = (rows, q_all.shape[1])
-    kept, *sent = local(
-        functools.partial(spread_pass_kernel, rows),
+    return local(
+        functools.partial(spread_pass_kernel, rows, blocks),
         "spread_pass",
-        [(block, f32)] + [(block, bf16)] * (len(pass_at) - 1),
+        [(block, dtype)] * len(blocks),
         (scale, coefs, sums, pick, q_all, p_all),
         3,
     )
-    return kept, sent
 
 
 def fold_query_kernel(own, other, kept, sent):
@@ -555,39 +646,49 @@
     return local(kernel, name, [(own.shape, f32), (own.shape, bf16)], (own, *operands))
 
 
-def decode_kernel(tower, tile, me, grad, mine, theirs, slope, w_in, w_out, *refs):
-    send, own, total = refs[-3:]
-    first = me[0] == 0
-    rows = grad.shape[0]
-    mine, theirs = mine[...], theirs[...]
-    rounded = jnp.concatenate(
-        [jnp.where(first, mine, theirs), jnp.where(first, theirs, mine)], axis=1
-    )
-    for t in range(w_in.shape[0] // tile):
+def decode_near_kernel(tile, mine, w_out, out):
+    for t in range(w_out.shape[1] // tile):
         at = slice(t * tile, (t + 1) * tile)
-        hidden = jnp.dot(rounded, w_out[:, at], preferred_element_type=f32)
-        grad_pre = (hidden * slope[tower * rows : (tower + 1) * rows, at].astype(f32)).astype(bf16)
-        part = jnp.dot(grad_pre, w_in[at, :], preferred_element_type=f32)
-        if t == 0:
-            total[...] = part
-        else:
-            total[...] += part
-    mine, theirs = halves(first, total[...])
-    send[...] = theirs.astype(bf16)
-    own[...] = grad[...] + mine
-
-
-def decode_one(me, grad, rounded, slope, tower, w_in, w_out, *after):
-    hidden, width = w_in.shape
+        out[:, at] = jnp.dot(mine[...], w_out[:, at], preferred_element_type=f32)
+
+
+def decode_far_kernel(tower, tile, near, theirs, slope, w_out, w_in, *refs):
+    grad_pre, send = refs[-2:]
+    rows = theirs.shape[0]
+    for t in range(w_out.shape[1] // tile):
+        at = slice(t * tile, (t + 1) * tile)
+        hidden = near[:, at] + jnp.dot(theirs[...], w_out[:, at], preferred_element_type=f32)
+        grad_pre[:, at] = (hidden * slope[tower * rows : (tower + 1) * rows, at].astype(f32)).astype(bf16)
+    send[...] = jnp.dot(grad_pre[...], w_in[...], preferred_element_type=f32).astype(bf16)
+
+
+def decode_own_kernel(grad, grad_pre, w_in, *refs):
+    refs[-1][...] = grad[...] + jnp.dot(grad_pre[...], w_in[...], preferred_element_type=f32)
+
+
+def decode_far(rounded, slope, tower, w_out_near, w_out_far, w_in_far, *after):
+    rows, hidden = rounded.shape[0], slope.shape[1]
+    tile = min(512, hidden)
+    near = local(
+        functools.partial(decode_near_kernel, tile),
+        "decode_near",
+        [((rows, hidden), f32)],
+        (rounded, w_out_near),
+        2,
+    )[0]
     return local(
-        functools.partial(decode_kernel, tower, min(512, hidden)),
-        "decode_one",
-        [(grad.shape, bf16), (grad.shape, f32)],
-        (grad, rounded, swap(rounded, "mp", 1), slope, w_in, w_out, *after),
-        3,
-        [pltpu.VMEM((grad.shape[0], width), f32)],
-        [me],
-    )
+        functools.partial(decode_far_kernel, tower, tile),
+        "decode_far",
+        [((rows, hidden), bf16), (rounded.shape, bf16)],
+        (near, swap(rounded, "mp", 1), slope, w_out_far, w_in_far, *after),
+        2,
+    )
+
+
+def decode_own(grad, grad_pre, w_in_near, *after):
+    return local(
+        decode_own_kernel, "decode_own", [(grad.shape, f32)], (grad, grad_pre, w_in_near, *after), 2
+    )[0]
 
 
 def finish_kernel(own, other, *refs):
@@ -614,23 +715,33 @@
     owners = served_rows.shape[1]
     me = lax.axis_index("mp").astype(jnp.int32).reshape(1)
     place = lax.axis_index("dp").astype(jnp.int32).reshape(1)
-    send_q, send_p, own_q, own_p, pre_act, slots, served, scale, w_in, w_out = encode_both(
-        me, place, loss_scale.reshape(1), query_states, passage_states, w_in, w_out, neg_owner, neg_mask, served_rows
+    send_q, send_p, states, hidden, pre_act, scale, w_in, w_out_far = encode_far(
+        me, place, loss_scale.reshape(1), query_states, passage_states, w_in, w_out
+    )
+    own_q, own_p, w_out_near, slots, served = encode_near(
+        me, w_out, neg_owner, neg_mask, served_rows, hidden, states
     )
     slope = local(slope_kernel, "slope", [(pre_act.shape, bf16)], (pre_act,))[0]
-    w_in, w_out = flip(w_in, "flip_in"), flip(w_out, "flip_out")
-    raw_q = pack(own_q, swap(send_q, "mp", 1), slots, slope, w_in, w_out)
+    w_in_far = flip_rows(me, w_in, True, "flip_in_far")
+    w_in_near = flip_rows(me, w_in, False, "flip_in_near")
+    w_out_far, w_out_near = flip(w_out_far, "flip_out_far"), flip(w_out_near, "flip_out_near")
+    raw_q = pack(own_q, swap(send_q, "mp", 1), slots)
     raw_p = pack(own_p, swap(send_p, "mp", 1), served)
+    q_blocks = gather_blocks(raw_q, query_bits)
     p_blocks = gather_blocks(raw_p, pass_bits)
-    q_blocks = gather_blocks(raw_q, query_bits)
-
-    table, valid, pick, q_all, p_all = score(place, q_blocks, p_blocks, rows, owners)
-    coefs, sums = weigh(table, swap(table, "mp", 1), valid, rows)
-    kept_q, sent_q = spread_query(coefs, pick, p_all, rows)
+
+    table, valid, pick, p_all, q_all = score(
+        place, q_blocks, p_blocks, rows, owners, w_out_near, slope, w_in_far
+    )
+    coefs, sums = weigh(table, swap(table, "mp", 1), valid, rows, w_out_far, w_in_near)
+    sent_q = spread_query(coefs, pick, p_all, rows, True)
     sums = exchange_sums(sums, query_bits[1], sent_q)
+    kept_q = spread_query(coefs, pick, p_all, rows, False)
     kept_q, sent_q = fold_query(kept_q, swap(sent_q, "dp", query_bits[1]))
     sums = exchange_sums(sums, query_bits[0], sent_q)
-    kept_p, sent_p = spread_pass(scale, coefs, sums, pick, q_all, p_all, rows)
+    operands = (scale, coefs, sums, pick, q_all, p_all, rows)
+    sent_p = spread_pass(*operands, tuple(range(1, len(pass_at))), bf16)
+    kept_p = spread_pass(*operands, (0,), f32)[0]
     others_p = [swap(x, "dp", at) for x, at in zip(sent_p, pass_at[1:])]
     grad_q, round_q = grad_out(
         grad_query_kernel,
@@ -644,8 +755,10 @@
         kept_p,
         (*others_p, coefs, round_q),
     )
-    send_q, own_q = decode_one(me, grad_q, round_q, slope, 0, w_in, w_out)
-    send_p, own_p = decode_one(me, grad_p, round_p, slope, 1, w_in, w_out, send_q)
+    pre_q, send_q = decode_far(round_q, slope, 0, w_out_near, w_out_far, w_in_far)
+    pre_p, send_p = decode_far(round_p, slope, 1, w_out_near, w_out_far, w_in_far, send_q)
+    own_q = decode_own(grad_q, pre_q, w_in_near, send_p)
+    own_p = decode_own(grad_p, pre_p, w_in_near)
     out_q, done_q = finish(own_q, swap(send_q, "mp", 1), "out_query")
     out_p, _ = finish(own_p, swap(send_p, "mp", 1), "out_pass", done_q)
     return (out_q, out_p)

time: 65 us -> 62.3 us (0.958)
  waiting for transfers between devices: 19.8 us -> 15.7 us
  Pallas kernels: 16 us -> 18.4 us
  starting transfers between devices: 26.9 us -> 25.5 us
    ppermute x20, waiting for transfers between devices: 19.8 us -> 15.7 us  [swap(): return lax.ppermute(values, axis, [(i, i ^ bit) for i in range(size)])]
    pallas_call x1 -> x2, Pallas kernels: 5.05 us -> 6.43 us  [the longest x1 4.3 us: encode_far(): pl.pallas_call(functools.partial(encode_far_kernel, tile), in_specs=[smem...]
    ppermute x20, starting transfers between devices: 26.9 us -> 25.5 us  [swap(): return lax.ppermute(values, axis, [(i, i ^ bit) for i in range(size)])]
    pallas_call x16 -> x25, Pallas kernels: 9.61 us -> 10.6 us  [local(): pl.pallas_call(kernel, in_specs=[smem] * len(scalars) + [vmem] * len(oper...]
  transfers between devices with their start and end apart: 20 -> 20, of which waited for: 13 -> 12; matrix products, arithmetic and copies ran while one was open for 0% -> 0% of each run, Pallas kernels for 13% -> 21%
where the time goes in v5:
time: 62.3 us; the launch traced here: 61.2 us
  starting transfers between devices  25.5 us (41%)
  Pallas kernels  18.4 us (30%)
  waiting for transfers between devices  15.7 us (25%)
  between operations  1.53 us (2%)
    ppermute x20, starting transfers between devices, swap(): return lax.ppermute(values, axis, [(i, i ^ bit) for i in range(size)])  25.5 us
    ppermute x20, waiting for transfers between devices, swap(): return lax.ppermute(values, axis, [(i, i ^ bit) for i in range(size)])  15.7 us
    pallas_call x25, Pallas kernels, local(): pl.pallas_call(kernel, in_specs=[smem] * len(scalars) + [vmem] * len(oper...  10.6 us
    pallas_call x1, Pallas kernels, encode_far(): pl.pallas_call(functools.partial(encode_far_kernel, tile), in_specs=[smem...  4.3 us
    pallas_call x1, Pallas kernels, encode_near(): pl.pallas_call(functools.partial(encode_near_kernel, tile), in_specs=[sme...  2.13 us
    pallas_call x2, Pallas kernels, finish(): pl.pallas_call(finish_kernel, in_specs=[vmem] * (2 + len(after)), out_spe...  1.37 us
  transfers between devices with their start and end apart: 20, of which 12 were waited for; matrix products, arithmetic and copies ran while one was open for 0% of the time, Pallas kernels for 21%

profile of v5, /device:TPU:0, one launch (start us, length us, event | category | flops | bytes accessed | tf_op | source)
XLA Modules:
  0.0 61.2 jit_solution(1398031265930984330)
XLA Ops:
  1.3 4.3 %encode_far.1 = (bf16[128,512]{1,0:T(8,128)(2,1)S(1)}, bf16[128,512]{1,0:T(8,128)(2,1)S(1)}, bf16[256,1024]{1,0:T(8,128)(2,1)S(1)}, bf16[256,2048]{1,0:T(8,128)(...) custom-call(s32[1]{0:T(128)} %bitcast.1.me, ...), custom_call_target="tpu_custom_call" | custom-call | tf_op jit(solution)/shard_map/encode_far/pallas_call | solution.py:241
  5.6 3.0 %collective-permute-start.3 = (bf16[128,512]{1,0:T(8,128)(2,1)S(1)}, bf16[128,512]{1,0:T(8,128)(2,1)S(1)}, u32[]{:S(2)}, u32[]{:S(2)}) collective-permute-start(bf16[128,512]{1,0:T(8,128)(2,1)S(1)} %get-tuple-element.49), channel_id=1, source_target_pairs={{0,1},{1,0},{2,3},{3,2},{4,5},{5,4},{6,7},{7,6},{8,9},{9,8},{10,11... | collective-permute-start | bytes 393224 | tf_op jit(solution)/shard_map/ppermute | solution.py:145
  8.6 0.1 collective-permute-start
  8.7 2.1 %encode_near.1 = (f32[128,512]{1,0:T(8,128)S(1)}, f32[128,512]{1,0:T(8,128)S(1)}, bf16[2048,512]{1,0:T(8,128)(2,1)S(1)}, bf16[16,128]{1,0:T(8,128)(2,1)S(1)}, bf16[16,128]{1,0:T(8,128)(2,1)S(1)}) custom-call(s32[1]{0:T(128)} %bitcast.1.me, bf16[2048,1024]{1,0:T(8,128)(2,1)} %w_out.3, s32[8,128]{1,0:T(8,128)} %bitcast.6, s32[8,128]{1,0:T(8,128)} %bitcast.7, ...), custom_call_target="tpu_custom_call" | custom-call | flops 1 | bytes 1 | tf_op jit(solution)/shard_map/encode_near/pallas_call | solution.py:312
  10.8 2.1 %collective-permute-done.3.other = bf16[128,512]{1,0:T(8,128)(2,1)S(1)} collective-permute-done((bf16[128,512]{1,0:T(8,128)(2,1)S(1)}, bf16[128,512]{1,0:T(8,128)(2,1)S(1)}, u32[]{:S(2)}, u32[]{:S(2)}) %collective-permute-start.3) | collective-permute-done | bytes 131104 | tf_op jit(solution)/shard_map/ppermute | solution.py:145
  13.0 3.2 %collective-permute-start.4 = (bf16[144,512]{1,0:T(8,128)(2,1)S(1)}, bf16[144,512]{1,0:T(8,128)(2,1)S(1)}, u32[]{:S(2)}, u32[]{:S(2)}) collective-permute-start(bf16[144,512]{1,0:T(8,128)(2,1)S(1)} %pack.3.refs_0_.raw), channel_id=1, source_target_pairs={{0,16},{2,18},{4,20},{6,22},{8,24},{10,26},{12,28},{14,30},{16,0},... | collective-permute-start | bytes 442376 | tf_op jit(solution)/shard_map/ppermute | solution.py:145
  16.2 0.0 collective-permute-done.other
  16.2 1.6 %collective-permute-start.1 = (bf16[144,512]{1,0:T(8,128)(2,1)S(1)}, bf16[144,512]{1,0:T(8,128)(2,1)S(1)}, u32[]{:S(2)}, u32[]{:S(2)}) collective-permute-start(bf16[144,512]{1,0:T(8,128)(2,1)S(1)} %pack.2.refs_4_.raw_pass), channel_id=1, source_target_pairs={{0,8},{2,10},{4,12},{6,14},{8,0},{10,2},{12,4},{14,6},{16,24},{18,... | collective-permute-start | bytes 442376 | tf_op jit(solution)/shard_map/ppermute | solution.py:145
  17.9 0.0 collective-permute-start.5
  17.9 1.5 %collective-permute-start.7 = (bf16[144,512]{1,0:T(8,128)(2,1)S(1)}, bf16[144,512]{1,0:T(8,128)(2,1)S(1)}, u32[]{:S(2)}, u32[]{:S(2)}) collective-permute-start(bf16[144,512]{1,0:T(8,128)(2,1)S(1)} %pack.2.refs_4_.raw_pass), channel_id=1, source_target_pairs={{0,4},{2,6},{4,0},{6,2},{8,12},{10,14},{12,8},{14,10},{16,20},{18,... | collective-permute-start | bytes 442376 | tf_op jit(solution)/shard_map/ppermute | solution.py:145
  19.4 1.1 %collective-permute-done.4.refs_1_ = bf16[144,512]{1,0:T(8,128)(2,1)S(1)} collective-permute-done((bf16[144,512]{1,0:T(8,128)(2,1)S(1)}, bf16[144,512]{1,0:T(8,128)(2,1)S(1)}, u32[]{:S(2)}, u32[]{:S(2)}) %collective-permute-start.4) | collective-permute-done | bytes 147488 | tf_op jit(solution)/shard_map/ppermute | solution.py:145
  20.5 0.0 collective-permute-start.6
  20.5 1.7 %collective-permute-done.1.refs_5_ = bf16[144,512]{1,0:T(8,128)(2,1)S(1)} collective-permute-done((bf16[144,512]{1,0:T(8,128)(2,1)S(1)}, bf16[144,512]{1,0:T(8,128)(2,1)S(1)}, u32[]{:S(2)}, u32[]{:S(2)}) %collective-permute-start.1) | collective-permute-done | bytes 147488 | tf_op jit(solution)/shard_map/ppermute | solution.py:145
  22.2 1.3 %collective-permute-start.2 = (bf16[144,512]{1,0:T(8,128)(2,1)S(1)}, bf16[144,512]{1,0:T(8,128)(2,1)S(1)}, u32[]{:S(2)}, u32[]{:S(2)}) collective-permute-start(bf16[144,512]{1,0:T(8,128)(2,1)S(1)} %collective-permute-done.1.refs_5_), channel_id=1, source_target_pairs={{0,4},{2,6},{4,0},{6,2},{8,12},{10,14},{12,8},{14,10},{16,20},{18,... | collective-permute-start | bytes 442376 | tf_op jit(solution)/shard_map/ppermute | solution.py:145
  23.5 0.8 %slope.1.refs_8_ = bf16[256,2048]{1,0:T(8,128)(2,1)S(1)} custom-call(f32[256,2048]{1,0:T(8,128)S(1)} %get-tuple-element.52.pre_act), custom_call_target="tpu_custom_call" | custom-call | flops 1 | bytes 1 | tf_op jit(solution)/shard_map/slope/pallas_call | solution.py:169
  24.3 0.7 %flip_out_near.1.refs_7_.w_out = bf16[512,2048]{1,0:T(8,128)(2,1)S(1)} custom-call(bf16[2048,512]{1,0:T(8,128)(2,1)S(1)} %get-tuple-element.51.weights), custom_call_target="tpu_custom_call" | custom-call | flops 1 | bytes 1 | tf_op jit(solution)/shard_map/flip_out_near/pallas_call | solution.py:169
  25.1 0.8 %flip_in_far.1.refs_9_.w_in = bf16[2048,512]{1,0:T(8,128)(2,1)S(1)} custom-call(s32[1]{0:T(128)} %bitcast.1.me, bf16[1024,2048]{1,0:T(8,128)(2,1)S(1)} %get-tuple-element.53.weights), custom_call_target="tpu_custom_call" | custom-call | flops 1 | bytes 1 | tf_op jit(solution)/shard_map/flip_in_far/pallas_call | solution.py:169
  25.9 0.0 collective-permute-done.5.refs_2_
  25.9 0.0 collective-permute-done.7.refs_6_
  25.9 0.0 collective-permute-done.6.refs_3_
  25.9 0.9 %score_early.1 = (f32[16,512]{1,0:T(8,128)S(1)}, f32[8,512]{1,0:T(8,128)S(1)}, bf16[512,512]{1,0:T(8,128)(2,1)S(1)}, bf16[512,512]{1,0:T(8,128)(2,1)S(1)}, bf16[...) custom-call(s32[1]{0:T(128)} %bitcast.place, bf16[144,512]{1,0:T(8,128)(2,1)S(1)} %pack.3.refs_0_.raw, ...), custom_call_target="tpu_custom_call" | custom-call | flops 1 | bytes 1 | tf_op jit(solution)/shard_map/score_early/pallas_call | solution.py:169
  26.8 0.6 collective-permute-done.2.ref
  27.4 0.4 score_last.1
  27.8 1.5 %collective-permute-start.8 = (f32[16,512]{1,0:T(8,128)S(1)}, f32[16,512]{1,0:T(8,128)S(1)}, u32[]{:S(2)}, u32[]{:S(2)}) collective-permute-start(f32[16,512]{1,0:T(8,128)S(1)} %get-tuple-element.60.table), channel_id=1, source_target_pairs={{0,1},{1,0},{2,3},{3,2},{4,5},{5,4},{6,7},{7,6},{8,9},{9,8},{10,11... | collective-permute-start | bytes 98312 | tf_op jit(solution)/shard_map/ppermute | solution.py:145
  29.3 0.7 %flip_in_near.1.refs_1_.w_in = bf16[2048,512]{1,0:T(8,128)(2,1)S(1)} custom-call(s32[1]{0:T(128)} %bitcast.1.me, bf16[1024,2048]{1,0:T(8,128)(2,1)S(1)} %get-tuple-element.53.weights), custom_call_target="tpu_custom_call" | custom-call | flops 1 | bytes 1 | tf_op jit(solution)/shard_map/flip_in_near/pallas_call | solution.py:169
  30.0 0.7 %flip_out_far.1.refs_0_.w_out = bf16[512,2048]{1,0:T(8,128)(2,1)S(1)} custom-call(bf16[2048,512]{1,0:T(8,128)(2,1)S(1)} %get-tuple-element.62.weights), custom_call_target="tpu_custom_call" | custom-call | flops 1 | bytes 1 | tf_op jit(solution)/shard_map/flip_out_far/pallas_call | solution.py:169
  30.8 1.0 %collective-permute-done.8.other = f32[16,512]{1,0:T(8,128)S(1)} collective-permute-done((f32[16,512]{1,0:T(8,128)S(1)}, f32[16,512]{1,0:T(8,128)S(1)}, u32[]{:S(2)}, u32[]{:S(2)}) %collective-permute-start.8) | collective-permute-done | bytes 32800 | tf_op jit(solution)/shard_map/ppermute | solution.py:145
  31.8 0.4 spread_query.3.refs_0_
  32.2 0.1 collective-permute-start.9
  32.2 0.5 collective-permute-start.11
  32.7 1.0 %collective-permute-done.11.other = f32[16,128]{1,0:T(8,128)S(1)} collective-permute-done((f32[16,128]{1,0:T(8,128)S(1)}, f32[16,128]{1,0:T(8,128)S(1)}, u32[]{:S(2)}, u32[]{:S(2)}) %collective-permute-start.11) | collective-permute-done | bytes 8224 | tf_op jit(solution)/shard_map/ppermute | solution.py:145
  33.8 2.2 %collective-permute-start.12 = (f32[16,128]{1,0:T(8,128)S(1)}, f32[16,128]{1,0:T(8,128)S(1)}, u32[]{:S(2)}, u32[]{:S(2)}) collective-permute-start(f32[16,128]{1,0:T(8,128)S(1)} %add_sums.2.sums), channel_id=1, source_target_pairs={{0,16},{2,18},{4,20},{6,22},{8,24},{10,26},{12,28},{14,30},{16,0},... | collective-permute-start | bytes 24584 | tf_op jit(solution)/shard_map/ppermute | solution.py:145
  36.0 0.4 spread_query.2.own
  36.3 0.0 collective-permute-done.9.other
  36.4 0.9 %collective-permute-start.10 = (bf16[128,512]{1,0:T(8,128)(2,1)S(1)}, bf16[128,512]{1,0:T(8,128)(2,1)S(1)}, u32[]{:S(2)}, u32[]{:S(2)}) collective-permute-start(bf16[128,512]{1,0:T(8,128)(2,1)S(1)} %get-tuple-element.67.refs_0_), channel_id=1, source_target_pairs={{0,16},{2,18},{4,20},{6,22},{8,24},{10,26},{12,28},{14,30},{16,0},... | collective-permute-start | bytes 393224 | tf_op jit(solution)/shard_map/ppermute | solution.py:145
  37.3 1.1 %collective-permute-done.12.other = f32[16,128]{1,0:T(8,128)S(1)} collective-permute-done((f32[16,128]{1,0:T(8,128)S(1)}, f32[16,128]{1,0:T(8,128)S(1)}, u32[]{:S(2)}, u32[]{:S(2)}) %collective-permute-start.12) | collective-permute-done | bytes 8224 | tf_op jit(solution)/shard_map/ppermute | solution.py:145
  38.4 0.5 spread_pass.3
  38.9 1.7 %collective-permute-start.14 = (bf16[128,512]{1,0:T(8,128)(2,1)S(1)}, bf16[128,512]{1,0:T(8,128)(2,1)S(1)}, u32[]{:S(2)}, u32[]{:S(2)}) collective-permute-start(bf16[128,512]{1,0:T(8,128)(2,1)S(1)} %get-tuple-element.73), channel_id=1, source_target_pairs={{0,8},{2,10},{4,12},{6,14},{8,0},{10,2},{12,4},{14,6},{16,24},{18,... | collective-permute-start | bytes 393224 | tf_op jit(solution)/shard_map/ppermute | solution.py:145
  40.7 1.6 %collective-permute-start.15 = (bf16[128,512]{1,0:T(8,128)(2,1)S(1)}, bf16[128,512]{1,0:T(8,128)(2,1)S(1)}, u32[]{:S(2)}, u32[]{:S(2)}) collective-permute-start(bf16[128,512]{1,0:T(8,128)(2,1)S(1)} %get-tuple-element.74), channel_id=1, source_target_pairs={{0,4},{2,6},{4,0},{6,2},{8,12},{10,14},{12,8},{14,10},{16,20},{18,... | collective-permute-start | bytes 393224 | tf_op jit(solution)/shard_map/ppermute | solution.py:145
  42.2 0.2 collective-permute-start.16
  42.5 0.3 spread_pass.2.own
  42.8 2.7 %collective-permute-done.10.other = bf16[128,512]{1,0:T(8,128)(2,1)S(1)} collective-permute-done((bf16[128,512]{1,0:T(8,128)(2,1)S(1)}, bf16[128,512]{1,0:T(8,128)(2,1)S(1)}, u32[]{:S(2)}, u32[]{:S(2)}) %collective-permute-start.10) | collective-permute-done | bytes 131104 | tf_op jit(solution)/shard_map/ppermute | solution.py:145
  45.5 0.2 grad_query.1
  45.7 1.6 %collective-permute-start.13 = (bf16[128,512]{1,0:T(8,128)(2,1)S(1)}, bf16[128,512]{1,0:T(8,128)(2,1)S(1)}, u32[]{:S(2)}, u32[]{:S(2)}) collective-permute-start(bf16[128,512]{1,0:T(8,128)(2,1)S(1)} %get-tuple-element.71.mine.after), channel_id=1, source_target_pairs={{0,1},{1,0},{2,3},{3,2},{4,5},{5,4},{6,7},{7,6},{8,9},{9,8},{10,11... | collective-permute-start | bytes 393224 | tf_op jit(solution)/shard_map/ppermute | solution.py:145
  47.3 0.0 collective-permute-done.14.first
  47.3 0.0 collective-permute-done.15.second
  47.3 1.9 %collective-permute-done.16.third = bf16[128,512]{1,0:T(8,128)(2,1)S(1)} collective-permute-done((bf16[128,512]{1,0:T(8,128)(2,1)S(1)}, bf16[128,512]{1,0:T(8,128)(2,1)S(1)}, u32[]{:S(2)}, u32[]{:S(2)}) %collective-permute-start.16) | collective-permute-done | bytes 131104 | tf_op jit(solution)/shard_map/ppermute | solution.py:145
  49.2 0.1 grad_pass.1
  49.3 1.6 %collective-permute-start.17 = (bf16[128,512]{1,0:T(8,128)(2,1)S(1)}, bf16[128,512]{1,0:T(8,128)(2,1)S(1)}, u32[]{:S(2)}, u32[]{:S(2)}) collective-permute-start(bf16[128,512]{1,0:T(8,128)(2,1)S(1)} %get-tuple-element.76.mine), channel_id=1, source_target_pairs={{0,1},{1,0},{2,3},{3,2},{4,5},{5,4},{6,7},{7,6},{8,9},{9,8},{10,11... | collective-permute-start | bytes 393224 | tf_op jit(solution)/shard_map/ppermute | solution.py:145
  50.9 0.5 decode_near.2.near
  51.3 0.5 decode_near.3.near
  51.8 0.0 collective-permute-done.13.theirs
  51.8 0.8 %decode_far.2 = (bf16[128,2048]{1,0:T(8,128)(2,1)S(1)}, bf16[128,512]{1,0:T(8,128)(2,1)S(1)}) custom-call(f32[128,2048]{1,0:T(8,128)S(1)} %decode_near.2.near, bf16[128,512]{1,0:T(8,128)(2,1)S(1)} %collective-permute-done.13.theirs, bf16[256,2048]{1,0:T(8,128)(2,1)S(1)} %slope.1.refs_8_, bf16[512,2048]{1,0:T(8,128)(2,1)S(1)} %flip_out_far.1.refs_0_.w_out, ...), custom_call_target="tpu_custom_call" | custom-call | flops 1 | bytes 1 | tf_op jit(solution)/shard_map/decode_far/pallas_call | solution.py:169
  52.7 0.6 collective-permute-start.18
  53.3 1.0 %collective-permute-done.17.theirs = bf16[128,512]{1,0:T(8,128)(2,1)S(1)} collective-permute-done((bf16[128,512]{1,0:T(8,128)(2,1)S(1)}, bf16[128,512]{1,0:T(8,128)(2,1)S(1)}, u32[]{:S(2)}, u32[]{:S(2)}) %collective-permute-start.17) | collective-permute-done | bytes 131104 | tf_op jit(solution)/shard_map/ppermute | solution.py:145
  54.3 0.8 %decode_far.3 = (bf16[128,2048]{1,0:T(8,128)(2,1)S(1)}, bf16[128,512]{1,0:T(8,128)(2,1)S(1)}) custom-call(f32[128,2048]{1,0:T(8,128)S(1)} %decode_near.3.near, bf16[128,512]{1,0:T(8,128)(2,1)S(1)} %collective-permute-done.17.theirs, bf16[256,2048]{1,0:T(8,128)(2,1)S(1)} %slope.1.refs_8_, bf16[512,2048]{1,0:T(8,128)(2,1)S(1)} %flip_out_far.1.refs_0_.w_out, ...), custom_call_target="tpu_custom_call" | custom-call | flops 1 | bytes 1 | tf_op jit(solution)/shard_map/decode_far/pallas_call | solution.py:169
  55.2 2.4 %collective-permute-start.19 = (bf16[128,512]{1,0:T(8,128)(2,1)S(1)}, bf16[128,512]{1,0:T(8,128)(2,1)S(1)}, u32[]{:S(2)}, u32[]{:S(2)}) collective-permute-start(bf16[128,512]{1,0:T(8,128)(2,1)S(1)} %get-tuple-element.78.refs_0_), channel_id=1, source_target_pairs={{0,1},{1,0},{2,3},{3,2},{4,5},{5,4},{6,7},{7,6},{8,9},{9,8},{10,11... | collective-permute-start | bytes 393224 | tf_op jit(solution)/shard_map/ppermute | solution.py:145
  57.6 0.5 decode_own.2.own
  58.1 0.5 decode_own.3.own
  58.5 0.4 collective-permute-done.18.other
  59.0 0.7 %out_query.1 = (bf16[128,512]{1,0:T(8,128)(2,1)}, f32[8,128]{1,0:T(8,128)S(1)}) custom-call(f32[128,512]{1,0:T(8,128)S(1)} %decode_own.2.own, bf16[128,512]{1,0:T(8,128)(2,1)S(1)} %collective-permute-done.18.other), custom_call_target="tpu_custom_call" | custom-call | tf_op jit(solution)/shard_map/out_query/pallas_call | solution.py:701
  59.6 0.9 %collective-permute-done.19.other = bf16[128,512]{1,0:T(8,128)(2,1)S(1)} collective-permute-done((bf16[128,512]{1,0:T(8,128)(2,1)S(1)}, bf16[128,512]{1,0:T(8,128)(2,1)S(1)}, u32[]{:S(2)}, u32[]{:S(2)}) %collective-permute-start.19) | collective-permute-done | bytes 131104 | tf_op jit(solution)/shard_map/ppermute | solution.py:145
  60.5 0.7 %out_pass.1 = (bf16[128,512]{1,0:T(8,128)(2,1)}, f32[8,128]{1,0:T(8,128)}) custom-call(f32[128,512]{1,0:T(8,128)S(1)} %decode_own.3.own, bf16[128,512]{1,0:T(8,128)(2,1)S(1)} %collective-permute-done.19.other, f32[8,128]{1,0:T(8,128)S(1)} %get-tuple-element.82.refs_0_), custom_call_target="tpu_custom_call" | custom-call | tf_op jit(solution)/shard_map/out_pass/pallas_call | solution.py:701
  (6 shorter events, 0.2 us)
Async XLA Ops:
  5.6 7.4 %collective-permute-start.3 = (bf16[128,512]{1,0:T(8,128)(2,1)S(1)}, bf16[128,512]{1,0:T(8,128)(2,1)S(1)}, u32[]{:S(2)}, u32[]{:S(2)}) collective-permute-start(bf16[128,512]{1,0:T(8,128)(2,1)S(1)} %get-tuple-element.49), channel_id=1, source_target_pairs={{0,1},{1,0},{2,3},{3,2},{4,5},{5,4},{6,7},{7,6},{8,9},{9,8},{10,11... | collective-permute-start | bytes 393224 | tf_op jit(solution)/shard_map/ppermute | solution.py:145
  8.6 7.6 %collective-permute-start = (bf16[128,512]{1,0:T(8,128)(2,1)S(1)}, bf16[128,512]{1,0:T(8,128)(2,1)S(1)}, u32[]{:S(2)}, u32[]{:S(2)}) collective-permute-start(bf16[128,512]{1,0:T(8,128)(2,1)S(1)} %get-tuple-element.46), channel_id=1, source_target_pairs={{0,1},{1,0},{2,3},{3,2},{4,5},{5,4},{6,7},{7,6},{8,9},{9,8},{10,11... | collective-permute-start | bytes 393224 | tf_op jit(solution)/shard_map/ppermute | solution.py:145
  13.0 7.5 %collective-permute-start.4 = (bf16[144,512]{1,0:T(8,128)(2,1)S(1)}, bf16[144,512]{1,0:T(8,128)(2,1)S(1)}, u32[]{:S(2)}, u32[]{:S(2)}) collective-permute-start(bf16[144,512]{1,0:T(8,128)(2,1)S(1)} %pack.3.refs_0_.raw), channel_id=1, source_target_pairs={{0,16},{2,18},{4,20},{6,22},{8,24},{10,26},{12,28},{14,30},{16,0},... | collective-permute-start | bytes 442376 | tf_op jit(solution)/shard_map/ppermute | solution.py:145
  16.2 6.0 %collective-permute-start.1 = (bf16[144,512]{1,0:T(8,128)(2,1)S(1)}, bf16[144,512]{1,0:T(8,128)(2,1)S(1)}, u32[]{:S(2)}, u32[]{:S(2)}) collective-permute-start(bf16[144,512]{1,0:T(8,128)(2,1)S(1)} %pack.2.refs_4_.raw_pass), channel_id=1, source_target_pairs={{0,8},{2,10},{4,12},{6,14},{8,0},{10,2},{12,4},{14,6},{16,24},{18,... | collective-permute-start | bytes 442376 | tf_op jit(solution)/shard_map/ppermute | solution.py:145
  17.9 8.0 %collective-permute-start.5 = (bf16[144,512]{1,0:T(8,128)(2,1)S(1)}, bf16[144,512]{1,0:T(8,128)(2,1)S(1)}, u32[]{:S(2)}, u32[]{:S(2)}) collective-permute-start(bf16[144,512]{1,0:T(8,128)(2,1)S(1)} %pack.3.refs_0_.raw), channel_id=1, source_target_pairs={{0,2},{2,0},{4,6},{6,4},{8,10},{10,8},{12,14},{14,12},{16,18},{18,... | collective-permute-start | bytes 442376 | tf_op jit(solution)/shard_map/ppermute | solution.py:145
  17.9 8.0 %collective-permute-start.7 = (bf16[144,512]{1,0:T(8,128)(2,1)S(1)}, bf16[144,512]{1,0:T(8,128)(2,1)S(1)}, u32[]{:S(2)}, u32[]{:S(2)}) collective-permute-start(bf16[144,512]{1,0:T(8,128)(2,1)S(1)} %pack.2.refs_4_.raw_pass), channel_id=1, source_target_pairs={{0,4},{2,6},{4,0},{6,2},{8,12},{10,14},{12,8},{14,10},{16,20},{18,... | collective-permute-start | bytes 442376 | tf_op jit(solution)/shard_map/ppermute | solution.py:145
  20.5 5.4 %collective-permute-start.6 = (bf16[144,512]{1,0:T(8,128)(2,1)S(1)}, bf16[144,512]{1,0:T(8,128)(2,1)S(1)}, u32[]{:S(2)}, u32[]{:S(2)}) collective-permute-start(bf16[144,512]{1,0:T(8,128)(2,1)S(1)} %collective-permute-done.4.refs_1_), channel_id=1, source_target_pairs={{0,2},{2,0},{4,6},{6,4},{8,10},{10,8},{12,14},{14,12},{16,18},{18,... | collective-permute-start | bytes 442376 | tf_op jit(solution)/shard_map/ppermute | solution.py:145
  22.2 5.1 %collective-permute-start.2 = (bf16[144,512]{1,0:T(8,128)(2,1)S(1)}, bf16[144,512]{1,0:T(8,128)(2,1)S(1)}, u32[]{:S(2)}, u32[]{:S(2)}) collective-permute-start(bf16[144,512]{1,0:T(8,128)(2,1)S(1)} %collective-permute-done.1.refs_5_), channel_id=1, source_target_pairs={{0,4},{2,6},{4,0},{6,2},{8,12},{10,14},{12,8},{14,10},{16,20},{18,... | collective-permute-start | bytes 442376 | tf_op jit(solution)/shard_map/ppermute | solution.py:145
  27.8 4.0 %collective-permute-start.8 = (f32[16,512]{1,0:T(8,128)S(1)}, f32[16,512]{1,0:T(8,128)S(1)}, u32[]{:S(2)}, u32[]{:S(2)}) collective-permute-start(f32[16,512]{1,0:T(8,128)S(1)} %get-tuple-element.60.table), channel_id=1, source_target_pairs={{0,1},{1,0},{2,3},{3,2},{4,5},{5,4},{6,7},{7,6},{8,9},{9,8},{10,11... | collective-permute-start | bytes 98312 | tf_op jit(solution)/shard_map/ppermute | solution.py:145
  32.2 4.2 %collective-permute-start.9 = (bf16[256,512]{1,0:T(8,128)(2,1)S(1)}, bf16[256,512]{1,0:T(8,128)(2,1)S(1)}, u32[]{:S(2)}, u32[]{:S(2)}) collective-permute-start(bf16[256,512]{1,0:T(8,128)(2,1)S(1)} %spread_query.3.refs_0_), channel_id=1, source_target_pairs={{0,2},{2,0},{4,6},{6,4},{8,10},{10,8},{12,14},{14,12},{16,18},{18,... | collective-permute-start | bytes 786440 | tf_op jit(solution)/shard_map/ppermute | solution.py:145
  32.2 1.5 %collective-permute-start.11 = (f32[16,128]{1,0:T(8,128)S(1)}, f32[16,128]{1,0:T(8,128)S(1)}, u32[]{:S(2)}, u32[]{:S(2)}) collective-permute-start(f32[16,128]{1,0:T(8,128)S(1)} %get-tuple-element.69.sums), channel_id=1, source_target_pairs={{0,2},{2,0},{4,6},{6,4},{8,10},{10,8},{12,14},{14,12},{16,18},{18,... | collective-permute-start | bytes 24584 | tf_op jit(solution)/shard_map/ppermute | solution.py:145
  33.8 4.6 %collective-permute-start.12 = (f32[16,128]{1,0:T(8,128)S(1)}, f32[16,128]{1,0:T(8,128)S(1)}, u32[]{:S(2)}, u32[]{:S(2)}) collective-permute-start(f32[16,128]{1,0:T(8,128)S(1)} %add_sums.2.sums), channel_id=1, source_target_pairs={{0,16},{2,18},{4,20},{6,22},{8,24},{10,26},{12,28},{14,30},{16,0},... | collective-permute-start | bytes 24584 | tf_op jit(solution)/shard_map/ppermute | solution.py:145
  36.4 9.1 %collective-permute-start.10 = (bf16[128,512]{1,0:T(8,128)(2,1)S(1)}, bf16[128,512]{1,0:T(8,128)(2,1)S(1)}, u32[]{:S(2)}, u32[]{:S(2)}) collective-permute-start(bf16[128,512]{1,0:T(8,128)(2,1)S(1)} %get-tuple-element.67.refs_0_), channel_id=1, source_target_pairs={{0,16},{2,18},{4,20},{6,22},{8,24},{10,26},{12,28},{14,30},{16,0},... | collective-permute-start | bytes 393224 | tf_op jit(solution)/shard_map/ppermute | solution.py:145
  38.9 8.3 %collective-permute-start.14 = (bf16[128,512]{1,0:T(8,128)(2,1)S(1)}, bf16[128,512]{1,0:T(8,128)(2,1)S(1)}, u32[]{:S(2)}, u32[]{:S(2)}) collective-permute-start(bf16[128,512]{1,0:T(8,128)(2,1)S(1)} %get-tuple-element.73), channel_id=1, source_target_pairs={{0,8},{2,10},{4,12},{6,14},{8,0},{10,2},{12,4},{14,6},{16,24},{18,... | collective-permute-start | bytes 393224 | tf_op jit(solution)/shard_map/ppermute | solution.py:145
  40.7 6.6 %collective-permute-start.15 = (bf16[128,512]{1,0:T(8,128)(2,1)S(1)}, bf16[128,512]{1,0:T(8,128)(2,1)S(1)}, u32[]{:S(2)}, u32[]{:S(2)}) collective-permute-start(bf16[128,512]{1,0:T(8,128)(2,1)S(1)} %get-tuple-element.74), channel_id=1, source_target_pairs={{0,4},{2,6},{4,0},{6,2},{8,12},{10,14},{12,8},{14,10},{16,20},{18,... | collective-permute-start | bytes 393224 | tf_op jit(solution)/shard_map/ppermute | solution.py:145
  42.2 6.9 %collective-permute-start.16 = (bf16[128,512]{1,0:T(8,128)(2,1)S(1)}, bf16[128,512]{1,0:T(8,128)(2,1)S(1)}, u32[]{:S(2)}, u32[]{:S(2)}) collective-permute-start(bf16[128,512]{1,0:T(8,128)(2,1)S(1)} %get-tuple-element.75), channel_id=1, source_target_pairs={{0,12},{2,14},{4,8},{6,10},{8,4},{10,6},{12,0},{14,2},{16,28},{18,... | collective-permute-start | bytes 393224 | tf_op jit(solution)/shard_map/ppermute | solution.py:145
  45.7 6.1 %collective-permute-start.13 = (bf16[128,512]{1,0:T(8,128)(2,1)S(1)}, bf16[128,512]{1,0:T(8,128)(2,1)S(1)}, u32[]{:S(2)}, u32[]{:S(2)}) collective-permute-start(bf16[128,512]{1,0:T(8,128)(2,1)S(1)} %get-tuple-element.71.mine.after), channel_id=1, source_target_pairs={{0,1},{1,0},{2,3},{3,2},{4,5},{5,4},{6,7},{7,6},{8,9},{9,8},{10,11... | collective-permute-start | bytes 393224 | tf_op jit(solution)/shard_map/ppermute | solution.py:145
  49.3 5.0 %collective-permute-start.17 = (bf16[128,512]{1,0:T(8,128)(2,1)S(1)}, bf16[128,512]{1,0:T(8,128)(2,1)S(1)}, u32[]{:S(2)}, u32[]{:S(2)}) collective-permute-start(bf16[128,512]{1,0:T(8,128)(2,1)S(1)} %get-tuple-element.76.mine), channel_id=1, source_target_pairs={{0,1},{1,0},{2,3},{3,2},{4,5},{5,4},{6,7},{7,6},{8,9},{9,8},{10,11... | collective-permute-start | bytes 393224 | tf_op jit(solution)/shard_map/ppermute | solution.py:145
  52.7 6.3 %collective-permute-start.18 = (bf16[128,512]{1,0:T(8,128)(2,1)S(1)}, bf16[128,512]{1,0:T(8,128)(2,1)S(1)}, u32[]{:S(2)}, u32[]{:S(2)}) collective-permute-start(bf16[128,512]{1,0:T(8,128)(2,1)S(1)} %get-tuple-element.77.refs_0_), channel_id=1, source_target_pairs={{0,1},{1,0},{2,3},{3,2},{4,5},{5,4},{6,7},{7,6},{8,9},{9,8},{10,11... | collective-permute-start | bytes 393224 | tf_op jit(solution)/shard_map/ppermute | solution.py:145
  55.2 5.3 %collective-permute-start.19 = (bf16[128,512]{1,0:T(8,128)(2,1)S(1)}, bf16[128,512]{1,0:T(8,128)(2,1)S(1)}, u32[]{:S(2)}, u32[]{:S(2)}) collective-permute-start(bf16[128,512]{1,0:T(8,128)(2,1)S(1)} %get-tuple-element.78.refs_0_), channel_id=1, source_target_pairs={{0,1},{1,0},{2,3},{3,2},{4,5},{5,4},{6,7},{7,6},{8,9},{9,8},{10,11... | collective-permute-start | bytes 393224 | tf_op jit(solution)/shard_map/ppermute | solution.py:145

commit v6 on v5

--- a/solution.py
+++ b/solution.py
@@ -742,7 +742,7 @@
     operands = (scale, coefs, sums, pick, q_all, p_all, rows)
     sent_p = spread_pass(*operands, tuple(range(1, len(pass_at))), bf16)
     kept_p = spread_pass(*operands, (0,), f32)[0]
-    others_p = [swap(x, "dp", at) for x, at in zip(sent_p, pass_at[1:])]
+    others_p = [swap(sent_p[n - 1], "dp", pass_at[n]) for n in (3, 2, 1)]
     grad_q, round_q = grad_out(
         grad_query_kernel,
         "grad_query",

time: 62.3 us -> 61.4 us (0.986)
  waiting for transfers between devices: 15.7 us -> 14.7 us
    ppermute x20, waiting for transfers between devices: 15.7 us -> 14.7 us  [swap(): return lax.ppermute(values, axis, [(i, i ^ bit) for i in range(size)])]
  transfers between devices with their start and end apart: 20 -> 20, of which waited for: 12 -> 11; matrix products, arithmetic and copies ran while one was open for 0% -> 0% of each run, Pallas kernels for 21% -> 21%
where the time goes in v6:
time: 61.4 us; the launch traced here: 60.8 us
  starting transfers between devices  26.1 us (43%)
  Pallas kernels  18.4 us (30%)
  waiting for transfers between devices  14.7 us (24%)
  between operations  1.53 us (2%)
    ppermute x20, starting transfers between devices, swap(): return lax.ppermute(values, axis, [(i, i ^ bit) for i in range(size)])  26.1 us
    ppermute x20, waiting for transfers between devices, swap(): return lax.ppermute(values, axis, [(i, i ^ bit) for i in range(size)])  14.7 us
    pallas_call x25, Pallas kernels, local(): pl.pallas_call(kernel, in_specs=[smem] * len(scalars) + [vmem] * len(oper...  10.6 us
    pallas_call x1, Pallas kernels, encode_far(): pl.pallas_call(functools.partial(encode_far_kernel, tile), in_specs=[smem...  4.3 us
    pallas_call x1, Pallas kernels, encode_near(): pl.pallas_call(functools.partial(encode_near_kernel, tile), in_specs=[sme...  2.13 us
    pallas_call x2, Pallas kernels, finish(): pl.pallas_call(finish_kernel, in_specs=[vmem] * (2 + len(after)), out_spe...  1.37 us
  transfers between devices with their start and end apart: 20, of which 11 were waited for; matrix products, arithmetic and copies ran while one was open for 0% of the time, Pallas kernels for 21%

profile of v6, /device:TPU:0, one launch (start us, length us, event | category | flops | bytes accessed | tf_op | source)
XLA Modules:
  0.0 60.8 jit_solution(18321052178458763815)
XLA Ops:
  1.3 4.3 %encode_far.1 = (bf16[128,512]{1,0:T(8,128)(2,1)S(1)}, bf16[128,512]{1,0:T(8,128)(2,1)S(1)}, bf16[256,1024]{1,0:T(8,128)(2,1)S(1)}, bf16[256,2048]{1,0:T(8,128)(...) custom-call(s32[1]{0:T(128)} %bitcast.1.me, ...), custom_call_target="tpu_custom_call" | custom-call | tf_op jit(solution)/shard_map/encode_far/pallas_call | solution.py:241
  5.6 3.0 %collective-permute-start.3 = (bf16[128,512]{1,0:T(8,128)(2,1)S(1)}, bf16[128,512]{1,0:T(8,128)(2,1)S(1)}, u32[]{:S(2)}, u32[]{:S(2)}) collective-permute-start(bf16[128,512]{1,0:T(8,128)(2,1)S(1)} %get-tuple-element.49), channel_id=1, source_target_pairs={{0,1},{1,0},{2,3},{3,2},{4,5},{5,4},{6,7},{7,6},{8,9},{9,8},{10,11... | collective-permute-start | bytes 393224 | tf_op jit(solution)/shard_map/ppermute | solution.py:145
  8.6 0.1 collective-permute-start
  8.7 2.1 %encode_near.1 = (f32[128,512]{1,0:T(8,128)S(1)}, f32[128,512]{1,0:T(8,128)S(1)}, bf16[2048,512]{1,0:T(8,128)(2,1)S(1)}, bf16[16,128]{1,0:T(8,128)(2,1)S(1)}, bf16[16,128]{1,0:T(8,128)(2,1)S(1)}) custom-call(s32[1]{0:T(128)} %bitcast.1.me, bf16[2048,1024]{1,0:T(8,128)(2,1)} %w_out.3, s32[8,128]{1,0:T(8,128)} %bitcast.6, s32[8,128]{1,0:T(8,128)} %bitcast.7, ...), custom_call_target="tpu_custom_call" | custom-call | flops 1 | bytes 1 | tf_op jit(solution)/shard_map/encode_near/pallas_call | solution.py:312
  10.8 2.1 %collective-permute-done.3.other = bf16[128,512]{1,0:T(8,128)(2,1)S(1)} collective-permute-done((bf16[128,512]{1,0:T(8,128)(2,1)S(1)}, bf16[128,512]{1,0:T(8,128)(2,1)S(1)}, u32[]{:S(2)}, u32[]{:S(2)}) %collective-permute-start.3) | collective-permute-done | bytes 131104 | tf_op jit(solution)/shard_map/ppermute | solution.py:145
  13.0 3.2 %collective-permute-start.4 = (bf16[144,512]{1,0:T(8,128)(2,1)S(1)}, bf16[144,512]{1,0:T(8,128)(2,1)S(1)}, u32[]{:S(2)}, u32[]{:S(2)}) collective-permute-start(bf16[144,512]{1,0:T(8,128)(2,1)S(1)} %pack.3.refs_0_.raw), channel_id=1, source_target_pairs={{0,16},{2,18},{4,20},{6,22},{8,24},{10,26},{12,28},{14,30},{16,0},... | collective-permute-start | bytes 442376 | tf_op jit(solution)/shard_map/ppermute | solution.py:145
  16.2 0.0 collective-permute-done.other
  16.2 1.6 %collective-permute-start.1 = (bf16[144,512]{1,0:T(8,128)(2,1)S(1)}, bf16[144,512]{1,0:T(8,128)(2,1)S(1)}, u32[]{:S(2)}, u32[]{:S(2)}) collective-permute-start(bf16[144,512]{1,0:T(8,128)(2,1)S(1)} %pack.2.refs_4_.raw_pass), channel_id=1, source_target_pairs={{0,8},{2,10},{4,12},{6,14},{8,0},{10,2},{12,4},{14,6},{16,24},{18,... | collective-permute-start | bytes 442376 | tf_op jit(solution)/shard_map/ppermute | solution.py:145
  17.9 0.0 collective-permute-start.5
  17.9 1.5 %collective-permute-start.7 = (bf16[144,512]{1,0:T(8,128)(2,1)S(1)}, bf16[144,512]{1,0:T(8,128)(2,1)S(1)}, u32[]{:S(2)}, u32[]{:S(2)}) collective-permute-start(bf16[144,512]{1,0:T(8,128)(2,1)S(1)} %pack.2.refs_4_.raw_pass), channel_id=1, source_target_pairs={{0,4},{2,6},{4,0},{6,2},{8,12},{10,14},{12,8},{14,10},{16,20},{18,... | collective-permute-start | bytes 442376 | tf_op jit(solution)/shard_map/ppermute | solution.py:145
  19.4 1.1 %collective-permute-done.4.refs_1_ = bf16[144,512]{1,0:T(8,128)(2,1)S(1)} collective-permute-done((bf16[144,512]{1,0:T(8,128)(2,1)S(1)}, bf16[144,512]{1,0:T(8,128)(2,1)S(1)}, u32[]{:S(2)}, u32[]{:S(2)}) %collective-permute-start.4) | collective-permute-done | bytes 147488 | tf_op jit(solution)/shard_map/ppermute | solution.py:145
  20.5 0.0 collective-permute-start.6
  20.5 1.7 %collective-permute-done.1.refs_5_ = bf16[144,512]{1,0:T(8,128)(2,1)S(1)} collective-permute-done((bf16[144,512]{1,0:T(8,128)(2,1)S(1)}, bf16[144,512]{1,0:T(8,128)(2,1)S(1)}, u32[]{:S(2)}, u32[]{:S(2)}) %collective-permute-start.1) | collective-permute-done | bytes 147488 | tf_op jit(solution)/shard_map/ppermute | solution.py:145
  22.2 1.3 %collective-permute-start.2 = (bf16[144,512]{1,0:T(8,128)(2,1)S(1)}, bf16[144,512]{1,0:T(8,128)(2,1)S(1)}, u32[]{:S(2)}, u32[]{:S(2)}) collective-permute-start(bf16[144,512]{1,0:T(8,128)(2,1)S(1)} %collective-permute-done.1.refs_5_), channel_id=1, source_target_pairs={{0,4},{2,6},{4,0},{6,2},{8,12},{10,14},{12,8},{14,10},{16,20},{18,... | collective-permute-start | bytes 442376 | tf_op jit(solution)/shard_map/ppermute | solution.py:145
  23.5 0.8 %slope.1.refs_8_ = bf16[256,2048]{1,0:T(8,128)(2,1)S(1)} custom-call(f32[256,2048]{1,0:T(8,128)S(1)} %get-tuple-element.52.pre_act), custom_call_target="tpu_custom_call" | custom-call | flops 1 | bytes 1 | tf_op jit(solution)/shard_map/slope/pallas_call | solution.py:169
  24.3 0.7 %flip_out_near.1.refs_7_.w_out = bf16[512,2048]{1,0:T(8,128)(2,1)S(1)} custom-call(bf16[2048,512]{1,0:T(8,128)(2,1)S(1)} %get-tuple-element.51.weights), custom_call_target="tpu_custom_call" | custom-call | flops 1 | bytes 1 | tf_op jit(solution)/shard_map/flip_out_near/pallas_call | solution.py:169
  25.1 0.8 %flip_in_far.1.refs_9_.w_in = bf16[2048,512]{1,0:T(8,128)(2,1)S(1)} custom-call(s32[1]{0:T(128)} %bitcast.1.me, bf16[1024,2048]{1,0:T(8,128)(2,1)S(1)} %get-tuple-element.53.weights), custom_call_target="tpu_custom_call" | custom-call | flops 1 | bytes 1 | tf_op jit(solution)/shard_map/flip_in_far/pallas_call | solution.py:169
  25.9 0.0 collective-permute-done.5.refs_2_
  25.9 0.0 collective-permute-done.7.refs_6_
  25.9 0.0 collective-permute-done.6.refs_3_
  25.9 0.9 %score_early.1 = (f32[16,512]{1,0:T(8,128)S(1)}, f32[8,512]{1,0:T(8,128)S(1)}, bf16[512,512]{1,0:T(8,128)(2,1)S(1)}, bf16[512,512]{1,0:T(8,128)(2,1)S(1)}, bf16[...) custom-call(s32[1]{0:T(128)} %bitcast.place, bf16[144,512]{1,0:T(8,128)(2,1)S(1)} %pack.3.refs_0_.raw, ...), custom_call_target="tpu_custom_call" | custom-call | flops 1 | bytes 1 | tf_op jit(solution)/shard_map/score_early/pallas_call | solution.py:169
  26.8 0.6 collective-permute-done.2.ref
  27.4 0.4 score_last.1
  27.8 1.5 %collective-permute-start.8 = (f32[16,512]{1,0:T(8,128)S(1)}, f32[16,512]{1,0:T(8,128)S(1)}, u32[]{:S(2)}, u32[]{:S(2)}) collective-permute-start(f32[16,512]{1,0:T(8,128)S(1)} %get-tuple-element.60.table), channel_id=1, source_target_pairs={{0,1},{1,0},{2,3},{3,2},{4,5},{5,4},{6,7},{7,6},{8,9},{9,8},{10,11... | collective-permute-start | bytes 98312 | tf_op jit(solution)/shard_map/ppermute | solution.py:145
  29.3 0.7 %flip_in_near.1.refs_1_.w_in = bf16[2048,512]{1,0:T(8,128)(2,1)S(1)} custom-call(s32[1]{0:T(128)} %bitcast.1.me, bf16[1024,2048]{1,0:T(8,128)(2,1)S(1)} %get-tuple-element.53.weights), custom_call_target="tpu_custom_call" | custom-call | flops 1 | bytes 1 | tf_op jit(solution)/shard_map/flip_in_near/pallas_call | solution.py:169
  30.0 0.7 %flip_out_far.1.refs_0_.w_out = bf16[512,2048]{1,0:T(8,128)(2,1)S(1)} custom-call(bf16[2048,512]{1,0:T(8,128)(2,1)S(1)} %get-tuple-element.62.weights), custom_call_target="tpu_custom_call" | custom-call | flops 1 | bytes 1 | tf_op jit(solution)/shard_map/flip_out_far/pallas_call | solution.py:169
  30.8 1.0 %collective-permute-done.8.other = f32[16,512]{1,0:T(8,128)S(1)} collective-permute-done((f32[16,512]{1,0:T(8,128)S(1)}, f32[16,512]{1,0:T(8,128)S(1)}, u32[]{:S(2)}, u32[]{:S(2)}) %collective-permute-start.8) | collective-permute-done | bytes 32800 | tf_op jit(solution)/shard_map/ppermute | solution.py:145
  31.8 0.4 spread_query.3.refs_0_
  32.2 0.1 collective-permute-start.9
  32.2 0.5 collective-permute-start.11
  32.7 1.0 %collective-permute-done.11.other = f32[16,128]{1,0:T(8,128)S(1)} collective-permute-done((f32[16,128]{1,0:T(8,128)S(1)}, f32[16,128]{1,0:T(8,128)S(1)}, u32[]{:S(2)}, u32[]{:S(2)}) %collective-permute-start.11) | collective-permute-done | bytes 8224 | tf_op jit(solution)/shard_map/ppermute | solution.py:145
  33.8 2.2 %collective-permute-start.12 = (f32[16,128]{1,0:T(8,128)S(1)}, f32[16,128]{1,0:T(8,128)S(1)}, u32[]{:S(2)}, u32[]{:S(2)}) collective-permute-start(f32[16,128]{1,0:T(8,128)S(1)} %add_sums.2.sums), channel_id=1, source_target_pairs={{0,16},{2,18},{4,20},{6,22},{8,24},{10,26},{12,28},{14,30},{16,0},... | collective-permute-start | bytes 24584 | tf_op jit(solution)/shard_map/ppermute | solution.py:145
  36.0 0.4 spread_query.2.own
  36.3 0.0 collective-permute-done.9.other
  36.4 0.9 %collective-permute-start.10 = (bf16[128,512]{1,0:T(8,128)(2,1)S(1)}, bf16[128,512]{1,0:T(8,128)(2,1)S(1)}, u32[]{:S(2)}, u32[]{:S(2)}) collective-permute-start(bf16[128,512]{1,0:T(8,128)(2,1)S(1)} %get-tuple-element.67.refs_0_), channel_id=1, source_target_pairs={{0,16},{2,18},{4,20},{6,22},{8,24},{10,26},{12,28},{14,30},{16,0},... | collective-permute-start | bytes 393224 | tf_op jit(solution)/shard_map/ppermute | solution.py:145
  37.3 1.1 %collective-permute-done.12.other = f32[16,128]{1,0:T(8,128)S(1)} collective-permute-done((f32[16,128]{1,0:T(8,128)S(1)}, f32[16,128]{1,0:T(8,128)S(1)}, u32[]{:S(2)}, u32[]{:S(2)}) %collective-permute-start.12) | collective-permute-done | bytes 8224 | tf_op jit(solution)/shard_map/ppermute | solution.py:145
  38.4 0.5 spread_pass.3
  38.9 2.7 %collective-permute-start.14 = (bf16[128,512]{1,0:T(8,128)(2,1)S(1)}, bf16[128,512]{1,0:T(8,128)(2,1)S(1)}, u32[]{:S(2)}, u32[]{:S(2)}) collective-permute-start(bf16[128,512]{1,0:T(8,128)(2,1)S(1)} %get-tuple-element.73), channel_id=1, source_target_pairs={{0,12},{2,14},{4,8},{6,10},{8,4},{10,6},{12,0},{14,2},{16,28},{18,... | collective-permute-start | bytes 393224 | tf_op jit(solution)/shard_map/ppermute | solution.py:145
  41.7 0.5 collective-permute-start.15
  42.1 0.3 collective-permute-start.16
  42.5 0.3 spread_pass.2.own
  42.8 2.7 %collective-permute-done.10.other = bf16[128,512]{1,0:T(8,128)(2,1)S(1)} collective-permute-done((bf16[128,512]{1,0:T(8,128)(2,1)S(1)}, bf16[128,512]{1,0:T(8,128)(2,1)S(1)}, u32[]{:S(2)}, u32[]{:S(2)}) %collective-permute-start.10) | collective-permute-done | bytes 131104 | tf_op jit(solution)/shard_map/ppermute | solution.py:145
  45.5 0.2 grad_query.1
  45.7 1.6 %collective-permute-start.13 = (bf16[128,512]{1,0:T(8,128)(2,1)S(1)}, bf16[128,512]{1,0:T(8,128)(2,1)S(1)}, u32[]{:S(2)}, u32[]{:S(2)}) collective-permute-start(bf16[128,512]{1,0:T(8,128)(2,1)S(1)} %get-tuple-element.71.mine.after), channel_id=1, source_target_pairs={{0,1},{1,0},{2,3},{3,2},{4,5},{5,4},{6,7},{7,6},{8,9},{9,8},{10,11... | collective-permute-start | bytes 393224 | tf_op jit(solution)/shard_map/ppermute | solution.py:145
  47.3 0.0 collective-permute-done.14.first
  47.3 1.2 %collective-permute-done.15.second = bf16[128,512]{1,0:T(8,128)(2,1)S(1)} collective-permute-done((bf16[128,512]{1,0:T(8,128)(2,1)S(1)}, bf16[128,512]{1,0:T(8,128)(2,1)S(1)}, u32[]{:S(2)}, u32[]{:S(2)}) %collective-permute-start.15) | collective-permute-done | bytes 131104 | tf_op jit(solution)/shard_map/ppermute | solution.py:145
  48.4 0.0 collective-permute-done.16.third
  48.4 0.1 grad_pass.1
  48.5 1.6 %collective-permute-start.17 = (bf16[128,512]{1,0:T(8,128)(2,1)S(1)}, bf16[128,512]{1,0:T(8,128)(2,1)S(1)}, u32[]{:S(2)}, u32[]{:S(2)}) collective-permute-start(bf16[128,512]{1,0:T(8,128)(2,1)S(1)} %get-tuple-element.76.mine), channel_id=1, source_target_pairs={{0,1},{1,0},{2,3},{3,2},{4,5},{5,4},{6,7},{7,6},{8,9},{9,8},{10,11... | collective-permute-start | bytes 393224 | tf_op jit(solution)/shard_map/ppermute | solution.py:145
  50.1 0.5 decode_near.2.near
  50.6 0.5 decode_near.3.near
  51.1 0.0 collective-permute-done.13.theirs
  51.1 0.8 %decode_far.2 = (bf16[128,2048]{1,0:T(8,128)(2,1)S(1)}, bf16[128,512]{1,0:T(8,128)(2,1)S(1)}) custom-call(f32[128,2048]{1,0:T(8,128)S(1)} %decode_near.2.near, bf16[128,512]{1,0:T(8,128)(2,1)S(1)} %collective-permute-done.13.theirs, bf16[256,2048]{1,0:T(8,128)(2,1)S(1)} %slope.1.refs_8_, bf16[512,2048]{1,0:T(8,128)(2,1)S(1)} %flip_out_far.1.refs_0_.w_out, ...), custom_call_target="tpu_custom_call" | custom-call | flops 1 | bytes 1 | tf_op jit(solution)/shard_map/decode_far/pallas_call | solution.py:169
  51.9 1.2 %collective-permute-start.18 = (bf16[128,512]{1,0:T(8,128)(2,1)S(1)}, bf16[128,512]{1,0:T(8,128)(2,1)S(1)}, u32[]{:S(2)}, u32[]{:S(2)}) collective-permute-start(bf16[128,512]{1,0:T(8,128)(2,1)S(1)} %get-tuple-element.77.refs_0_), channel_id=1, source_target_pairs={{0,1},{1,0},{2,3},{3,2},{4,5},{5,4},{6,7},{7,6},{8,9},{9,8},{10,11... | collective-permute-start | bytes 393224 | tf_op jit(solution)/shard_map/ppermute | solution.py:145
  53.2 0.8 %collective-permute-done.17.theirs = bf16[128,512]{1,0:T(8,128)(2,1)S(1)} collective-permute-done((bf16[128,512]{1,0:T(8,128)(2,1)S(1)}, bf16[128,512]{1,0:T(8,128)(2,1)S(1)}, u32[]{:S(2)}, u32[]{:S(2)}) %collective-permute-start.17) | collective-permute-done | bytes 131104 | tf_op jit(solution)/shard_map/ppermute | solution.py:145
  53.9 0.8 %decode_far.3 = (bf16[128,2048]{1,0:T(8,128)(2,1)S(1)}, bf16[128,512]{1,0:T(8,128)(2,1)S(1)}) custom-call(f32[128,2048]{1,0:T(8,128)S(1)} %decode_near.3.near, bf16[128,512]{1,0:T(8,128)(2,1)S(1)} %collective-permute-done.17.theirs, bf16[256,2048]{1,0:T(8,128)(2,1)S(1)} %slope.1.refs_8_, bf16[512,2048]{1,0:T(8,128)(2,1)S(1)} %flip_out_far.1.refs_0_.w_out, ...), custom_call_target="tpu_custom_call" | custom-call | flops 1 | bytes 1 | tf_op jit(solution)/shard_map/decode_far/pallas_call | solution.py:169
  54.8 2.4 %collective-permute-start.19 = (bf16[128,512]{1,0:T(8,128)(2,1)S(1)}, bf16[128,512]{1,0:T(8,128)(2,1)S(1)}, u32[]{:S(2)}, u32[]{:S(2)}) collective-permute-start(bf16[128,512]{1,0:T(8,128)(2,1)S(1)} %get-tuple-element.78.refs_0_), channel_id=1, source_target_pairs={{0,1},{1,0},{2,3},{3,2},{4,5},{5,4},{6,7},{7,6},{8,9},{9,8},{10,11... | collective-permute-start | bytes 393224 | tf_op jit(solution)/shard_map/ppermute | solution.py:145
  57.1 0.5 decode_own.2.own
  57.6 0.5 decode_own.3.own
  58.1 0.0 collective-permute-done.18.other
  58.1 0.7 %out_query.1 = (bf16[128,512]{1,0:T(8,128)(2,1)}, f32[8,128]{1,0:T(8,128)S(1)}) custom-call(f32[128,512]{1,0:T(8,128)S(1)} %decode_own.2.own, bf16[128,512]{1,0:T(8,128)(2,1)S(1)} %collective-permute-done.18.other), custom_call_target="tpu_custom_call" | custom-call | tf_op jit(solution)/shard_map/out_query/pallas_call | solution.py:701
  58.8 1.3 %collective-permute-done.19.other = bf16[128,512]{1,0:T(8,128)(2,1)S(1)} collective-permute-done((bf16[128,512]{1,0:T(8,128)(2,1)S(1)}, bf16[128,512]{1,0:T(8,128)(2,1)S(1)}, u32[]{:S(2)}, u32[]{:S(2)}) %collective-permute-start.19) | collective-permute-done | bytes 131104 | tf_op jit(solution)/shard_map/ppermute | solution.py:145
  60.1 0.7 %out_pass.1 = (bf16[128,512]{1,0:T(8,128)(2,1)}, f32[8,128]{1,0:T(8,128)}) custom-call(f32[128,512]{1,0:T(8,128)S(1)} %decode_own.3.own, bf16[128,512]{1,0:T(8,128)(2,1)S(1)} %collective-permute-done.19.other, f32[8,128]{1,0:T(8,128)S(1)} %get-tuple-element.82.refs_0_), custom_call_target="tpu_custom_call" | custom-call | tf_op jit(solution)/shard_map/out_pass/pallas_call | solution.py:701
  (6 shorter events, 0.2 us)
Async XLA Ops:
  5.6 7.4 %collective-permute-start.3 = (bf16[128,512]{1,0:T(8,128)(2,1)S(1)}, bf16[128,512]{1,0:T(8,128)(2,1)S(1)}, u32[]{:S(2)}, u32[]{:S(2)}) collective-permute-start(bf16[128,512]{1,0:T(8,128)(2,1)S(1)} %get-tuple-element.49), channel_id=1, source_target_pairs={{0,1},{1,0},{2,3},{3,2},{4,5},{5,4},{6,7},{7,6},{8,9},{9,8},{10,11... | collective-permute-start | bytes 393224 | tf_op jit(solution)/shard_map/ppermute | solution.py:145
  8.6 7.6 %collective-permute-start = (bf16[128,512]{1,0:T(8,128)(2,1)S(1)}, bf16[128,512]{1,0:T(8,128)(2,1)S(1)}, u32[]{:S(2)}, u32[]{:S(2)}) collective-permute-start(bf16[128,512]{1,0:T(8,128)(2,1)S(1)} %get-tuple-element.46), channel_id=1, source_target_pairs={{0,1},{1,0},{2,3},{3,2},{4,5},{5,4},{6,7},{7,6},{8,9},{9,8},{10,11... | collective-permute-start | bytes 393224 | tf_op jit(solution)/shard_map/ppermute | solution.py:145
  13.0 7.5 %collective-permute-start.4 = (bf16[144,512]{1,0:T(8,128)(2,1)S(1)}, bf16[144,512]{1,0:T(8,128)(2,1)S(1)}, u32[]{:S(2)}, u32[]{:S(2)}) collective-permute-start(bf16[144,512]{1,0:T(8,128)(2,1)S(1)} %pack.3.refs_0_.raw), channel_id=1, source_target_pairs={{0,16},{2,18},{4,20},{6,22},{8,24},{10,26},{12,28},{14,30},{16,0},... | collective-permute-start | bytes 442376 | tf_op jit(solution)/shard_map/ppermute | solution.py:145
  16.2 6.0 %collective-permute-start.1 = (bf16[144,512]{1,0:T(8,128)(2,1)S(1)}, bf16[144,512]{1,0:T(8,128)(2,1)S(1)}, u32[]{:S(2)}, u32[]{:S(2)}) collective-permute-start(bf16[144,512]{1,0:T(8,128)(2,1)S(1)} %pack.2.refs_4_.raw_pass), channel_id=1, source_target_pairs={{0,8},{2,10},{4,12},{6,14},{8,0},{10,2},{12,4},{14,6},{16,24},{18,... | collective-permute-start | bytes 442376 | tf_op jit(solution)/shard_map/ppermute | solution.py:145
  17.9 8.0 %collective-permute-start.5 = (bf16[144,512]{1,0:T(8,128)(2,1)S(1)}, bf16[144,512]{1,0:T(8,128)(2,1)S(1)}, u32[]{:S(2)}, u32[]{:S(2)}) collective-permute-start(bf16[144,512]{1,0:T(8,128)(2,1)S(1)} %pack.3.refs_0_.raw), channel_id=1, source_target_pairs={{0,2},{2,0},{4,6},{6,4},{8,10},{10,8},{12,14},{14,12},{16,18},{18,... | collective-permute-start | bytes 442376 | tf_op jit(solution)/shard_map/ppermute | solution.py:145
  17.9 8.0 %collective-permute-start.7 = (bf16[144,512]{1,0:T(8,128)(2,1)S(1)}, bf16[144,512]{1,0:T(8,128)(2,1)S(1)}, u32[]{:S(2)}, u32[]{:S(2)}) collective-permute-start(bf16[144,512]{1,0:T(8,128)(2,1)S(1)} %pack.2.refs_4_.raw_pass), channel_id=1, source_target_pairs={{0,4},{2,6},{4,0},{6,2},{8,12},{10,14},{12,8},{14,10},{16,20},{18,... | collective-permute-start | bytes 442376 | tf_op jit(solution)/shard_map/ppermute | solution.py:145
  20.5 5.4 %collective-permute-start.6 = (bf16[144,512]{1,0:T(8,128)(2,1)S(1)}, bf16[144,512]{1,0:T(8,128)(2,1)S(1)}, u32[]{:S(2)}, u32[]{:S(2)}) collective-permute-start(bf16[144,512]{1,0:T(8,128)(2,1)S(1)} %collective-permute-done.4.refs_1_), channel_id=1, source_target_pairs={{0,2},{2,0},{4,6},{6,4},{8,10},{10,8},{12,14},{14,12},{16,18},{18,... | collective-permute-start | bytes 442376 | tf_op jit(solution)/shard_map/ppermute | solution.py:145
  22.2 5.1 %collective-permute-start.2 = (bf16[144,512]{1,0:T(8,128)(2,1)S(1)}, bf16[144,512]{1,0:T(8,128)(2,1)S(1)}, u32[]{:S(2)}, u32[]{:S(2)}) collective-permute-start(bf16[144,512]{1,0:T(8,128)(2,1)S(1)} %collective-permute-done.1.refs_5_), channel_id=1, source_target_pairs={{0,4},{2,6},{4,0},{6,2},{8,12},{10,14},{12,8},{14,10},{16,20},{18,... | collective-permute-start | bytes 442376 | tf_op jit(solution)/shard_map/ppermute | solution.py:145
  27.8 4.0 %collective-permute-start.8 = (f32[16,512]{1,0:T(8,128)S(1)}, f32[16,512]{1,0:T(8,128)S(1)}, u32[]{:S(2)}, u32[]{:S(2)}) collective-permute-start(f32[16,512]{1,0:T(8,128)S(1)} %get-tuple-element.60.table), channel_id=1, source_target_pairs={{0,1},{1,0},{2,3},{3,2},{4,5},{5,4},{6,7},{7,6},{8,9},{9,8},{10,11... | collective-permute-start | bytes 98312 | tf_op jit(solution)/shard_map/ppermute | solution.py:145
  32.2 4.2 %collective-permute-start.9 = (bf16[256,512]{1,0:T(8,128)(2,1)S(1)}, bf16[256,512]{1,0:T(8,128)(2,1)S(1)}, u32[]{:S(2)}, u32[]{:S(2)}) collective-permute-start(bf16[256,512]{1,0:T(8,128)(2,1)S(1)} %spread_query.3.refs_0_), channel_id=1, source_target_pairs={{0,2},{2,0},{4,6},{6,4},{8,10},{10,8},{12,14},{14,12},{16,18},{18,... | collective-permute-start | bytes 786440 | tf_op jit(solution)/shard_map/ppermute | solution.py:145
  32.2 1.5 %collective-permute-start.11 = (f32[16,128]{1,0:T(8,128)S(1)}, f32[16,128]{1,0:T(8,128)S(1)}, u32[]{:S(2)}, u32[]{:S(2)}) collective-permute-start(f32[16,128]{1,0:T(8,128)S(1)} %get-tuple-element.69.sums), channel_id=1, source_target_pairs={{0,2},{2,0},{4,6},{6,4},{8,10},{10,8},{12,14},{14,12},{16,18},{18,... | collective-permute-start | bytes 24584 | tf_op jit(solution)/shard_map/ppermute | solution.py:145
  33.8 4.6 %collective-permute-start.12 = (f32[16,128]{1,0:T(8,128)S(1)}, f32[16,128]{1,0:T(8,128)S(1)}, u32[]{:S(2)}, u32[]{:S(2)}) collective-permute-start(f32[16,128]{1,0:T(8,128)S(1)} %add_sums.2.sums), channel_id=1, source_target_pairs={{0,16},{2,18},{4,20},{6,22},{8,24},{10,26},{12,28},{14,30},{16,0},... | collective-permute-start | bytes 24584 | tf_op jit(solution)/shard_map/ppermute | solution.py:145
  36.4 9.1 %collective-permute-start.10 = (bf16[128,512]{1,0:T(8,128)(2,1)S(1)}, bf16[128,512]{1,0:T(8,128)(2,1)S(1)}, u32[]{:S(2)}, u32[]{:S(2)}) collective-permute-start(bf16[128,512]{1,0:T(8,128)(2,1)S(1)} %get-tuple-element.67.refs_0_), channel_id=1, source_target_pairs={{0,16},{2,18},{4,20},{6,22},{8,24},{10,26},{12,28},{14,30},{16,0},... | collective-permute-start | bytes 393224 | tf_op jit(solution)/shard_map/ppermute | solution.py:145
  38.9 8.3 %collective-permute-start.14 = (bf16[128,512]{1,0:T(8,128)(2,1)S(1)}, bf16[128,512]{1,0:T(8,128)(2,1)S(1)}, u32[]{:S(2)}, u32[]{:S(2)}) collective-permute-start(bf16[128,512]{1,0:T(8,128)(2,1)S(1)} %get-tuple-element.73), channel_id=1, source_target_pairs={{0,12},{2,14},{4,8},{6,10},{8,4},{10,6},{12,0},{14,2},{16,28},{18,... | collective-permute-start | bytes 393224 | tf_op jit(solution)/shard_map/ppermute | solution.py:145
  41.7 6.7 %collective-permute-start.15 = (bf16[128,512]{1,0:T(8,128)(2,1)S(1)}, bf16[128,512]{1,0:T(8,128)(2,1)S(1)}, u32[]{:S(2)}, u32[]{:S(2)}) collective-permute-start(bf16[128,512]{1,0:T(8,128)(2,1)S(1)} %get-tuple-element.74), channel_id=1, source_target_pairs={{0,4},{2,6},{4,0},{6,2},{8,12},{10,14},{12,8},{14,10},{16,20},{18,... | collective-permute-start | bytes 393224 | tf_op jit(solution)/shard_map/ppermute | solution.py:145
  42.1 6.3 %collective-permute-start.16 = (bf16[128,512]{1,0:T(8,128)(2,1)S(1)}, bf16[128,512]{1,0:T(8,128)(2,1)S(1)}, u32[]{:S(2)}, u32[]{:S(2)}) collective-permute-start(bf16[128,512]{1,0:T(8,128)(2,1)S(1)} %get-tuple-element.75), channel_id=1, source_target_pairs={{0,8},{2,10},{4,12},{6,14},{8,0},{10,2},{12,4},{14,6},{16,24},{18,... | collective-permute-start | bytes 393224 | tf_op jit(solution)/shard_map/ppermute | solution.py:145
  45.7 5.4 %collective-permute-start.13 = (bf16[128,512]{1,0:T(8,128)(2,1)S(1)}, bf16[128,512]{1,0:T(8,128)(2,1)S(1)}, u32[]{:S(2)}, u32[]{:S(2)}) collective-permute-start(bf16[128,512]{1,0:T(8,128)(2,1)S(1)} %get-tuple-element.71.mine.after), channel_id=1, source_target_pairs={{0,1},{1,0},{2,3},{3,2},{4,5},{5,4},{6,7},{7,6},{8,9},{9,8},{10,11... | collective-permute-start | bytes 393224 | tf_op jit(solution)/shard_map/ppermute | solution.py:145
  48.5 5.4 %collective-permute-start.17 = (bf16[128,512]{1,0:T(8,128)(2,1)S(1)}, bf16[128,512]{1,0:T(8,128)(2,1)S(1)}, u32[]{:S(2)}, u32[]{:S(2)}) collective-permute-start(bf16[128,512]{1,0:T(8,128)(2,1)S(1)} %get-tuple-element.76.mine), channel_id=1, source_target_pairs={{0,1},{1,0},{2,3},{3,2},{4,5},{5,4},{6,7},{7,6},{8,9},{9,8},{10,11... | collective-permute-start | bytes 393224 | tf_op jit(solution)/shard_map/ppermute | solution.py:145
  51.9 6.2 %collective-permute-start.18 = (bf16[128,512]{1,0:T(8,128)(2,1)S(1)}, bf16[128,512]{1,0:T(8,128)(2,1)S(1)}, u32[]{:S(2)}, u32[]{:S(2)}) collective-permute-start(bf16[128,512]{1,0:T(8,128)(2,1)S(1)} %get-tuple-element.77.refs_0_), channel_id=1, source_target_pairs={{0,1},{1,0},{2,3},{3,2},{4,5},{5,4},{6,7},{7,6},{8,9},{9,8},{10,11... | collective-permute-start | bytes 393224 | tf_op jit(solution)/shard_map/ppermute | solution.py:145
  54.8 5.3 %collective-permute-start.19 = (bf16[128,512]{1,0:T(8,128)(2,1)S(1)}, bf16[128,512]{1,0:T(8,128)(2,1)S(1)}, u32[]{:S(2)}, u32[]{:S(2)}) collective-permute-start(bf16[128,512]{1,0:T(8,128)(2,1)S(1)} %get-tuple-element.78.refs_0_), channel_id=1, source_target_pairs={{0,1},{1,0},{2,3},{3,2},{4,5},{5,4},{6,7},{7,6},{8,9},{9,8},{10,11... | collective-permute-start | bytes 393224 | tf_op jit(solution)/shard_map/ppermute | solution.py:145

commit v7 on v6

--- a/solution.py
+++ b/solution.py
@@ -140,9 +140,10 @@
 query_at, pass_at = offsets(query_bits), offsets(pass_bits)
 
 
-def swap(values, axis, bit):
+def swap(values, axis, bit, odd_bit=None):
     size = lax.axis_size(axis)
-    return lax.ppermute(values, axis, [(i, i ^ bit) for i in range(size)])
+    bits = (bit, bit if odd_bit is None else odd_bit)
+    return lax.ppermute(values, axis, [(i, i ^ bits[i % 2]) for i in range(size)])
 
 
 def gather_blocks(block, bits):
@@ -566,7 +567,7 @@
     return jnp.sum(eye * row, axis=1, keepdims=True)
 
 
-def spread_pass_kernel(rows, blocks, scale, coefs, sums, pick, q_all, p_all, *outs):
+def spread_pass_kernel(rows, blocks, place, scale, coefs, sums, pick, q_all, p_all, *outs):
     nq, npass = len(query_at), len(pass_at)
     eye = eye_of(rows)
     share = scale[:nq] / (sums[:nq] + sums[nq : 2 * nq])
@@ -574,7 +575,8 @@
     share = jnp.concatenate([share[n : n + 1] for n in range(nq)], axis=1)
     scaled = share * coefs[3 * npass : 3 * npass + 1]
     queries = q_all[...]
-    for out, a in zip(outs, blocks):
+    found = {}
+    for a in sorted({a for pair in blocks for a in pair}):
         at = slice(a * rows, (a + 1) * rows)
         chosen = pick[at, :]
         weights = chosen.astype(f32) * (coefs[a : a + 1] * scaled)
@@ -589,11 +591,14 @@
             dot = dot + pos * coefs[3 * npass + 2 : 3 * npass + 3, :rows]
         values = jnp.dot(weights.astype(bf16), queries, preferred_element_type=f32)
         along = column_of(eye, dot * coefs[3 * npass + 1 : 3 * npass + 2, at])
-        values = values - along * p_all[at, :].astype(f32)
+        found[a] = values - along * p_all[at, :].astype(f32)
+    odd = place[0] % 2 == 1
+    for out, (a, b) in zip(outs, blocks):
+        values = found[a] if a == b else jnp.where(odd, found[b], found[a])
         out[...] = values.astype(out.dtype)
 
 
-def spread_pass(scale, coefs, sums, pick, q_all, p_all, rows, blocks, dtype):
+def spread_pass(place, scale, coefs, sums, pick, q_all, p_all, rows, blocks, dtype):
     block = (rows, q_all.shape[1])
     return local(
         functools.partial(spread_pass_kernel, rows, blocks),
@@ -601,6 +606,7 @@
         [(block, dtype)] * len(blocks),
         (scale, coefs, sums, pick, q_all, p_all),
         3,
+        scalars=[place],
     )
 
 
@@ -739,10 +745,13 @@
     kept_q = spread_query(coefs, pick, p_all, rows, False)
     kept_q, sent_q = fold_query(kept_q, swap(sent_q, "dp", query_bits[1]))
     sums = exchange_sums(sums, query_bits[0], sent_q)
-    operands = (scale, coefs, sums, pick, q_all, p_all, rows)
-    sent_p = spread_pass(*operands, tuple(range(1, len(pass_at))), bf16)
-    kept_p = spread_pass(*operands, (0,), f32)[0]
-    others_p = [swap(sent_p[n - 1], "dp", pass_at[n]) for n in (3, 2, 1)]
+    operands = (place, scale, coefs, sums, pick, q_all, p_all, rows)
+    order = tuple(zip((3, 2, 1), (2, 3, 1)))
+    sent_p = spread_pass(*operands, order, bf16)
+    kept_p = spread_pass(*operands, ((0, 0),), f32)[0]
+    others_p = [
+        swap(block, "dp", pass_at[a], pass_at[b]) for block, (a, b) in zip(sent_p, order)
+    ]
     grad_q, round_q = grad_out(
         grad_query_kernel,
         "grad_query",

time: 61.4 us -> 61.3 us (level)
  transfers between devices with their start and end apart: 20 -> 20, of which waited for: 11 -> 12; matrix products, arithmetic and copies ran while one was open for 0% -> 0% of each run, Pallas kernels for 21% -> 21%
where the time goes in v7:
time: 61.3 us; the launch traced here: 61 us
  starting transfers between devices  26.5 us (43%)
  Pallas kernels  18.4 us (30%)
  waiting for transfers between devices  14.6 us (24%)
  between operations  1.53 us (2%)
    ppermute x20, starting transfers between devices, swap(): lax.ppermute(values, axis, [(i, i ^ bits[i % 2]) for i in range(size)])  26.5 us
    ppermute x20, waiting for transfers between devices, swap(): lax.ppermute(values, axis, [(i, i ^ bits[i % 2]) for i in range(size)])  14.6 us
    pallas_call x25, Pallas kernels, local(): pl.pallas_call(kernel, in_specs=[smem] * len(scalars) + [vmem] * len(oper...  10.6 us
    pallas_call x1, Pallas kernels, encode_far(): pl.pallas_call(functools.partial(encode_far_kernel, tile), in_specs=[smem...  4.3 us
    pallas_call x1, Pallas kernels, encode_near(): pl.pallas_call(functools.partial(encode_near_kernel, tile), in_specs=[sme...  2.13 us
    pallas_call x2, Pallas kernels, finish(): pl.pallas_call(finish_kernel, in_specs=[vmem] * (2 + len(after)), out_spe...  1.37 us
  transfers between devices with their start and end apart: 20, of which 12 were waited for; matrix products, arithmetic and copies ran while one was open for 0% of the time, Pallas kernels for 21%

profile of v7, /device:TPU:0, one launch (start us, length us, event | category | flops | bytes accessed | tf_op | source)
XLA Modules:
  0.0 61.0 jit_solution(6952162644057106807)
XLA Ops:
  1.3 4.3 %encode_far.1 = (bf16[128,512]{1,0:T(8,128)(2,1)S(1)}, bf16[128,512]{1,0:T(8,128)(2,1)S(1)}, bf16[256,1024]{1,0:T(8,128)(2,1)S(1)}, bf16[256,2048]{1,0:T(8,128)(...) custom-call(s32[1]{0:T(128)} %bitcast.1.me, ...), custom_call_target="tpu_custom_call" | custom-call | tf_op jit(solution)/shard_map/encode_far/pallas_call | solution.py:242
  5.6 3.0 %collective-permute-start.3 = (bf16[128,512]{1,0:T(8,128)(2,1)S(1)}, bf16[128,512]{1,0:T(8,128)(2,1)S(1)}, u32[]{:S(2)}, u32[]{:S(2)}) collective-permute-start(bf16[128,512]{1,0:T(8,128)(2,1)S(1)} %get-tuple-element.49), channel_id=1, source_target_pairs={{0,1},{1,0},{2,3},{3,2},{4,5},{5,4},{6,7},{7,6},{8,9},{9,8},{10,11... | collective-permute-start | bytes 393224 | tf_op jit(solution)/shard_map/ppermute | solution.py:146
  8.6 0.1 collective-permute-start
  8.7 2.1 %encode_near.1 = (f32[128,512]{1,0:T(8,128)S(1)}, f32[128,512]{1,0:T(8,128)S(1)}, bf16[2048,512]{1,0:T(8,128)(2,1)S(1)}, bf16[16,128]{1,0:T(8,128)(2,1)S(1)}, bf16[16,128]{1,0:T(8,128)(2,1)S(1)}) custom-call(s32[1]{0:T(128)} %bitcast.1.me, bf16[2048,1024]{1,0:T(8,128)(2,1)} %w_out.3, s32[8,128]{1,0:T(8,128)} %bitcast.6, s32[8,128]{1,0:T(8,128)} %bitcast.7, ...), custom_call_target="tpu_custom_call" | custom-call | flops 1 | bytes 1 | tf_op jit(solution)/shard_map/encode_near/pallas_call | solution.py:313
  10.8 2.1 %collective-permute-done.3.other = bf16[128,512]{1,0:T(8,128)(2,1)S(1)} collective-permute-done((bf16[128,512]{1,0:T(8,128)(2,1)S(1)}, bf16[128,512]{1,0:T(8,128)(2,1)S(1)}, u32[]{:S(2)}, u32[]{:S(2)}) %collective-permute-start.3) | collective-permute-done | bytes 131104 | tf_op jit(solution)/shard_map/ppermute | solution.py:146
  13.0 3.2 %collective-permute-start.4 = (bf16[144,512]{1,0:T(8,128)(2,1)S(1)}, bf16[144,512]{1,0:T(8,128)(2,1)S(1)}, u32[]{:S(2)}, u32[]{:S(2)}) collective-permute-start(bf16[144,512]{1,0:T(8,128)(2,1)S(1)} %pack.3.refs_0_.raw), channel_id=1, source_target_pairs={{0,16},{2,18},{4,20},{6,22},{8,24},{10,26},{12,28},{14,30},{16,0},... | collective-permute-start | bytes 442376 | tf_op jit(solution)/shard_map/ppermute | solution.py:146
  16.2 0.0 collective-permute-done.other
  16.2 1.6 %collective-permute-start.1 = (bf16[144,512]{1,0:T(8,128)(2,1)S(1)}, bf16[144,512]{1,0:T(8,128)(2,1)S(1)}, u32[]{:S(2)}, u32[]{:S(2)}) collective-permute-start(bf16[144,512]{1,0:T(8,128)(2,1)S(1)} %pack.2.refs_4_.raw_pass), channel_id=1, source_target_pairs={{0,8},{2,10},{4,12},{6,14},{8,0},{10,2},{12,4},{14,6},{16,24},{18,... | collective-permute-start | bytes 442376 | tf_op jit(solution)/shard_map/ppermute | solution.py:146
  17.9 0.0 collective-permute-start.5
  17.9 1.5 %collective-permute-start.7 = (bf16[144,512]{1,0:T(8,128)(2,1)S(1)}, bf16[144,512]{1,0:T(8,128)(2,1)S(1)}, u32[]{:S(2)}, u32[]{:S(2)}) collective-permute-start(bf16[144,512]{1,0:T(8,128)(2,1)S(1)} %pack.2.refs_4_.raw_pass), channel_id=1, source_target_pairs={{0,4},{2,6},{4,0},{6,2},{8,12},{10,14},{12,8},{14,10},{16,20},{18,... | collective-permute-start | bytes 442376 | tf_op jit(solution)/shard_map/ppermute | solution.py:146
  19.4 1.1 %collective-permute-done.4.refs_1_ = bf16[144,512]{1,0:T(8,128)(2,1)S(1)} collective-permute-done((bf16[144,512]{1,0:T(8,128)(2,1)S(1)}, bf16[144,512]{1,0:T(8,128)(2,1)S(1)}, u32[]{:S(2)}, u32[]{:S(2)}) %collective-permute-start.4) | collective-permute-done | bytes 147488 | tf_op jit(solution)/shard_map/ppermute | solution.py:146
  20.5 0.0 collective-permute-start.6
  20.5 1.7 %collective-permute-done.1.refs_5_ = bf16[144,512]{1,0:T(8,128)(2,1)S(1)} collective-permute-done((bf16[144,512]{1,0:T(8,128)(2,1)S(1)}, bf16[144,512]{1,0:T(8,128)(2,1)S(1)}, u32[]{:S(2)}, u32[]{:S(2)}) %collective-permute-start.1) | collective-permute-done | bytes 147488 | tf_op jit(solution)/shard_map/ppermute | solution.py:146
  22.2 1.3 %collective-permute-start.2 = (bf16[144,512]{1,0:T(8,128)(2,1)S(1)}, bf16[144,512]{1,0:T(8,128)(2,1)S(1)}, u32[]{:S(2)}, u32[]{:S(2)}) collective-permute-start(bf16[144,512]{1,0:T(8,128)(2,1)S(1)} %collective-permute-done.1.refs_5_), channel_id=1, source_target_pairs={{0,4},{2,6},{4,0},{6,2},{8,12},{10,14},{12,8},{14,10},{16,20},{18,... | collective-permute-start | bytes 442376 | tf_op jit(solution)/shard_map/ppermute | solution.py:146
  23.5 0.8 %slope.1.refs_8_ = bf16[256,2048]{1,0:T(8,128)(2,1)S(1)} custom-call(f32[256,2048]{1,0:T(8,128)S(1)} %get-tuple-element.52.pre_act), custom_call_target="tpu_custom_call" | custom-call | flops 1 | bytes 1 | tf_op jit(solution)/shard_map/slope/pallas_call | solution.py:170
  24.3 0.7 %flip_out_near.1.refs_7_.w_out = bf16[512,2048]{1,0:T(8,128)(2,1)S(1)} custom-call(bf16[2048,512]{1,0:T(8,128)(2,1)S(1)} %get-tuple-element.51.weights), custom_call_target="tpu_custom_call" | custom-call | flops 1 | bytes 1 | tf_op jit(solution)/shard_map/flip_out_near/pallas_call | solution.py:170
  25.1 0.8 %flip_in_far.1.refs_9_.w_in = bf16[2048,512]{1,0:T(8,128)(2,1)S(1)} custom-call(s32[1]{0:T(128)} %bitcast.1.me, bf16[1024,2048]{1,0:T(8,128)(2,1)S(1)} %get-tuple-element.53.weights), custom_call_target="tpu_custom_call" | custom-call | flops 1 | bytes 1 | tf_op jit(solution)/shard_map/flip_in_far/pallas_call | solution.py:170
  25.9 0.0 collective-permute-done.5.refs_2_
  25.9 0.0 collective-permute-done.7.refs_6_
  25.9 0.0 collective-permute-done.6.refs_3_
  25.9 0.9 %score_early.1 = (f32[16,512]{1,0:T(8,128)S(1)}, f32[8,512]{1,0:T(8,128)S(1)}, bf16[512,512]{1,0:T(8,128)(2,1)S(1)}, bf16[512,512]{1,0:T(8,128)(2,1)S(1)}, bf16[...) custom-call(s32[1]{0:T(128)} %bitcast.place, bf16[144,512]{1,0:T(8,128)(2,1)S(1)} %pack.3.refs_0_.raw, ...), custom_call_target="tpu_custom_call" | custom-call | flops 1 | bytes 1 | tf_op jit(solution)/shard_map/score_early/pallas_call | solution.py:170
  26.8 0.6 collective-permute-done.2.ref
  27.4 0.4 score_last.1
  27.8 1.5 %collective-permute-start.8 = (f32[16,512]{1,0:T(8,128)S(1)}, f32[16,512]{1,0:T(8,128)S(1)}, u32[]{:S(2)}, u32[]{:S(2)}) collective-permute-start(f32[16,512]{1,0:T(8,128)S(1)} %get-tuple-element.60.table), channel_id=1, source_target_pairs={{0,1},{1,0},{2,3},{3,2},{4,5},{5,4},{6,7},{7,6},{8,9},{9,8},{10,11... | collective-permute-start | bytes 98312 | tf_op jit(solution)/shard_map/ppermute | solution.py:146
  29.3 0.7 %flip_in_near.1.refs_1_.w_in = bf16[2048,512]{1,0:T(8,128)(2,1)S(1)} custom-call(s32[1]{0:T(128)} %bitcast.1.me, bf16[1024,2048]{1,0:T(8,128)(2,1)S(1)} %get-tuple-element.53.weights), custom_call_target="tpu_custom_call" | custom-call | flops 1 | bytes 1 | tf_op jit(solution)/shard_map/flip_in_near/pallas_call | solution.py:170
  30.0 0.7 %flip_out_far.1.refs_0_.w_out = bf16[512,2048]{1,0:T(8,128)(2,1)S(1)} custom-call(bf16[2048,512]{1,0:T(8,128)(2,1)S(1)} %get-tuple-element.62.weights), custom_call_target="tpu_custom_call" | custom-call | flops 1 | bytes 1 | tf_op jit(solution)/shard_map/flip_out_far/pallas_call | solution.py:170
  30.8 1.0 %collective-permute-done.8.other = f32[16,512]{1,0:T(8,128)S(1)} collective-permute-done((f32[16,512]{1,0:T(8,128)S(1)}, f32[16,512]{1,0:T(8,128)S(1)}, u32[]{:S(2)}, u32[]{:S(2)}) %collective-permute-start.8) | collective-permute-done | bytes 32800 | tf_op jit(solution)/shard_map/ppermute | solution.py:146
  31.8 0.4 spread_query.3.refs_0_
  32.2 0.1 collective-permute-start.9
  32.2 0.5 collective-permute-start.11
  32.7 1.0 %collective-permute-done.11.other = f32[16,128]{1,0:T(8,128)S(1)} collective-permute-done((f32[16,128]{1,0:T(8,128)S(1)}, f32[16,128]{1,0:T(8,128)S(1)}, u32[]{:S(2)}, u32[]{:S(2)}) %collective-permute-start.11) | collective-permute-done | bytes 8224 | tf_op jit(solution)/shard_map/ppermute | solution.py:146
  33.8 2.2 %collective-permute-start.12 = (f32[16,128]{1,0:T(8,128)S(1)}, f32[16,128]{1,0:T(8,128)S(1)}, u32[]{:S(2)}, u32[]{:S(2)}) collective-permute-start(f32[16,128]{1,0:T(8,128)S(1)} %add_sums.2.sums), channel_id=1, source_target_pairs={{0,16},{2,18},{4,20},{6,22},{8,24},{10,26},{12,28},{14,30},{16,0},... | collective-permute-start | bytes 24584 | tf_op jit(solution)/shard_map/ppermute | solution.py:146
  36.0 0.4 spread_query.2.own
  36.3 0.0 collective-permute-done.9.other
  36.4 0.9 %collective-permute-start.10 = (bf16[128,512]{1,0:T(8,128)(2,1)S(1)}, bf16[128,512]{1,0:T(8,128)(2,1)S(1)}, u32[]{:S(2)}, u32[]{:S(2)}) collective-permute-start(bf16[128,512]{1,0:T(8,128)(2,1)S(1)} %get-tuple-element.67.refs_0_), channel_id=1, source_target_pairs={{0,16},{2,18},{4,20},{6,22},{8,24},{10,26},{12,28},{14,30},{16,0},... | collective-permute-start | bytes 393224 | tf_op jit(solution)/shard_map/ppermute | solution.py:146
  37.3 1.1 %collective-permute-done.12.other = f32[16,128]{1,0:T(8,128)S(1)} collective-permute-done((f32[16,128]{1,0:T(8,128)S(1)}, f32[16,128]{1,0:T(8,128)S(1)}, u32[]{:S(2)}, u32[]{:S(2)}) %collective-permute-start.12) | collective-permute-done | bytes 8224 | tf_op jit(solution)/shard_map/ppermute | solution.py:146
  38.4 0.6 spread_pass.3
  39.0 2.7 %collective-permute-start.14 = (bf16[128,512]{1,0:T(8,128)(2,1)S(1)}, bf16[128,512]{1,0:T(8,128)(2,1)S(1)}, u32[]{:S(2)}, u32[]{:S(2)}) collective-permute-start(bf16[128,512]{1,0:T(8,128)(2,1)S(1)} %get-tuple-element.73), channel_id=1, source_target_pairs={{0,12},{2,6},{4,8},{6,2},{8,4},{10,14},{12,0},{14,10},{16,28},{18,... | collective-permute-start | bytes 393224 | tf_op jit(solution)/shard_map/ppermute | solution.py:146
  41.7 0.5 collective-permute-start.15
  42.2 0.3 collective-permute-start.16
  42.5 0.3 spread_pass.2.own
  42.8 2.7 %collective-permute-done.10.other = bf16[128,512]{1,0:T(8,128)(2,1)S(1)} collective-permute-done((bf16[128,512]{1,0:T(8,128)(2,1)S(1)}, bf16[128,512]{1,0:T(8,128)(2,1)S(1)}, u32[]{:S(2)}, u32[]{:S(2)}) %collective-permute-start.10) | collective-permute-done | bytes 131104 | tf_op jit(solution)/shard_map/ppermute | solution.py:146
  45.5 0.2 grad_query.1
  45.7 1.6 %collective-permute-start.13 = (bf16[128,512]{1,0:T(8,128)(2,1)S(1)}, bf16[128,512]{1,0:T(8,128)(2,1)S(1)}, u32[]{:S(2)}, u32[]{:S(2)}) collective-permute-start(bf16[128,512]{1,0:T(8,128)(2,1)S(1)} %get-tuple-element.71.mine.after), channel_id=1, source_target_pairs={{0,1},{1,0},{2,3},{3,2},{4,5},{5,4},{6,7},{7,6},{8,9},{9,8},{10,11... | collective-permute-start | bytes 393224 | tf_op jit(solution)/shard_map/ppermute | solution.py:146
  47.3 0.0 collective-permute-done.14.first
  47.3 0.0 collective-permute-done.15.second
  47.3 1.2 %collective-permute-done.16.third = bf16[128,512]{1,0:T(8,128)(2,1)S(1)} collective-permute-done((bf16[128,512]{1,0:T(8,128)(2,1)S(1)}, bf16[128,512]{1,0:T(8,128)(2,1)S(1)}, u32[]{:S(2)}, u32[]{:S(2)}) %collective-permute-start.16) | collective-permute-done | bytes 131104 | tf_op jit(solution)/shard_map/ppermute | solution.py:146
  48.5 0.1 grad_pass.1
  48.6 1.6 %collective-permute-start.17 = (bf16[128,512]{1,0:T(8,128)(2,1)S(1)}, bf16[128,512]{1,0:T(8,128)(2,1)S(1)}, u32[]{:S(2)}, u32[]{:S(2)}) collective-permute-start(bf16[128,512]{1,0:T(8,128)(2,1)S(1)} %get-tuple-element.76.mine), channel_id=1, source_target_pairs={{0,1},{1,0},{2,3},{3,2},{4,5},{5,4},{6,7},{7,6},{8,9},{9,8},{10,11... | collective-permute-start | bytes 393224 | tf_op jit(solution)/shard_map/ppermute | solution.py:146
  50.2 0.5 decode_near.2.near
  50.7 0.5 decode_near.3.near
  51.1 0.3 collective-permute-done.13.theirs
  51.4 0.8 %decode_far.2 = (bf16[128,2048]{1,0:T(8,128)(2,1)S(1)}, bf16[128,512]{1,0:T(8,128)(2,1)S(1)}) custom-call(f32[128,2048]{1,0:T(8,128)S(1)} %decode_near.2.near, bf16[128,512]{1,0:T(8,128)(2,1)S(1)} %collective-permute-done.13.theirs, bf16[256,2048]{1,0:T(8,128)(2,1)S(1)} %slope.1.refs_8_, bf16[512,2048]{1,0:T(8,128)(2,1)S(1)} %flip_out_far.1.refs_0_.w_out, ...), custom_call_target="tpu_custom_call" | custom-call | flops 1 | bytes 1 | tf_op jit(solution)/shard_map/decode_far/pallas_call | solution.py:170
  52.3 1.6 %collective-permute-start.18 = (bf16[128,512]{1,0:T(8,128)(2,1)S(1)}, bf16[128,512]{1,0:T(8,128)(2,1)S(1)}, u32[]{:S(2)}, u32[]{:S(2)}) collective-permute-start(bf16[128,512]{1,0:T(8,128)(2,1)S(1)} %get-tuple-element.77.refs_0_), channel_id=1, source_target_pairs={{0,1},{1,0},{2,3},{3,2},{4,5},{5,4},{6,7},{7,6},{8,9},{9,8},{10,11... | collective-permute-start | bytes 393224 | tf_op jit(solution)/shard_map/ppermute | solution.py:146
  53.9 0.3 collective-permute-done.17.theirs
  54.2 0.8 %decode_far.3 = (bf16[128,2048]{1,0:T(8,128)(2,1)S(1)}, bf16[128,512]{1,0:T(8,128)(2,1)S(1)}) custom-call(f32[128,2048]{1,0:T(8,128)S(1)} %decode_near.3.near, bf16[128,512]{1,0:T(8,128)(2,1)S(1)} %collective-permute-done.17.theirs, bf16[256,2048]{1,0:T(8,128)(2,1)S(1)} %slope.1.refs_8_, bf16[512,2048]{1,0:T(8,128)(2,1)S(1)} %flip_out_far.1.refs_0_.w_out, ...), custom_call_target="tpu_custom_call" | custom-call | flops 1 | bytes 1 | tf_op jit(solution)/shard_map/decode_far/pallas_call | solution.py:170
  55.0 2.3 %collective-permute-start.19 = (bf16[128,512]{1,0:T(8,128)(2,1)S(1)}, bf16[128,512]{1,0:T(8,128)(2,1)S(1)}, u32[]{:S(2)}, u32[]{:S(2)}) collective-permute-start(bf16[128,512]{1,0:T(8,128)(2,1)S(1)} %get-tuple-element.78.refs_0_), channel_id=1, source_target_pairs={{0,1},{1,0},{2,3},{3,2},{4,5},{5,4},{6,7},{7,6},{8,9},{9,8},{10,11... | collective-permute-start | bytes 393224 | tf_op jit(solution)/shard_map/ppermute | solution.py:146
  57.4 0.5 decode_own.2.own
  57.9 0.5 decode_own.3.own
  58.4 0.0 collective-permute-done.18.other
  58.4 0.7 %out_query.1 = (bf16[128,512]{1,0:T(8,128)(2,1)}, f32[8,128]{1,0:T(8,128)S(1)}) custom-call(f32[128,512]{1,0:T(8,128)S(1)} %decode_own.2.own, bf16[128,512]{1,0:T(8,128)(2,1)S(1)} %collective-permute-done.18.other), custom_call_target="tpu_custom_call" | custom-call | tf_op jit(solution)/shard_map/out_query/pallas_call | solution.py:707
  59.1 1.3 %collective-permute-done.19.other = bf16[128,512]{1,0:T(8,128)(2,1)S(1)} collective-permute-done((bf16[128,512]{1,0:T(8,128)(2,1)S(1)}, bf16[128,512]{1,0:T(8,128)(2,1)S(1)}, u32[]{:S(2)}, u32[]{:S(2)}) %collective-permute-start.19) | collective-permute-done | bytes 131104 | tf_op jit(solution)/shard_map/ppermute | solution.py:146
  60.3 0.7 %out_pass.1 = (bf16[128,512]{1,0:T(8,128)(2,1)}, f32[8,128]{1,0:T(8,128)}) custom-call(f32[128,512]{1,0:T(8,128)S(1)} %decode_own.3.own, bf16[128,512]{1,0:T(8,128)(2,1)S(1)} %collective-permute-done.19.other, f32[8,128]{1,0:T(8,128)S(1)} %get-tuple-element.82.refs_0_), custom_call_target="tpu_custom_call" | custom-call | tf_op jit(solution)/shard_map/out_pass/pallas_call | solution.py:707
  (6 shorter events, 0.2 us)
Async XLA Ops:
  5.6 7.4 %collective-permute-start.3 = (bf16[128,512]{1,0:T(8,128)(2,1)S(1)}, bf16[128,512]{1,0:T(8,128)(2,1)S(1)}, u32[]{:S(2)}, u32[]{:S(2)}) collective-permute-start(bf16[128,512]{1,0:T(8,128)(2,1)S(1)} %get-tuple-element.49), channel_id=1, source_target_pairs={{0,1},{1,0},{2,3},{3,2},{4,5},{5,4},{6,7},{7,6},{8,9},{9,8},{10,11... | collective-permute-start | bytes 393224 | tf_op jit(solution)/shard_map/ppermute | solution.py:146
  8.6 7.6 %collective-permute-start = (bf16[128,512]{1,0:T(8,128)(2,1)S(1)}, bf16[128,512]{1,0:T(8,128)(2,1)S(1)}, u32[]{:S(2)}, u32[]{:S(2)}) collective-permute-start(bf16[128,512]{1,0:T(8,128)(2,1)S(1)} %get-tuple-element.46), channel_id=1, source_target_pairs={{0,1},{1,0},{2,3},{3,2},{4,5},{5,4},{6,7},{7,6},{8,9},{9,8},{10,11... | collective-permute-start | bytes 393224 | tf_op jit(solution)/shard_map/ppermute | solution.py:146
  13.0 7.5 %collective-permute-start.4 = (bf16[144,512]{1,0:T(8,128)(2,1)S(1)}, bf16[144,512]{1,0:T(8,128)(2,1)S(1)}, u32[]{:S(2)}, u32[]{:S(2)}) collective-permute-start(bf16[144,512]{1,0:T(8,128)(2,1)S(1)} %pack.3.refs_0_.raw), channel_id=1, source_target_pairs={{0,16},{2,18},{4,20},{6,22},{8,24},{10,26},{12,28},{14,30},{16,0},... | collective-permute-start | bytes 442376 | tf_op jit(solution)/shard_map/ppermute | solution.py:146
  16.2 6.0 %collective-permute-start.1 = (bf16[144,512]{1,0:T(8,128)(2,1)S(1)}, bf16[144,512]{1,0:T(8,128)(2,1)S(1)}, u32[]{:S(2)}, u32[]{:S(2)}) collective-permute-start(bf16[144,512]{1,0:T(8,128)(2,1)S(1)} %pack.2.refs_4_.raw_pass), channel_id=1, source_target_pairs={{0,8},{2,10},{4,12},{6,14},{8,0},{10,2},{12,4},{14,6},{16,24},{18,... | collective-permute-start | bytes 442376 | tf_op jit(solution)/shard_map/ppermute | solution.py:146
  17.9 8.0 %collective-permute-start.5 = (bf16[144,512]{1,0:T(8,128)(2,1)S(1)}, bf16[144,512]{1,0:T(8,128)(2,1)S(1)}, u32[]{:S(2)}, u32[]{:S(2)}) collective-permute-start(bf16[144,512]{1,0:T(8,128)(2,1)S(1)} %pack.3.refs_0_.raw), channel_id=1, source_target_pairs={{0,2},{2,0},{4,6},{6,4},{8,10},{10,8},{12,14},{14,12},{16,18},{18,... | collective-permute-start | bytes 442376 | tf_op jit(solution)/shard_map/ppermute | solution.py:146
  17.9 8.0 %collective-permute-start.7 = (bf16[144,512]{1,0:T(8,128)(2,1)S(1)}, bf16[144,512]{1,0:T(8,128)(2,1)S(1)}, u32[]{:S(2)}, u32[]{:S(2)}) collective-permute-start(bf16[144,512]{1,0:T(8,128)(2,1)S(1)} %pack.2.refs_4_.raw_pass), channel_id=1, source_target_pairs={{0,4},{2,6},{4,0},{6,2},{8,12},{10,14},{12,8},{14,10},{16,20},{18,... | collective-permute-start | bytes 442376 | tf_op jit(solution)/shard_map/ppermute | solution.py:146
  20.5 5.4 %collective-permute-start.6 = (bf16[144,512]{1,0:T(8,128)(2,1)S(1)}, bf16[144,512]{1,0:T(8,128)(2,1)S(1)}, u32[]{:S(2)}, u32[]{:S(2)}) collective-permute-start(bf16[144,512]{1,0:T(8,128)(2,1)S(1)} %collective-permute-done.4.refs_1_), channel_id=1, source_target_pairs={{0,2},{2,0},{4,6},{6,4},{8,10},{10,8},{12,14},{14,12},{16,18},{18,... | collective-permute-start | bytes 442376 | tf_op jit(solution)/shard_map/ppermute | solution.py:146
  22.2 5.1 %collective-permute-start.2 = (bf16[144,512]{1,0:T(8,128)(2,1)S(1)}, bf16[144,512]{1,0:T(8,128)(2,1)S(1)}, u32[]{:S(2)}, u32[]{:S(2)}) collective-permute-start(bf16[144,512]{1,0:T(8,128)(2,1)S(1)} %collective-permute-done.1.refs_5_), channel_id=1, source_target_pairs={{0,4},{2,6},{4,0},{6,2},{8,12},{10,14},{12,8},{14,10},{16,20},{18,... | collective-permute-start | bytes 442376 | tf_op jit(solution)/shard_map/ppermute | solution.py:146
  27.8 4.0 %collective-permute-start.8 = (f32[16,512]{1,0:T(8,128)S(1)}, f32[16,512]{1,0:T(8,128)S(1)}, u32[]{:S(2)}, u32[]{:S(2)}) collective-permute-start(f32[16,512]{1,0:T(8,128)S(1)} %get-tuple-element.60.table), channel_id=1, source_target_pairs={{0,1},{1,0},{2,3},{3,2},{4,5},{5,4},{6,7},{7,6},{8,9},{9,8},{10,11... | collective-permute-start | bytes 98312 | tf_op jit(solution)/shard_map/ppermute | solution.py:146
  32.2 4.2 %collective-permute-start.9 = (bf16[256,512]{1,0:T(8,128)(2,1)S(1)}, bf16[256,512]{1,0:T(8,128)(2,1)S(1)}, u32[]{:S(2)}, u32[]{:S(2)}) collective-permute-start(bf16[256,512]{1,0:T(8,128)(2,1)S(1)} %spread_query.3.refs_0_), channel_id=1, source_target_pairs={{0,2},{2,0},{4,6},{6,4},{8,10},{10,8},{12,14},{14,12},{16,18},{18,... | collective-permute-start | bytes 786440 | tf_op jit(solution)/shard_map/ppermute | solution.py:146
  32.2 1.5 %collective-permute-start.11 = (f32[16,128]{1,0:T(8,128)S(1)}, f32[16,128]{1,0:T(8,128)S(1)}, u32[]{:S(2)}, u32[]{:S(2)}) collective-permute-start(f32[16,128]{1,0:T(8,128)S(1)} %get-tuple-element.69.sums), channel_id=1, source_target_pairs={{0,2},{2,0},{4,6},{6,4},{8,10},{10,8},{12,14},{14,12},{16,18},{18,... | collective-permute-start | bytes 24584 | tf_op jit(solution)/shard_map/ppermute | solution.py:146
  33.8 4.6 %collective-permute-start.12 = (f32[16,128]{1,0:T(8,128)S(1)}, f32[16,128]{1,0:T(8,128)S(1)}, u32[]{:S(2)}, u32[]{:S(2)}) collective-permute-start(f32[16,128]{1,0:T(8,128)S(1)} %add_sums.2.sums), channel_id=1, source_target_pairs={{0,16},{2,18},{4,20},{6,22},{8,24},{10,26},{12,28},{14,30},{16,0},... | collective-permute-start | bytes 24584 | tf_op jit(solution)/shard_map/ppermute | solution.py:146
  36.4 9.1 %collective-permute-start.10 = (bf16[128,512]{1,0:T(8,128)(2,1)S(1)}, bf16[128,512]{1,0:T(8,128)(2,1)S(1)}, u32[]{:S(2)}, u32[]{:S(2)}) collective-permute-start(bf16[128,512]{1,0:T(8,128)(2,1)S(1)} %get-tuple-element.67.refs_0_), channel_id=1, source_target_pairs={{0,16},{2,18},{4,20},{6,22},{8,24},{10,26},{12,28},{14,30},{16,0},... | collective-permute-start | bytes 393224 | tf_op jit(solution)/shard_map/ppermute | solution.py:146
  39.0 8.3 %collective-permute-start.14 = (bf16[128,512]{1,0:T(8,128)(2,1)S(1)}, bf16[128,512]{1,0:T(8,128)(2,1)S(1)}, u32[]{:S(2)}, u32[]{:S(2)}) collective-permute-start(bf16[128,512]{1,0:T(8,128)(2,1)S(1)} %get-tuple-element.73), channel_id=1, source_target_pairs={{0,12},{2,6},{4,8},{6,2},{8,4},{10,14},{12,0},{14,10},{16,28},{18,... | collective-permute-start | bytes 393224 | tf_op jit(solution)/shard_map/ppermute | solution.py:146
  41.7 5.6 %collective-permute-start.15 = (bf16[128,512]{1,0:T(8,128)(2,1)S(1)}, bf16[128,512]{1,0:T(8,128)(2,1)S(1)}, u32[]{:S(2)}, u32[]{:S(2)}) collective-permute-start(bf16[128,512]{1,0:T(8,128)(2,1)S(1)} %get-tuple-element.74), channel_id=1, source_target_pairs={{0,4},{2,14},{4,0},{6,10},{8,12},{10,6},{12,8},{14,2},{16,20},{18,... | collective-permute-start | bytes 393224 | tf_op jit(solution)/shard_map/ppermute | solution.py:146
  42.2 6.3 %collective-permute-start.16 = (bf16[128,512]{1,0:T(8,128)(2,1)S(1)}, bf16[128,512]{1,0:T(8,128)(2,1)S(1)}, u32[]{:S(2)}, u32[]{:S(2)}) collective-permute-start(bf16[128,512]{1,0:T(8,128)(2,1)S(1)} %get-tuple-element.75), channel_id=1, source_target_pairs={{0,8},{2,10},{4,12},{6,14},{8,0},{10,2},{12,4},{14,6},{16,24},{18,... | collective-permute-start | bytes 393224 | tf_op jit(solution)/shard_map/ppermute | solution.py:146
  45.7 5.8 %collective-permute-start.13 = (bf16[128,512]{1,0:T(8,128)(2,1)S(1)}, bf16[128,512]{1,0:T(8,128)(2,1)S(1)}, u32[]{:S(2)}, u32[]{:S(2)}) collective-permute-start(bf16[128,512]{1,0:T(8,128)(2,1)S(1)} %get-tuple-element.71.mine.after), channel_id=1, source_target_pairs={{0,1},{1,0},{2,3},{3,2},{4,5},{5,4},{6,7},{7,6},{8,9},{9,8},{10,11... | collective-permute-start | bytes 393224 | tf_op jit(solution)/shard_map/ppermute | solution.py:146
  48.6 5.6 %collective-permute-start.17 = (bf16[128,512]{1,0:T(8,128)(2,1)S(1)}, bf16[128,512]{1,0:T(8,128)(2,1)S(1)}, u32[]{:S(2)}, u32[]{:S(2)}) collective-permute-start(bf16[128,512]{1,0:T(8,128)(2,1)S(1)} %get-tuple-element.76.mine), channel_id=1, source_target_pairs={{0,1},{1,0},{2,3},{3,2},{4,5},{5,4},{6,7},{7,6},{8,9},{9,8},{10,11... | collective-permute-start | bytes 393224 | tf_op jit(solution)/shard_map/ppermute | solution.py:146
  52.3 6.1 %collective-permute-start.18 = (bf16[128,512]{1,0:T(8,128)(2,1)S(1)}, bf16[128,512]{1,0:T(8,128)(2,1)S(1)}, u32[]{:S(2)}, u32[]{:S(2)}) collective-permute-start(bf16[128,512]{1,0:T(8,128)(2,1)S(1)} %get-tuple-element.77.refs_0_), channel_id=1, source_target_pairs={{0,1},{1,0},{2,3},{3,2},{4,5},{5,4},{6,7},{7,6},{8,9},{9,8},{10,11... | collective-permute-start | bytes 393224 | tf_op jit(solution)/shard_map/ppermute | solution.py:146
  55.0 5.3 %collective-permute-start.19 = (bf16[128,512]{1,0:T(8,128)(2,1)S(1)}, bf16[128,512]{1,0:T(8,128)(2,1)S(1)}, u32[]{:S(2)}, u32[]{:S(2)}) collective-permute-start(bf16[128,512]{1,0:T(8,128)(2,1)S(1)} %get-tuple-element.78.refs_0_), channel_id=1, source_target_pairs={{0,1},{1,0},{2,3},{3,2},{4,5},{5,4},{6,7},{7,6},{8,9},{9,8},{10,11... | collective-permute-start | bytes 393224 | tf_op jit(solution)/shard_map/ppermute | solution.py:146
